TPU v7x, 128 devices: a whole 4x4x4 slice. The times are simulated.
128 devices in a mesh: gx: 8 (over x, core), gy: 16 (over z, y).
Axes of the slice: x: 4, y: 4, z: 4, core: 2. Of those that a mesh axis runs over, the one named last changes fastest.
Arguments:
- cell_local_coords: float32 [12288, 3, 128], P(('gx', 'gy')), may hold values from 0 to 1
- particle_speeds: float32 [12288, 3, 128], P(('gx', 'gy')), may hold values from -4 to 4
- thermal_state: float32 [12288, 128], P(('gx', 'gy')), may hold values from 0 to 2
- particle_weights: float32 [12288, 128], P(('gx', 'gy')), may hold values from 0.0018 to 0.0071
- boundary_flag: int32 [12288, 128], P(('gx', 'gy')), may hold values 0 or 1
- departing_local_groups: int32 [128, 2], P(('gx', 'gy')), may hold values from 0 to 95, as said below
- migrant_target_holder: int32 [128, 2], replicated, may hold values from 0 to 127, as said below
- target_entry_inputs: int32 [13312, 8], P(('gx', 'gy')), may hold values from 0 to 231
- adjacent_cell_label: int32 [13312, 4], P(('gx', 'gy')), may hold values from 0 to 25
Outputs:
- density: float32 [13312, 128], P(('gx', 'gy'))
- acceleration: float32 [13312, 3, 128], P(('gx', 'gy'))
- heating: float32 [13312, 128], P(('gx', 'gy'))
Inputs may be any that keep to these rules, and one draw needn't show every extreme that they name: `departing_local_groups`: each row holds 2 different own block numbers of that owner. `migrant_target_holder`: an owner number for each crossing block; no owner receives more than 8 crossing blocks, and some owner receives exactly 8.
All inputs are finite; a program needn't handle non-finite values. No bound on the sum of `boundary_flag` on one device may be relied on, other than what follows from the above.
Results may differ from a plain program's by a relative error of at most 0.0003.
Values sent between devices are 32-bit elements; how exact they have to be, the bound alone decides.
No kernel may reach another device: no remote copies, remote signals or barrier semaphores. Data moves between devices by JAX's collectives and lax.ppermute only.
A program may use at most 64 MiB of HBM per device.

v0:
```python
import math

import jax
import jax.numpy as jnp
from jax import lax
from jax.sharding import PartitionSpec as P

IN_CAP = 8
BND = 16


SMOOTH = 0.5
KERNEL = 21.0 / (16.0 * math.pi * SMOOTH**3)
REST = 1.0
BULK = 1.0
SOUND = math.sqrt(7.0 * BULK / REST)
VISC = 0.1
SOFT = 0.01 * SMOOTH**2
COND_FLUID = 1.0
COND_WALL = 4.0
GRAVITY = 1.0


def padded(shard, sides, width):
    for axis, dim in sides:
        size, length = (lax.axis_size(axis), shard.shape[dim])
        up = [(i, (i + 1) % size) for i in range(size - 1)]
        down = [(j, i) for i, j in up]
        last = lax.slice_in_dim(shard, length - width, length, axis=dim)
        first = lax.slice_in_dim(shard, 0, width, axis=dim)
        before = lax.ppermute(last, axis, up)
        after = lax.ppermute(first, axis, down)
        shard = jnp.concatenate([before, shard, after], axis=dim)
    return shard


def separation(target, sources, shifts):
    deltas = [
        target[:, None, axis_id, :, None]
        - sources[:, :, axis_id, None, :]
        - shifts[:, :, axis_id, None, None]
        for axis_id in range(3)
    ]
    square = deltas[0] * deltas[0] + deltas[1] * deltas[1] + deltas[2] * deltas[2]
    spread = jnp.sqrt(square) / SMOOTH
    window = jnp.maximum(1.0 - 0.5 * spread, 0.0)
    return (deltas, square, spread, window)


def density_terms(target, sources, shifts):
    deltas, square, spread, window = separation(target, sources, shifts)
    weight = KERNEL * window**4 * (2.0 * spread + 1.0)
    return jnp.sum(weight * sources[:, :, 7, None, :], axis=(1, 3))


def safe_density(density_now, masses):
    return jnp.where(masses > 0.0, density_now, 1.0)


def pressure_term(density_now):
    return BULK * ((density_now / REST) ** 7 - 1.0) / (density_now * density_now)


def force_terms(target, sources, shifts, target_rho, source_rho):
    deltas, square, spread, window = separation(target, sources, shifts)
    slope = -5.0 * KERNEL / SMOOTH**2 * window**3
    closing = (target[:, None, 3, :, None] - sources[:, :, 3, None, :]) * deltas[0]
    closing = closing + (target[:, None, 4, :, None] - sources[:, :, 4, None, :]) * deltas[1]
    closing = closing + (target[:, None, 5, :, None] - sources[:, :, 5, None, :]) * deltas[2]
    approach = jnp.minimum(closing, 0.0) / (square + SOFT)
    mean_rho = 0.5 * (target_rho[:, None, :, None] + source_rho[:, :, None, :])
    viscous = -VISC * SOUND * SMOOTH * approach / mean_rho
    masses = sources[:, :, 7, None, :]
    coupling = (
        masses
        * (
            pressure_term(target_rho)[:, None, :, None]
            + pressure_term(source_rho)[:, :, None, :]
            + viscous
        )
        * slope
    )
    acceleration = jnp.stack(
        [-jnp.sum(coupling * deltas[axis_id], axis=(1, 3)) for axis_id in range(3)], 1
    )
    cond_target = (COND_FLUID + (COND_WALL - COND_FLUID) * target[:, 8])[:, None, :, None]
    cond_source = (COND_FLUID + (COND_WALL - COND_FLUID) * sources[:, :, 8])[:, :, None, :]
    pair_cond = 4.0 * cond_target * cond_source / (cond_target + cond_source)
    gap = target[:, None, 6, :, None] - sources[:, :, 6, None, :]
    product_rho = target_rho[:, None, :, None] * source_rho[:, :, None, :]
    heating = jnp.sum(
        masses * pair_cond / product_rho * gap * slope * square / (square + SOFT), axis=(1, 3)
    )
    return (acceleration, heating)


def pair_lists(target_entry_inputs, adjacent_cell_label):
    own_rows = jnp.arange(target_entry_inputs.shape[0])[:, None]
    indices = jnp.concatenate([own_rows, target_entry_inputs], 1)
    codes = adjacent_cell_label + (adjacent_cell_label >= 13).astype(jnp.int32)
    steps_xyz = jnp.stack([codes // 9 - 1, codes // 3 % 3 - 1, codes % 3 - 1], -1).astype(
        jnp.float32
    )
    still = jnp.zeros(
        (
            target_entry_inputs.shape[0],
            1 + target_entry_inputs.shape[1] - adjacent_cell_label.shape[1],
            3,
        ),
        jnp.float32,
    )
    return (indices, jnp.concatenate([still, steps_xyz], 1))


def density_pass(blocks, source_table, indices, shifts):
    groups = blocks.shape[0] // 8

    def density_group(holding, inputs):
        target, rows, moves = inputs
        return (holding, density_terms(target, jnp.take(source_table, rows, axis=0), moves))

    unused, result = lax.scan(
        density_group,
        jnp.zeros((), jnp.float32),
        (
            blocks.reshape((groups, 8) + blocks.shape[1:]),
            indices.reshape(groups, 8, -1),
            shifts.reshape(groups, 8, -1, 3),
        ),
    )
    return result.reshape(blocks.shape[0], blocks.shape[2])


def force_pass(blocks, source_table, indices, shifts, density_now, rho_table):
    target_rho = safe_density(density_now, blocks[:, 7])
    table_rho = safe_density(rho_table, source_table[:, 7])
    groups = blocks.shape[0] // 8

    def force_group(holding, inputs):
        target, rows, moves, own_rho = inputs
        result = force_terms(
            target,
            jnp.take(source_table, rows, axis=0),
            moves,
            own_rho,
            jnp.take(table_rho, rows, axis=0),
        )
        return (holding, result)

    unused, result = lax.scan(
        force_group,
        jnp.zeros((), jnp.float32),
        (
            blocks.reshape((groups, 8) + blocks.shape[1:]),
            indices.reshape(groups, 8, -1),
            shifts.reshape(groups, 8, -1, 3),
            target_rho.reshape(groups, 8, -1),
        ),
    )
    acceleration, heating = result
    return (acceleration.reshape(blocks.shape[0], 3, -1), heating.reshape(blocks.shape[0], -1))


def finish(blocks, density_now, acceleration, heating):
    living = blocks[:, 7] > 0.0
    fluid = 1.0 - blocks[:, 8]
    pull = jnp.array([0.0, 0.0, -GRAVITY], dtype=blocks.dtype)[None, :, None]
    moved = jnp.where(living[:, None, :], (acceleration + pull) * fluid[:, None, :], 0.0)
    return (jnp.where(living, density_now, 0.0), moved, jnp.where(living, heating, 0.0))


def eight_around(haloed):
    flat = haloed.reshape((9,) + haloed.shape[2:])
    picked = jnp.concatenate([flat[:4], flat[5:]], 0)
    return picked.reshape((8 * haloed.shape[2],) + haloed.shape[3:])


def local(
    cell_local_coords,
    particle_speeds,
    thermal_state,
    particle_weights,
    boundary_flag,
    departing_local_groups,
    migrant_target_holder,
    target_entry_inputs,
    adjacent_cell_label,
):
    along = lax.axis_size("gy")
    myself = lax.axis_index("gx") * along + lax.axis_index("gy")
    state_tables = jnp.concatenate(
        [
            cell_local_coords,
            particle_speeds,
            thermal_state[:, None, :],
            particle_weights[:, None, :],
            boundary_flag.astype(jnp.float32)[:, None, :],
        ],
        1,
    )
    width = state_tables.shape[1]
    lanes = state_tables.shape[2]
    chosen = departing_local_groups[0]
    leaving = jnp.take(state_tables, chosen, axis=0)
    dest_flat = migrant_target_holder.reshape(-1)
    total = dest_flat.shape[0]
    listing = jnp.arange(total)
    match = dest_flat == myself
    ranking = jnp.cumsum(match.astype(jnp.int32)) - 1
    slot_ids = jnp.arange(IN_CAP)
    taken = match[None, :] & (ranking[None, :] == slot_ids[:, None])
    wanted = jnp.sum(jnp.where(taken, listing[None, :], 0), 1)
    present = jnp.any(taken, 1)
    incoming = lax.all_gather(leaving, ("gx", "gy"), axis=0, tiled=True)
    inside = present & (wanted >= 0) & (wanted < incoming.shape[0])
    picked = jnp.take(incoming, jnp.clip(wanted, 0, incoming.shape[0] - 1), axis=0)
    arrived = jnp.where(
        inside[:, None, None], picked, jnp.zeros((IN_CAP, width, lanes), jnp.float32)
    )
    numbers = jnp.arange(state_tables.shape[0])
    departed = jnp.any(numbers[:, None] == chosen[None, :], 1)
    blocks = jnp.concatenate([arrived, jnp.where(departed[:, None, None], 0.0, state_tables)], 0)
    exported = blocks[:BND].reshape((1, 1, BND, width, lanes))
    haloed = padded(exported, (("gx", 0), ("gy", 1)), 1)
    source_table = jnp.concatenate([blocks, eight_around(haloed)], 0)
    indices, shifts = pair_lists(target_entry_inputs, adjacent_cell_label)
    density_now = density_pass(blocks, source_table, indices, shifts)
    again = eight_around(
        padded(density_now[:BND].reshape((1, 1, BND, lanes)), (("gx", 0), ("gy", 1)), 1)
    )
    rho_table = jnp.concatenate([density_now, again], 0)
    acceleration, heating = force_pass(
        blocks, source_table, indices, shifts, density_now, rho_table
    )
    return finish(blocks, density_now, acceleration, heating)


def solution(mesh):
    return jax.shard_map(
        local,
        mesh=mesh,
        in_specs=(
            P(("gx", "gy"), None, None),
            P(("gx", "gy"), None, None),
            P(("gx", "gy"), None),
            P(("gx", "gy"), None),
            P(("gx", "gy"), None),
            P(("gx", "gy"), None),
            P(),
            P(("gx", "gy"), None),
            P(("gx", "gy"), None),
        ),
        out_specs=(P(("gx", "gy"), None), P(("gx", "gy"), None, None), P(("gx", "gy"), None)),
        check_vma=False,
    )
```

profile of v0, /device:TPU:0, one launch (start us, length us, event | category | flops | bytes accessed | tf_op | source)
XLA Modules:
  0.0 826.5 jit_solution(831502257083031264)
XLA Ops:
  15.8 65.9 %all-gather.2.cloned.1.call-done = f32[256,9,128]{2,1,0:T(8,128)} async-done(((f32[2,9,128]{2,1,0:T(8,128)}), f32[256,9,128]{2,1,0:T(8,128)}) %all-gather.2.cloned.1.call-update) | async-done | bytes 1179664 | tf_op jit(solution)/shard_map/all_gather | solution.py:214
  103.8 137.2 %while.27 = (s32[]{:T(128)}, f32[13,8,128]{2,1,0:T(8,128)S(1)}, f32[13,8,9,128]{3,1,2,0:T(8,128)S(1)}, s32[13,8,9]{2,1,0:T(8,128)S(1)}, f32[232,9,128]{2,1,0:T(8...) while((s32[]{:T(128)}, f32[13,8,128]{2,1,0:T(8,128)S(1)}, f32[13,8,9,128]{3,1,2,0:T(8,128)S(1)}, ...), condition=%wide.region_7.9_spmd, body=%wide.region_5.8_spmd.sunk | while | flops 24855984 | bytes 5766661 | solution.py:122
  255.4 561.2 %while.28 = (s32[]{:T(128)}, f32[13,8,3,128]{3,1,0,2:T(8,128)}, f32[13,8,128]{2,1,0:T(8,128)}, s32[13,8,9]{2,1,0:T(8,128)}, f32[232,9,128]{2,1,0:T(8,128)S(1)}, ...) while((s32[]{:T(128)}, f32[13,8,3,128]{3,1,0,2:T(8,128)}, ...), condition=%wide.region_13.15_spmd, body=%wide.region_8.14_spmd.sunk | while | flops 165335680 | bytes 4991129 | solution.py:150
  260.0 10.4 %multiply_reduce_fusion.11 = f32[8,128]{1,0:T(8,128)S(1)} fusion(f32[8,9]{1,0:T(8,128)} %get-tuple-element.559, f32[8,9,128]{2,1,0:T(8,128)S(1)} %copy.232, f32[8,128]{1,0:T(8,128)S(1)} %get-tuple-element.561, f32[8,9,128]{2,1,0:T(8,128)S(1)} %get-tuple-element.550, f32[8,128]{1,0:T(8,128)S(1)} %get-tuple-element.551, f32[8,9]{1,0:T(8,128)} %get-tuple-element.545, ...), kind=kLoop, calls=%fused_computation.28.clone.1 | loop fusion | flops 43645952 | bytes 369504 | tf_op jit(solution)/shard_map/while/body/eval_jaxpr/reduce_sum | solution.py:84
  303.2 10.4 %multiply_reduce_fusion.11 = f32[8,128]{1,0:T(8,128)S(1)} fusion(f32[8,9]{1,0:T(8,128)} %get-tuple-element.559, f32[8,9,128]{2,1,0:T(8,128)S(1)} %copy.232, f32[8,128]{1,0:T(8,128)S(1)} %get-tuple-element.561, f32[8,9,128]{2,1,0:T(8,128)S(1)} %get-tuple-element.550, f32[8,128]{1,0:T(8,128)S(1)} %get-tuple-element.551, f32[8,9]{1,0:T(8,128)} %get-tuple-element.545, ...), kind=kLoop, calls=%fused_computation.28.clone.1 | loop fusion | flops 43645952 | bytes 369504 | tf_op jit(solution)/shard_map/while/body/eval_jaxpr/reduce_sum | solution.py:84
  346.3 10.4 %multiply_reduce_fusion.11 = f32[8,128]{1,0:T(8,128)S(1)} fusion(f32[8,9]{1,0:T(8,128)} %get-tuple-element.559, f32[8,9,128]{2,1,0:T(8,128)S(1)} %copy.232, f32[8,128]{1,0:T(8,128)S(1)} %get-tuple-element.561, f32[8,9,128]{2,1,0:T(8,128)S(1)} %get-tuple-element.550, f32[8,128]{1,0:T(8,128)S(1)} %get-tuple-element.551, f32[8,9]{1,0:T(8,128)} %get-tuple-element.545, ...), kind=kLoop, calls=%fused_computation.28.clone.1 | loop fusion | flops 43645952 | bytes 369504 | tf_op jit(solution)/shard_map/while/body/eval_jaxpr/reduce_sum | solution.py:84
  366.4 9.7 %multiply_reduce_fusion.9 = f32[8,128]{1,0:T(8,128)S(1)} fusion(f32[8,9]{1,0:T(8,128)S(1)} %copy-done.9, f32[8,9,128]{2,1,0:T(8,128)S(1)} %copy.228, f32[8,128]{1,0:T(8,128)S(1)} %get-tuple-element.549, f32[8,9,128]{2,1,0:T(8,128)S(1)} %get-tuple-element.550, f32[8,128]{1,0:T(8,128)S(1)} %get-tuple-element.551, f32[8,9,128]{2,1,0:T(8,128)S(1)} %copy.229, ...), kind=kLoop, calls=%fused_computation.26.clone.1 | loop fusion | flops 43645952 | bytes 369504 | tf_op jit(solution)/shard_map/while/body/eval_jaxpr/reduce_sum | solution.py:84
  389.5 10.4 %multiply_reduce_fusion.11 = f32[8,128]{1,0:T(8,128)S(1)} fusion(f32[8,9]{1,0:T(8,128)} %get-tuple-element.559, f32[8,9,128]{2,1,0:T(8,128)S(1)} %copy.232, f32[8,128]{1,0:T(8,128)S(1)} %get-tuple-element.561, f32[8,9,128]{2,1,0:T(8,128)S(1)} %get-tuple-element.550, f32[8,128]{1,0:T(8,128)S(1)} %get-tuple-element.551, f32[8,9]{1,0:T(8,128)} %get-tuple-element.545, ...), kind=kLoop, calls=%fused_computation.28.clone.1 | loop fusion | flops 43645952 | bytes 369504 | tf_op jit(solution)/shard_map/while/body/eval_jaxpr/reduce_sum | solution.py:84
  409.6 9.7 %multiply_reduce_fusion.9 = f32[8,128]{1,0:T(8,128)S(1)} fusion(f32[8,9]{1,0:T(8,128)S(1)} %copy-done.9, f32[8,9,128]{2,1,0:T(8,128)S(1)} %copy.228, f32[8,128]{1,0:T(8,128)S(1)} %get-tuple-element.549, f32[8,9,128]{2,1,0:T(8,128)S(1)} %get-tuple-element.550, f32[8,128]{1,0:T(8,128)S(1)} %get-tuple-element.551, f32[8,9,128]{2,1,0:T(8,128)S(1)} %copy.229, ...), kind=kLoop, calls=%fused_computation.26.clone.1 | loop fusion | flops 43645952 | bytes 369504 | tf_op jit(solution)/shard_map/while/body/eval_jaxpr/reduce_sum | solution.py:84
  432.7 10.4 %multiply_reduce_fusion.11 = f32[8,128]{1,0:T(8,128)S(1)} fusion(f32[8,9]{1,0:T(8,128)} %get-tuple-element.559, f32[8,9,128]{2,1,0:T(8,128)S(1)} %copy.232, f32[8,128]{1,0:T(8,128)S(1)} %get-tuple-element.561, f32[8,9,128]{2,1,0:T(8,128)S(1)} %get-tuple-element.550, f32[8,128]{1,0:T(8,128)S(1)} %get-tuple-element.551, f32[8,9]{1,0:T(8,128)} %get-tuple-element.545, ...), kind=kLoop, calls=%fused_computation.28.clone.1 | loop fusion | flops 43645952 | bytes 369504 | tf_op jit(solution)/shard_map/while/body/eval_jaxpr/reduce_sum | solution.py:84
  452.8 9.7 %multiply_reduce_fusion.9 = f32[8,128]{1,0:T(8,128)S(1)} fusion(f32[8,9]{1,0:T(8,128)S(1)} %copy-done.9, f32[8,9,128]{2,1,0:T(8,128)S(1)} %copy.228, f32[8,128]{1,0:T(8,128)S(1)} %get-tuple-element.549, f32[8,9,128]{2,1,0:T(8,128)S(1)} %get-tuple-element.550, f32[8,128]{1,0:T(8,128)S(1)} %get-tuple-element.551, f32[8,9,128]{2,1,0:T(8,128)S(1)} %copy.229, ...), kind=kLoop, calls=%fused_computation.26.clone.1 | loop fusion | flops 43645952 | bytes 369504 | tf_op jit(solution)/shard_map/while/body/eval_jaxpr/reduce_sum | solution.py:84
  475.9 10.4 %multiply_reduce_fusion.11 = f32[8,128]{1,0:T(8,128)S(1)} fusion(f32[8,9]{1,0:T(8,128)} %get-tuple-element.559, f32[8,9,128]{2,1,0:T(8,128)S(1)} %copy.232, f32[8,128]{1,0:T(8,128)S(1)} %get-tuple-element.561, f32[8,9,128]{2,1,0:T(8,128)S(1)} %get-tuple-element.550, f32[8,128]{1,0:T(8,128)S(1)} %get-tuple-element.551, f32[8,9]{1,0:T(8,128)} %get-tuple-element.545, ...), kind=kLoop, calls=%fused_computation.28.clone.1 | loop fusion | flops 43645952 | bytes 369504 | tf_op jit(solution)/shard_map/while/body/eval_jaxpr/reduce_sum | solution.py:84
  496.0 9.7 %multiply_reduce_fusion.9 = f32[8,128]{1,0:T(8,128)S(1)} fusion(f32[8,9]{1,0:T(8,128)S(1)} %copy-done.9, f32[8,9,128]{2,1,0:T(8,128)S(1)} %copy.228, f32[8,128]{1,0:T(8,128)S(1)} %get-tuple-element.549, f32[8,9,128]{2,1,0:T(8,128)S(1)} %get-tuple-element.550, f32[8,128]{1,0:T(8,128)S(1)} %get-tuple-element.551, f32[8,9,128]{2,1,0:T(8,128)S(1)} %copy.229, ...), kind=kLoop, calls=%fused_computation.26.clone.1 | loop fusion | flops 43645952 | bytes 369504 | tf_op jit(solution)/shard_map/while/body/eval_jaxpr/reduce_sum | solution.py:84
  519.0 10.4 %multiply_reduce_fusion.11 = f32[8,128]{1,0:T(8,128)S(1)} fusion(f32[8,9]{1,0:T(8,128)} %get-tuple-element.559, f32[8,9,128]{2,1,0:T(8,128)S(1)} %copy.232, f32[8,128]{1,0:T(8,128)S(1)} %get-tuple-element.561, f32[8,9,128]{2,1,0:T(8,128)S(1)} %get-tuple-element.550, f32[8,128]{1,0:T(8,128)S(1)} %get-tuple-element.551, f32[8,9]{1,0:T(8,128)} %get-tuple-element.545, ...), kind=kLoop, calls=%fused_computation.28.clone.1 | loop fusion | flops 43645952 | bytes 369504 | tf_op jit(solution)/shard_map/while/body/eval_jaxpr/reduce_sum | solution.py:84
  539.1 9.7 %multiply_reduce_fusion.9 = f32[8,128]{1,0:T(8,128)S(1)} fusion(f32[8,9]{1,0:T(8,128)S(1)} %copy-done.9, f32[8,9,128]{2,1,0:T(8,128)S(1)} %copy.228, f32[8,128]{1,0:T(8,128)S(1)} %get-tuple-element.549, f32[8,9,128]{2,1,0:T(8,128)S(1)} %get-tuple-element.550, f32[8,128]{1,0:T(8,128)S(1)} %get-tuple-element.551, f32[8,9,128]{2,1,0:T(8,128)S(1)} %copy.229, ...), kind=kLoop, calls=%fused_computation.26.clone.1 | loop fusion | flops 43645952 | bytes 369504 | tf_op jit(solution)/shard_map/while/body/eval_jaxpr/reduce_sum | solution.py:84
  562.2 10.4 %multiply_reduce_fusion.11 = f32[8,128]{1,0:T(8,128)S(1)} fusion(f32[8,9]{1,0:T(8,128)} %get-tuple-element.559, f32[8,9,128]{2,1,0:T(8,128)S(1)} %copy.232, f32[8,128]{1,0:T(8,128)S(1)} %get-tuple-element.561, f32[8,9,128]{2,1,0:T(8,128)S(1)} %get-tuple-element.550, f32[8,128]{1,0:T(8,128)S(1)} %get-tuple-element.551, f32[8,9]{1,0:T(8,128)} %get-tuple-element.545, ...), kind=kLoop, calls=%fused_computation.28.clone.1 | loop fusion | flops 43645952 | bytes 369504 | tf_op jit(solution)/shard_map/while/body/eval_jaxpr/reduce_sum | solution.py:84
  582.3 9.7 %multiply_reduce_fusion.9 = f32[8,128]{1,0:T(8,128)S(1)} fusion(f32[8,9]{1,0:T(8,128)S(1)} %copy-done.9, f32[8,9,128]{2,1,0:T(8,128)S(1)} %copy.228, f32[8,128]{1,0:T(8,128)S(1)} %get-tuple-element.549, f32[8,9,128]{2,1,0:T(8,128)S(1)} %get-tuple-element.550, f32[8,128]{1,0:T(8,128)S(1)} %get-tuple-element.551, f32[8,9,128]{2,1,0:T(8,128)S(1)} %copy.229, ...), kind=kLoop, calls=%fused_computation.26.clone.1 | loop fusion | flops 43645952 | bytes 369504 | tf_op jit(solution)/shard_map/while/body/eval_jaxpr/reduce_sum | solution.py:84
  605.4 10.4 %multiply_reduce_fusion.11 = f32[8,128]{1,0:T(8,128)S(1)} fusion(f32[8,9]{1,0:T(8,128)} %get-tuple-element.559, f32[8,9,128]{2,1,0:T(8,128)S(1)} %copy.232, f32[8,128]{1,0:T(8,128)S(1)} %get-tuple-element.561, f32[8,9,128]{2,1,0:T(8,128)S(1)} %get-tuple-element.550, f32[8,128]{1,0:T(8,128)S(1)} %get-tuple-element.551, f32[8,9]{1,0:T(8,128)} %get-tuple-element.545, ...), kind=kLoop, calls=%fused_computation.28.clone.1 | loop fusion | flops 43645952 | bytes 369504 | tf_op jit(solution)/shard_map/while/body/eval_jaxpr/reduce_sum | solution.py:84
  625.5 9.7 %multiply_reduce_fusion.9 = f32[8,128]{1,0:T(8,128)S(1)} fusion(f32[8,9]{1,0:T(8,128)S(1)} %copy-done.9, f32[8,9,128]{2,1,0:T(8,128)S(1)} %copy.228, f32[8,128]{1,0:T(8,128)S(1)} %get-tuple-element.549, f32[8,9,128]{2,1,0:T(8,128)S(1)} %get-tuple-element.550, f32[8,128]{1,0:T(8,128)S(1)} %get-tuple-element.551, f32[8,9,128]{2,1,0:T(8,128)S(1)} %copy.229, ...), kind=kLoop, calls=%fused_computation.26.clone.1 | loop fusion | flops 43645952 | bytes 369504 | tf_op jit(solution)/shard_map/while/body/eval_jaxpr/reduce_sum | solution.py:84
  648.5 10.4 %multiply_reduce_fusion.11 = f32[8,128]{1,0:T(8,128)S(1)} fusion(f32[8,9]{1,0:T(8,128)} %get-tuple-element.559, f32[8,9,128]{2,1,0:T(8,128)S(1)} %copy.232, f32[8,128]{1,0:T(8,128)S(1)} %get-tuple-element.561, f32[8,9,128]{2,1,0:T(8,128)S(1)} %get-tuple-element.550, f32[8,128]{1,0:T(8,128)S(1)} %get-tuple-element.551, f32[8,9]{1,0:T(8,128)} %get-tuple-element.545, ...), kind=kLoop, calls=%fused_computation.28.clone.1 | loop fusion | flops 43645952 | bytes 369504 | tf_op jit(solution)/shard_map/while/body/eval_jaxpr/reduce_sum | solution.py:84
  691.7 10.4 %multiply_reduce_fusion.11 = f32[8,128]{1,0:T(8,128)S(1)} fusion(f32[8,9]{1,0:T(8,128)} %get-tuple-element.559, f32[8,9,128]{2,1,0:T(8,128)S(1)} %copy.232, f32[8,128]{1,0:T(8,128)S(1)} %get-tuple-element.561, f32[8,9,128]{2,1,0:T(8,128)S(1)} %get-tuple-element.550, f32[8,128]{1,0:T(8,128)S(1)} %get-tuple-element.551, f32[8,9]{1,0:T(8,128)} %get-tuple-element.545, ...), kind=kLoop, calls=%fused_computation.28.clone.1 | loop fusion | flops 43645952 | bytes 369504 | tf_op jit(solution)/shard_map/while/body/eval_jaxpr/reduce_sum | solution.py:84
  711.8 9.7 %multiply_reduce_fusion.9 = f32[8,128]{1,0:T(8,128)S(1)} fusion(f32[8,9]{1,0:T(8,128)S(1)} %copy-done.9, f32[8,9,128]{2,1,0:T(8,128)S(1)} %copy.228, f32[8,128]{1,0:T(8,128)S(1)} %get-tuple-element.549, f32[8,9,128]{2,1,0:T(8,128)S(1)} %get-tuple-element.550, f32[8,128]{1,0:T(8,128)S(1)} %get-tuple-element.551, f32[8,9,128]{2,1,0:T(8,128)S(1)} %copy.229, ...), kind=kLoop, calls=%fused_computation.26.clone.1 | loop fusion | flops 43645952 | bytes 369504 | tf_op jit(solution)/shard_map/while/body/eval_jaxpr/reduce_sum | solution.py:84
  734.9 10.4 %multiply_reduce_fusion.11 = f32[8,128]{1,0:T(8,128)S(1)} fusion(f32[8,9]{1,0:T(8,128)} %get-tuple-element.559, f32[8,9,128]{2,1,0:T(8,128)S(1)} %copy.232, f32[8,128]{1,0:T(8,128)S(1)} %get-tuple-element.561, f32[8,9,128]{2,1,0:T(8,128)S(1)} %get-tuple-element.550, f32[8,128]{1,0:T(8,128)S(1)} %get-tuple-element.551, f32[8,9]{1,0:T(8,128)} %get-tuple-element.545, ...), kind=kLoop, calls=%fused_computation.28.clone.1 | loop fusion | flops 43645952 | bytes 369504 | tf_op jit(solution)/shard_map/while/body/eval_jaxpr/reduce_sum | solution.py:84
  778.0 10.4 %multiply_reduce_fusion.11 = f32[8,128]{1,0:T(8,128)S(1)} fusion(f32[8,9]{1,0:T(8,128)} %get-tuple-element.559, f32[8,9,128]{2,1,0:T(8,128)S(1)} %copy.232, f32[8,128]{1,0:T(8,128)S(1)} %get-tuple-element.561, f32[8,9,128]{2,1,0:T(8,128)S(1)} %get-tuple-element.550, f32[8,128]{1,0:T(8,128)S(1)} %get-tuple-element.551, f32[8,9]{1,0:T(8,128)} %get-tuple-element.545, ...), kind=kLoop, calls=%fused_computation.28.clone.1 | loop fusion | flops 43645952 | bytes 369504 | tf_op jit(solution)/shard_map/while/body/eval_jaxpr/reduce_sum | solution.py:84
  (954 shorter events, 528.1 us)
Async XLA Ops:
  7.2 74.5 %all-gather.2.cloned.1.call-start = ((), (), s32[]{:S(2)}) async-start(), calls=%async_computation | async-start | bytes 2113536 | tf_op jit(solution)/shard_map/all_gather | solution.py:214
  84.0 4.8 collective-permute-start.1
  85.3 4.0 collective-permute-start
  89.3 12.3 %collective-permute-start.3 = (f32[3,1,16,9,128]{4,3,2,1,0:T(8,128)S(1)}, f32[3,1,16,9,128]{4,3,2,1,0:T(8,128)S(1)}, u32[]{:S(2)}, u32[]{:S(2)}) collective-permute-start(f32[3,1,16,9,128]{4,3,2,1,0:T(8,128)S(1)} %pad_maximum_fusion.4), channel_id=1, source_target_pairs={{1,0},{2,1},{3,2},{4,3},{5,4},{6,5},{7,6},{8,7},{9,8},{10,9},{11,1... | collective-permute-start | bytes 663560 | tf_op jit(solution)/shard_map/ppermute | solution.py:32
  90.6 12.8 %collective-permute-start.2 = (f32[3,1,16,9,128]{4,3,2,1,0:T(8,128)S(1)}, f32[3,1,16,9,128]{4,3,2,1,0:T(8,128)S(1)}, u32[]{:S(2)}, u32[]{:S(2)}) collective-permute-start(f32[3,1,16,9,128]{4,3,2,1,0:T(8,128)S(1)} %pad_maximum_fusion.4), channel_id=1, source_target_pairs={{0,1},{1,2},{2,3},{3,4},{4,5},{5,6},{6,7},{7,8},{8,9},{9,10},{10,1... | collective-permute-start | bytes 663560 | tf_op jit(solution)/shard_map/ppermute | solution.py:31
  241.1 5.9 collective-permute-start.5
  242.4 4.7 collective-permute-start.4
  247.1 7.5 collective-permute-start.7
  248.4 6.3 collective-permute-start.6
  255.4 561.2 %copy-start.6 = (pred[104,1,128]{2,0,1:T(8,128)(4,1)S(1)}, pred[104,1,128]{2,0,1:T(8,128)(4,1)}, u32[]{:S(2)}) copy-start(pred[104,1,128]{2,0,1:T(8,128)(4,1)} %get-tuple-element.355) | copy-start | bytes 39940
  255.4 562.6 %copy-start.5 = (f32[104,1,128]{2,1,0:T(1,128)S(1)}, f32[104,1,128]{2,1,0:T(1,128)}, u32[]{:S(2)}) copy-start(f32[104,1,128]{2,1,0:T(1,128)} %fusion.18) | copy-start | bytes 159748
  270.5 19.4 %copy-start.7 = (f32[8,128]{1,0:T(8,128)S(1)}, f32[8,128]{1,0:T(8,128)}, u32[]{:S(2)}) copy-start(f32[8,128]{1,0:T(8,128)} %broadcast_multiply_fusion.2) | copy-start | bytes 12292 | tf_op jit(solution)/shard_map/while
  313.7 19.4 %copy-start.7 = (f32[8,128]{1,0:T(8,128)S(1)}, f32[8,128]{1,0:T(8,128)}, u32[]{:S(2)}) copy-start(f32[8,128]{1,0:T(8,128)} %broadcast_multiply_fusion.2) | copy-start | bytes 12292 | tf_op jit(solution)/shard_map/while
  356.8 19.4 %copy-start.7 = (f32[8,128]{1,0:T(8,128)S(1)}, f32[8,128]{1,0:T(8,128)}, u32[]{:S(2)}) copy-start(f32[8,128]{1,0:T(8,128)} %broadcast_multiply_fusion.2) | copy-start | bytes 12292 | tf_op jit(solution)/shard_map/while
  400.0 19.4 %copy-start.7 = (f32[8,128]{1,0:T(8,128)S(1)}, f32[8,128]{1,0:T(8,128)}, u32[]{:S(2)}) copy-start(f32[8,128]{1,0:T(8,128)} %broadcast_multiply_fusion.2) | copy-start | bytes 12292 | tf_op jit(solution)/shard_map/while
  443.2 19.4 %copy-start.7 = (f32[8,128]{1,0:T(8,128)S(1)}, f32[8,128]{1,0:T(8,128)}, u32[]{:S(2)}) copy-start(f32[8,128]{1,0:T(8,128)} %broadcast_multiply_fusion.2) | copy-start | bytes 12292 | tf_op jit(solution)/shard_map/while
  486.4 19.4 %copy-start.7 = (f32[8,128]{1,0:T(8,128)S(1)}, f32[8,128]{1,0:T(8,128)}, u32[]{:S(2)}) copy-start(f32[8,128]{1,0:T(8,128)} %broadcast_multiply_fusion.2) | copy-start | bytes 12292 | tf_op jit(solution)/shard_map/while
  529.5 19.4 %copy-start.7 = (f32[8,128]{1,0:T(8,128)S(1)}, f32[8,128]{1,0:T(8,128)}, u32[]{:S(2)}) copy-start(f32[8,128]{1,0:T(8,128)} %broadcast_multiply_fusion.2) | copy-start | bytes 12292 | tf_op jit(solution)/shard_map/while
  572.7 19.4 %copy-start.7 = (f32[8,128]{1,0:T(8,128)S(1)}, f32[8,128]{1,0:T(8,128)}, u32[]{:S(2)}) copy-start(f32[8,128]{1,0:T(8,128)} %broadcast_multiply_fusion.2) | copy-start | bytes 12292 | tf_op jit(solution)/shard_map/while
  615.9 19.4 %copy-start.7 = (f32[8,128]{1,0:T(8,128)S(1)}, f32[8,128]{1,0:T(8,128)}, u32[]{:S(2)}) copy-start(f32[8,128]{1,0:T(8,128)} %broadcast_multiply_fusion.2) | copy-start | bytes 12292 | tf_op jit(solution)/shard_map/while
  659.0 19.4 %copy-start.7 = (f32[8,128]{1,0:T(8,128)S(1)}, f32[8,128]{1,0:T(8,128)}, u32[]{:S(2)}) copy-start(f32[8,128]{1,0:T(8,128)} %broadcast_multiply_fusion.2) | copy-start | bytes 12292 | tf_op jit(solution)/shard_map/while
  702.2 19.4 %copy-start.7 = (f32[8,128]{1,0:T(8,128)S(1)}, f32[8,128]{1,0:T(8,128)}, u32[]{:S(2)}) copy-start(f32[8,128]{1,0:T(8,128)} %broadcast_multiply_fusion.2) | copy-start | bytes 12292 | tf_op jit(solution)/shard_map/while
  745.4 19.4 %copy-start.7 = (f32[8,128]{1,0:T(8,128)S(1)}, f32[8,128]{1,0:T(8,128)}, u32[]{:S(2)}) copy-start(f32[8,128]{1,0:T(8,128)} %broadcast_multiply_fusion.2) | copy-start | bytes 12292 | tf_op jit(solution)/shard_map/while
  788.5 19.4 %copy-start.7 = (f32[8,128]{1,0:T(8,128)S(1)}, f32[8,128]{1,0:T(8,128)}, u32[]{:S(2)}) copy-start(f32[8,128]{1,0:T(8,128)} %broadcast_multiply_fusion.2) | copy-start | bytes 12292 | tf_op jit(solution)/shard_map/while
  (122 other events, 968.0 us)
Sparse Core Ops, SparseCore 0:
  14.0 67.6 all-gather.1
where the time goes:
time: 837 us; the launch traced here: 827 us
  other arithmetic  639 us (76%)
  waiting for transfers between devices  73.8 us (9%)
  local copies, waits for them, and re-layouts  73 us (9%)
  starting transfers between devices  21.4 us (3%)
  between operations  14.4 us (2%)
    reduce_sum x39, other arithmetic, force_terms(): jnp.sum(coupling * deltas[axis_id], axis=(1, 3))  386 us
    reduce_sum x13, other arithmetic, force_terms(): jnp.sum(masses * pair_cond / product_rho * gap * slope * square / (square...  96.7 us
    reduce_sum x13, other arithmetic, density_terms(): return jnp.sum(weight * sources[:, :, 7, None, :], axis=(1, 3))  82.3 us
    all_gather x1, waiting for transfers between devices, local(): incoming = lax.all_gather(leaving, ('gx', 'gy'), axis=0, tiled=True)  65.9 us
    sub x91, local copies, waits for them, and re-layouts, separation(): target[:, None, axis_id, :, None] - sources[:, :, axis_id, None, :]  24.3 us
  transfers between devices with their start and end apart: 9, of which 5 were waited for; matrix products, arithmetic and copies ran while one was open for 1% of the time, Pallas kernels for 0%

commit v1 on v0

v1 whole, which is shorter than its diff:
```python
import functools
import math

import jax
import jax.numpy as jnp
import numpy as np
from jax import lax
from jax.experimental import pallas as pl
from jax.experimental.pallas import tpu as pltpu
from jax.sharding import PartitionSpec as P

IN_CAP = 8
BND = 16
SLOTS = 104
SOURCES = 232
LANES = 128
LINKS = 9

SMOOTH = 0.5
KERNEL = 21.0 / (16.0 * math.pi * SMOOTH**3)
SOUND = math.sqrt(7.0)
VISC = 0.1
SOFT = 0.01 * SMOOTH**2
GRAVITY = 1.0
KAPPA = -2.0 * VISC * SOUND * SMOOTH
SLOPE = 5.0 * KERNEL / SMOOTH**2
TINY = 1e-30

F32 = jnp.float32
BF16 = jnp.bfloat16

PARTS = ((0, 0), (0, 1), (0, 2), (1, 0), (1, 1), (2, 0))
ONE = 24


def place_rows(entries, rows):
    left = np.zeros((rows, 32), np.float32)
    right = np.zeros((rows, 32), np.float32)
    for at, ((ls, lrow), (rs, rrow)) in enumerate(entries):
        left[at, lrow] = ls
        right[at, rrow] = rs
    return left, right


def pair_rows():
    x, v, n, vx = (0, 1, 2), (3, 4, 5), 6, 7
    part = lambda p, channel: 8 * p + channel
    still, moved = [], []
    for k in range(3):
        still += [((-2, part(a, x[k])), (1, part(b, x[k]))) for a, b in PARTS]
    still += [((1, ONE), (1, part(p, n))) for p in range(3)]
    still += [((1, part(p, n)), (1, ONE)) for p in range(3)]
    weights = np.zeros((27, 64), np.float32)
    steps = np.array([(c // 9 - 1, c // 3 % 3 - 1, c % 3 - 1) for c in range(27)], np.float32)
    for k in range(3):
        for p in range(3):
            weights[:, len(moved)] = steps[:, k]
            moved.append(((-2, part(p, x[k])), (1, ONE)))
            weights[:, len(moved)] = steps[:, k]
            moved.append(((2, ONE), (1, part(p, x[k]))))
    weights[:, len(moved)] = (steps * steps).sum(1)
    moved.append(((1, ONE), (1, ONE)))
    c_still, c_moved = [], []
    c_still += [((1, part(p, vx)), (1, ONE)) for p in range(3)]
    c_still += [((1, ONE), (1, part(p, vx))) for p in range(3)]
    for k in range(3):
        c_still += [((-1, part(a, v[k])), (1, part(b, x[k]))) for a, b in PARTS]
        c_still += [((-1, part(a, x[k])), (1, part(b, v[k]))) for a, b in PARTS]
    for k in range(3):
        for p in range(3):
            weights[:, 32 + len(c_moved)] = steps[:, k]
            c_moved.append(((-1, part(p, v[k])), (1, ONE)))
            weights[:, 32 + len(c_moved)] = steps[:, k]
            c_moved.append(((1, ONE), (1, part(p, v[k]))))
    tables = [
        place_rows(still, 32), place_rows(moved, 32), place_rows(c_still, 48), place_rows(c_moved, 32)
    ]
    left = np.concatenate([t[0] for t in tables])
    right = np.concatenate([t[1] for t in tables])
    full = np.zeros((32, 64, LANES), np.float32)
    full[:27] = weights[:, :, None]
    shift = np.zeros((32, 8, LANES), np.float32)
    shift[:27, 3:6] = steps[:, :, None]
    return left, right, full, shift


def heat_rows():
    part = lambda p, channel: 8 * p + channel
    rows = [((1, part(a, 0)), (1, part(b, 3))) for a, b in PARTS]
    rows += [((1, part(a, 1)), (1, part(b, 4))) for a, b in PARTS]
    rows += [((-1, ONE), (1, part(p, 5))) for p in range(3)]
    rows += [((-1, part(0, 2)), (1, part(p, 6))) for p in range(3)]
    return place_rows(rows, 32)


def parts_of(block):
    high = block.astype(BF16)
    rest = block - high.astype(F32)
    middle = rest.astype(BF16)
    low = rest - middle.astype(F32)
    row = lax.broadcasted_iota(jnp.int32, block.shape, 0)
    ones = jnp.where(row == 0, 1.0, 0.0)
    return jnp.concatenate(
        [high.astype(F32), middle.astype(F32), low, ones], 0
    ).astype(BF16)


def channels(state, b):
    x = state[b, 0:3, :]
    v = state[b, 3:6, :] * KAPPA
    n = jnp.sum(x * x, 0, keepdims=True)
    vx = jnp.sum(x * v, 0, keepdims=True)
    return jnp.concatenate([x, v, n, vx], 0)


def dot(a, b, contract):
    return lax.dot_general(a, b, ((contract), ((), ())), preferred_element_type=F32)


def spread(place, parts, out, b, base):
    got = dot(place, parts, ((1,), (0,))).astype(BF16)
    for q in range(2):
        out[base + b + q] = got[:, LANES * q : LANES * (q + 1)]


def build_pairs(state, place_left, place_right, left, right):
    def both(b, carry):
        parts = jnp.concatenate([parts_of(channels(state, 2 * b + q)) for q in range(2)], 1)
        spread(place_left[...], parts, left, 2 * b, 0)
        spread(place_right[...], parts, right, 2 * b, 0)
        return carry

    def one(b, carry):
        parts = jnp.concatenate([parts_of(channels(state, 2 * b + q)) for q in range(2)], 1)
        spread(place_right[...], parts, right, 2 * b, 0)
        return carry

    lax.fori_loop(0, SLOTS // 2, both, 0)
    lax.fori_loop(SLOTS // 2, SOURCES // 2, one, 0)


GROUPS = ((0, 1), (2, 3), (4,), (5, 6), (7, 8))


def source_row(rows, t, k):
    return t if k == 0 else rows[t * 8 + k - 1]


def pair_products(t, rows, codes, left, right, weights, at, still, moved, wat, into):
    near = left[t, at : at + still, :]
    far = left[t, at : at + still + moved, :]
    for group in GROUPS:
        columns = []
        for k in group:
            row = source_row(rows, t, k)
            column = right[row, at : at + still, :]
            if k >= 5:
                extra = right[row, at + still : at + still + moved, :]
                code = codes[t * 4 + k - 5]
                extra = extra * weights[code, wat : wat + moved, :]
                column = jnp.concatenate([column, extra], 0)
            columns.append(column)
        sources = columns[0] if len(columns) == 1 else jnp.concatenate(columns, 1)
        made = dot(far if group[0] >= 5 else near, sources, ((0,), (0,)))
        into[:, LANES * group[0] : LANES * (group[-1] + 1)] = made


def paired_loop(stage, work, close):
    stage(0, 0)

    def step(u, carry):
        t = 2 * u
        stage(t + 1, 1)
        work(t, 0)
        close(jnp.maximum(t - 1, 0), 1)
        stage(jnp.minimum(t + 2, SLOTS - 1), 0)
        work(t + 1, 1)
        close(t, 0)
        return carry

    lax.fori_loop(0, SLOTS // 2, step, 0)
    close(SLOTS - 1, 1)


def density_kernel(rows, codes, state, place_left, place_right, weights, out, left, right, s0, s1, a0, a1):
    build_pairs(state, place_left, place_right, left, right)
    squares, sums = (s0, s1), (a0, a1)

    def stage(t, slot):
        pair_products(t, rows, codes, left, right, weights, 0, 32, 32, 0, squares[slot])

    def work(t, slot):
        square = squares[slot]
        masses = [state.at[source_row(rows, t, k)] for k in range(LINKS)]
        for o in range(16):
            total = None
            for k in range(LINKS):
                s = jnp.maximum(square[8 * o : 8 * o + 8, LANES * k : LANES * (k + 1)], TINY)
                w = jnp.maximum(1.0 - s * lax.rsqrt(s), 0.0)
                w2 = w * w
                term = (w2 * w2) * (1.25 - w) * masses[k][7:8, :]
                total = term if total is None else total + term
            sums[slot][8 * o : 8 * o + 8, :] = total

    def close(t, slot):
        rho = jnp.sum(sums[slot][...].T, 0, keepdims=True) * (4.0 * KERNEL)
        out[pl.ds(t, 1), :] = jnp.where(state[t, 7:8, :] > 0.0, rho, 0.0)

    paired_loop(stage, work, close)


def force_kernel(rows, codes, state, rho_table, place_left, place_right, heat_left, heat_right, weights, shift,
                 out_a, out_h, left, right, hleft, hright, per_source,
                 s0, s1, c0, c1, h0, h1, r0, r1, i0, i1, a0, a1):
    build_pairs(state, place_left, place_right, left, right)

    def build(b2, carry, both):
        mixed = []
        for q in range(2):
            b = 2 * b2 + q
            x, heat, mass, wall = state[b, 0:3, :], state[b, 6:7, :], state[b, 7:8, :], state[b, 8:9, :]
            rho = jnp.where(mass > 0.0, rho_table[pl.ds(b, 1), :], 1.0)
            inverse = 1.0 / rho
            r2 = rho * rho
            pressure = (r2 * r2 * r2 * rho - 1.0) * (inverse * inverse)
            zero = jnp.zeros_like(rho)
            per_source[b] = jnp.concatenate([rho, pressure, mass, mass * x, inverse, zero], 0)
            ratio = mass * inverse
            a = ratio * (2.0 + 1.2 * wall)
            bb = ratio * (1.2 + 3.6 * wall)
            mixed.append(parts_of(jnp.concatenate([heat, heat * wall, wall, a, bb, a * heat, bb * heat, zero], 0)))
        parts = jnp.concatenate(mixed, 1)
        if both:
            spread(heat_left[...], parts, hleft, 2 * b2, 0)
        spread(heat_right[...], parts, hright, 2 * b2, 0)
        return carry

    lax.fori_loop(0, SLOTS // 2, functools.partial(build, both=True), 0)
    lax.fori_loop(SLOTS // 2, SOURCES // 2, functools.partial(build, both=False), 0)
    squares, closings, heats, shifted, own, sums = (s0, s1), (c0, c1), (h0, h1), (r0, r1), (i0, i1), (a0, a1)

    def stage(t, slot):
        pair_products(t, rows, codes, left, right, weights, 0, 32, 32, 0, squares[slot])
        pair_products(t, rows, codes, left, right, weights, 64, 48, 32, 32, closings[slot])
        for group in GROUPS:
            columns = [hright[source_row(rows, t, k)] for k in group]
            sources = columns[0] if len(columns) == 1 else jnp.concatenate(columns, 1)
            heats[slot][:, LANES * group[0] : LANES * (group[-1] + 1)] = dot(hleft[t], sources, ((0,), (0,)))
        for f in range(4):
            row = source_row(rows, t, 5 + f)
            shifted[slot][f] = per_source[row] + shift[codes[t * 4 + f]] * per_source[row, 2:3, :]
        for at in range(2):
            own[slot][:, LANES * at : LANES * (at + 1)] = jnp.broadcast_to(per_source[t, at : at + 1, :], (LANES, LANES)).T

    def work(t, slot):
        views = [per_source.at[source_row(rows, t, k)] if k < 5 else shifted[slot].at[k - 5] for k in range(LINKS)]
        for o in range(16):
            eight = slice(8 * o, 8 * o + 8)
            rho_i = own[slot][eight, 0:LANES]
            p_i = own[slot][eight, LANES : 2 * LANES]
            totals = [None] * 5
            for k in range(LINKS):
                lanes = slice(LANES * k, LANES * (k + 1))
                view = views[k]
                s = jnp.maximum(squares[slot][eight, lanes], TINY)
                w = jnp.maximum(1.0 - s * lax.rsqrt(s), 0.0)
                w3 = w * w * w
                z = w3 * pl.reciprocal(s + SOFT, approx=True)
                viscous = jnp.maximum(closings[slot][eight, lanes], 0.0) * pl.reciprocal(rho_i + view[0:1, :], approx=True)
                coupling = (p_i + view[1:2, :]) * w3 + viscous * z
                terms = [coupling * view[2 + at : 3 + at, :] for at in range(4)]
                terms.append((s * z) * heats[slot][eight, lanes])
                totals = [term if total is None else total + term for total, term in zip(totals, terms)]
            for at in range(5):
                sums[slot][eight, LANES * at : LANES * (at + 1)] = totals[at]

    def close(t, slot):
        got = [jnp.sum(sums[slot][:, LANES * at : LANES * (at + 1)].T, 0, keepdims=True) for at in range(5)]
        living = state[t, 7:8, :] > 0.0
        fluid = 1.0 - state[t, 8:9, :]
        lines = []
        for k in range(3):
            push = SLOPE * (state[t, k : k + 1, :] * got[0] - got[1 + k])
            if k == 2:
                push = push - GRAVITY
            lines.append(jnp.where(living, push * fluid, 0.0))
        out_a[t] = jnp.concatenate(lines, 0)
        out_h[pl.ds(t, 1), :] = jnp.where(living, -SLOPE * got[4] * per_source[t, 6:7, :], 0.0)

    paired_loop(stage, work, close)


SMEM = pl.BlockSpec(memory_space=pltpu.SMEM)
VMEM = pl.BlockSpec(memory_space=pltpu.VMEM)


def density_call(rows, codes, state, place_left, place_right, weights):
    wide = (LANES, LINKS * LANES)
    return pl.pallas_call(
        density_kernel,
        out_shape=jax.ShapeDtypeStruct((SLOTS, LANES), F32),
        in_specs=[SMEM] * 2 + [VMEM] * 4,
        out_specs=VMEM,
        scratch_shapes=[
            pltpu.VMEM((SLOTS, 64, LANES), BF16),
            pltpu.VMEM((SOURCES, 64, LANES), BF16),
            pltpu.VMEM(wide, F32), pltpu.VMEM(wide, F32),
            pltpu.VMEM((LANES, LANES), F32), pltpu.VMEM((LANES, LANES), F32),
        ],
        compiler_params=pltpu.CompilerParams(vmem_limit_bytes=32 << 20),
        name="density_pass",
    )(rows, codes, state, place_left, place_right, weights)


def force_call(rows, codes, state, rho_table, place_left, place_right, heat_left, heat_right, weights, shift):
    wide = (LANES, LINKS * LANES)
    return pl.pallas_call(
        force_kernel,
        out_shape=(
            jax.ShapeDtypeStruct((SLOTS, 3, LANES), F32),
            jax.ShapeDtypeStruct((SLOTS, LANES), F32),
        ),
        in_specs=[SMEM] * 2 + [VMEM] * 8,
        out_specs=(VMEM, VMEM),
        scratch_shapes=[
            pltpu.VMEM((SLOTS, 144, LANES), BF16),
            pltpu.VMEM((SOURCES, 144, LANES), BF16),
            pltpu.VMEM((SLOTS, 32, LANES), BF16),
            pltpu.VMEM((SOURCES, 32, LANES), BF16),
            pltpu.VMEM((SOURCES, 8, LANES), F32),
        ]
        + [pltpu.VMEM(wide, F32)] * 6
        + [pltpu.VMEM((4, 8, LANES), F32)] * 2
        + [pltpu.VMEM((LANES, 2 * LANES), F32)] * 2
        + [pltpu.VMEM((LANES, 5 * LANES), F32)] * 2,
        compiler_params=pltpu.CompilerParams(vmem_limit_bytes=48 << 20),
        name="force_pass",
    )(rows, codes, state, rho_table, place_left, place_right, heat_left, heat_right, weights, shift)


def padded(shard, sides, width):
    for axis, dim in sides:
        size, length = (lax.axis_size(axis), shard.shape[dim])
        up = [(i, (i + 1) % size) for i in range(size - 1)]
        down = [(j, i) for i, j in up]
        last = lax.slice_in_dim(shard, length - width, length, axis=dim)
        first = lax.slice_in_dim(shard, 0, width, axis=dim)
        before = lax.ppermute(last, axis, up)
        after = lax.ppermute(first, axis, down)
        shard = jnp.concatenate([before, shard, after], axis=dim)
    return shard


def eight_around(haloed):
    flat = haloed.reshape((9,) + haloed.shape[2:])
    picked = jnp.concatenate([flat[:4], flat[5:]], 0)
    return picked.reshape((8 * haloed.shape[2],) + haloed.shape[3:])


def local(
    cell_local_coords,
    particle_speeds,
    thermal_state,
    particle_weights,
    boundary_flag,
    departing_local_groups,
    migrant_target_holder,
    target_entry_inputs,
    adjacent_cell_label,
):
    along = lax.axis_size("gy")
    myself = lax.axis_index("gx") * along + lax.axis_index("gy")
    state_tables = jnp.concatenate(
        [
            cell_local_coords,
            particle_speeds,
            thermal_state[:, None, :],
            particle_weights[:, None, :],
            boundary_flag.astype(jnp.float32)[:, None, :],
        ],
        1,
    )
    width = state_tables.shape[1]
    lanes = state_tables.shape[2]
    chosen = departing_local_groups[0]
    leaving = jnp.take(state_tables, chosen, axis=0)
    dest_flat = migrant_target_holder.reshape(-1)
    total = dest_flat.shape[0]
    listing = jnp.arange(total)
    match = dest_flat == myself
    ranking = jnp.cumsum(match.astype(jnp.int32)) - 1
    slot_ids = jnp.arange(IN_CAP)
    taken = match[None, :] & (ranking[None, :] == slot_ids[:, None])
    wanted = jnp.sum(jnp.where(taken, listing[None, :], 0), 1)
    present = jnp.any(taken, 1)
    incoming = lax.all_gather(leaving, ("gx", "gy"), axis=0, tiled=True)
    picked = jnp.take(incoming, wanted, axis=0)
    arrived = jnp.where(present[:, None, None], picked, 0.0)
    numbers = jnp.arange(state_tables.shape[0])
    departed = jnp.any(numbers[:, None] == chosen[None, :], 1)
    blocks = jnp.concatenate([arrived, jnp.where(departed[:, None, None], 0.0, state_tables)], 0)
    exported = blocks[:BND].reshape((1, 1, BND, width, lanes))
    haloed = padded(exported, (("gx", 0), ("gy", 1)), 1)
    state = jnp.concatenate([blocks, eight_around(haloed)], 0)
    rows = target_entry_inputs.reshape(-1)
    codes = (adjacent_cell_label + (adjacent_cell_label >= 13).astype(jnp.int32)).reshape(-1)
    left, right, weights, shift = pair_rows()
    heat_left, heat_right = heat_rows()
    left, right, weights, heat_left, heat_right = (
        jnp.asarray(a, BF16) for a in (left, right, weights, heat_left, heat_right)
    )
    shift = jnp.asarray(shift)
    density = density_call(rows, codes, state, left[:64], right[:64], weights)
    again = eight_around(
        padded(density[:BND].reshape((1, 1, BND, lanes)), (("gx", 0), ("gy", 1)), 1)
    )
    rho_table = jnp.concatenate([density, again], 0)
    acceleration, heating = force_call(
        rows, codes, state, rho_table, left, right, heat_left, heat_right, weights, shift
    )
    return density, acceleration, heating


def solution(mesh):
    return jax.shard_map(
        local,
        mesh=mesh,
        in_specs=(
            P(("gx", "gy"), None, None),
            P(("gx", "gy"), None, None),
            P(("gx", "gy"), None),
            P(("gx", "gy"), None),
            P(("gx", "gy"), None),
            P(("gx", "gy"), None),
            P(),
            P(("gx", "gy"), None),
            P(("gx", "gy"), None),
        ),
        out_specs=(P(("gx", "gy"), None), P(("gx", "gy"), None, None), P(("gx", "gy"), None)),
        check_vma=False,
    )
```

time: 837 us -> 312 us (0.37)
  other arithmetic: 639 us -> 5.06 us
  Pallas kernels: 0 us -> 174 us
  local copies, waits for them, and re-layouts: 73 us -> 9.5 us
  waiting for transfers between devices: 73.8 us -> 86.6 us
    reduce_sum x65 -> x0, other arithmetic: 565 us -> none  [the longest x39 386 us: force_terms(): jnp.sum(coupling * deltas[axis_id], axis=(1, 3))]
    pallas_call x0 -> x2, Pallas kernels: none -> 174 us  [the longest x1 123 us: force_call(): pl.pallas_call(force_kernel, out_shape=(jax.ShapeDtypeStruct((SLOTS, 3, L...]
    gather x53 -> x1, local copies, waits for them, and re-layouts: 28.4 us -> 2.14 us  [local(): picked = jnp.take(incoming, wanted, axis=0)]
    select_n x45 -> x2, other arithmetic: 25.7 us -> 0.09 us  [the longest x1 0.08 us: local(): arrived = jnp.where(present[:, None, None], picked, 0.0)]
    sub x143 -> x0, local copies, waits for them, and re-layouts: 24.9 us -> none  [the longest x91 24.3 us: separation(): target[:, None, axis_id, :, None] - sources[:, :, axis_id, None, :]]
    and x27 -> x1, other arithmetic: 17.2 us -> 0.01 us  [local(): picked = jnp.take(incoming, wanted, axis=0)]
    ppermute x4, waiting for transfers between devices: 5.49 us -> 14.9 us  [padded(): after = lax.ppermute(first, axis, down)]
  transfers between devices with their start and end apart: 9 -> 9, of which waited for: 5 -> 7; matrix products, arithmetic and copies ran while one was open for 1% -> 1% of each run, Pallas kernels for 0% -> 0%
where the time goes in v1:
time: 312 us; the launch traced here: 307 us
  Pallas kernels  174 us (56%)
  waiting for transfers between devices  86.6 us (28%)
  starting transfers between devices  17.1 us (5%)
  between operations  14.4 us (5%)
  local copies, waits for them, and re-layouts  9.5 us (3%)
  other arithmetic  5.06 us (2%)
    pallas_call x1, Pallas kernels, force_call(): pl.pallas_call(force_kernel, out_shape=(jax.ShapeDtypeStruct((SLOTS, 3, L...  123 us
    all_gather x1, waiting for transfers between devices, local(): incoming = lax.all_gather(leaving, ('gx', 'gy'), axis=0, tiled=True)  66.1 us
    pallas_call x1, Pallas kernels, density_call(): pl.pallas_call(density_kernel, out_shape=jax.ShapeDtypeStruct((SLOTS, LAN...  51.2 us
    ppermute x4, waiting for transfers between devices, padded(): after = lax.ppermute(first, axis, down)  14.9 us
    ppermute x4, starting transfers between devices, padded(): before = lax.ppermute(last, axis, up)  11.9 us
  transfers between devices with their start and end apart: 9, of which 7 were waited for; matrix products, arithmetic and copies ran while one was open for 1% of the time, Pallas kernels for 0%

profile of v1, /device:TPU:0, one launch (start us, length us, event | category | flops | bytes accessed | tf_op | source)
XLA Modules:
  0.0 307.0 jit_solution(8744437458637751334)
XLA Ops:
  8.5 1.0 copy.39
  9.6 1.0 copy.40
  10.6 0.8 convert_element_type.16
  11.4 1.2 concatenate.31
  15.6 66.1 %all-gather.2.cloned.1.call-done = f32[256,9,128]{2,1,0:T(8,128)} async-done(((f32[2,9,128]{2,1,0:T(8,128)}), f32[256,9,128]{2,1,0:T(8,128)}) %all-gather.2.cloned.1.call-update) | async-done | bytes 1179664 | tf_op jit(solution)/shard_map/all_gather | solution.py:396
  81.7 2.1 gather_fusion.1
  84.0 2.2 collective-permute-start
  86.2 1.3 collective-permute-start.1
  87.7 1.7 collective-permute-done.1
  89.5 2.2 collective-permute-start.2
  91.6 1.3 collective-permute-start.3
  93.2 5.4 %collective-permute-done.2 = f32[3,1,16,9,128]{4,3,2,1,0:T(8,128)S(1)} collective-permute-done((f32[3,1,16,9,128]{4,3,2,1,0:T(8,128)S(1)}, f32[3,1,16,9,128]{4,3,2,1,0:T(8,128)S(1)}, u32[]{:S(2)}, u32[]{:S(2)}) %collective-permute-start.2) | collective-permute-done | bytes 221216 | tf_op jit(solution)/shard_map/ppermute | solution.py:348
  98.5 4.7 %collective-permute-done.3 = f32[3,1,16,9,128]{4,3,2,1,0:T(8,128)S(1)} collective-permute-done((f32[3,1,16,9,128]{4,3,2,1,0:T(8,128)S(1)}, f32[3,1,16,9,128]{4,3,2,1,0:T(8,128)S(1)}, u32[]{:S(2)}, u32[]{:S(2)}) %collective-permute-start.3) | collective-permute-done | bytes 221216 | tf_op jit(solution)/shard_map/ppermute | solution.py:349
  103.8 0.9 copy-done
  104.7 51.2 %density_pass.1 = f32[104,128]{1,0:T(8,128)} custom-call(s32[832]{0:T(1024)S(1)} %reshape.122.rows, s32[416]{0:T(512)S(1)} %reshape.123.codes, f32[232,9,128]{2,1,0:T(8,128)S(1)} %pad_maximum_fusion.state, bf16[64,32]{1,0:T(8,128)(2,1)S(1)} %copy-done.4, bf16[64,32]{1,0:T(8,128)(2,1)S(1)} %copy-done.5, bf16[32,64,128]{2,1,0:T(8,128)(2,1)S(1)} %copy-done), custom_call_target="tpu_custom_call" | custom-call | tf_op jit(solution)/shard_map/density_pass/pallas_call | solution.py:299
  155.9 0.7 slice_bitcast_fusion
  156.6 4.1 %collective-permute-start.4 = (f32[1,1,16,128]{3,2,1,0:T(8,128)S(1)}, f32[1,1,16,128]{3,2,1,0:T(8,128)S(1)}, u32[]{:S(2)}, u32[]{:S(2)}) collective-permute-start(f32[1,1,16,128]{3,2,1,0:T(8,128)S(1)} %slice_bitcast_fusion), channel_id=1, source_target_pairs={{0,16},{16,32},{32,48},{48,64},{64,80},{80,96},{96,112},{1,17},{17... | collective-permute-start | bytes 24584 | tf_op jit(solution)/shard_map/ppermute | solution.py:348
  160.7 1.3 collective-permute-start.5
  162.0 4.3 %collective-permute-done.5 = f32[1,1,16,128]{3,2,1,0:T(8,128)S(1)} collective-permute-done((f32[1,1,16,128]{3,2,1,0:T(8,128)S(1)}, f32[1,1,16,128]{3,2,1,0:T(8,128)S(1)}, u32[]{:S(2)}, u32[]{:S(2)}) %collective-permute-start.5) | collective-permute-done | bytes 8224 | tf_op jit(solution)/shard_map/ppermute | solution.py:349
  166.3 3.5 %collective-permute-start.6 = (f32[3,1,16,128]{3,2,1,0:T(8,128)S(1)}, f32[3,1,16,128]{3,2,1,0:T(8,128)S(1)}, u32[]{:S(2)}, u32[]{:S(2)}) collective-permute-start(f32[3,1,16,128]{3,2,1,0:T(8,128)S(1)} %pad_maximum_fusion.8), channel_id=1, source_target_pairs={{0,1},{1,2},{2,3},{3,4},{4,5},{5,6},{6,7},{7,8},{8,9},{9,10},{10,1... | collective-permute-start | bytes 73736 | tf_op jit(solution)/shard_map/ppermute | solution.py:348
  169.8 1.3 collective-permute-start.7
  171.3 4.2 %collective-permute-done.7 = f32[3,1,16,128]{3,2,1,0:T(8,128)S(1)} collective-permute-done((f32[3,1,16,128]{3,2,1,0:T(8,128)S(1)}, f32[3,1,16,128]{3,2,1,0:T(8,128)S(1)}, u32[]{:S(2)}, u32[]{:S(2)}) %collective-permute-start.7) | collective-permute-done | bytes 24608 | tf_op jit(solution)/shard_map/ppermute | solution.py:349
  175.5 0.8 pad_maximum_fusion.5.rho_table
  176.4 123.1 %force_pass.1 = (f32[104,3,128]{2,1,0:T(4,128)S(1)}, f32[104,128]{1,0:T(8,128)}) custom-call(s32[832]{0:T(1024)S(1)} %reshape.122.rows, s32[416]{0:T(512)S(1)} %reshape.123.codes, f32[232,9,128]{2,1,0:T(8,128)S(1)} %pad_maximum_fusion.state, f32[232,128]{1,0:T(8,128)S(1)} %pad_maximum_fusion.5.rho_table, bf16[144,32]{1,0:T(8,128)(2,1)S(1)} %copy-done.2, ...), custom_call_target="tpu_custom_call" | custom-call | tf_op jit(solution)/shard_map/force_pass/pallas_call | solution.py:317
  (67 shorter events, 6.2 us)
Async XLA Ops:
  7.2 6.7 %copy-start.10 = (s32[128,2]{0,1:T(2,128)S(1)}, s32[128,2]{0,1:T(2,128)}, u32[]{:S(2)}) copy-start(s32[128,2]{0,1:T(2,128)} %param.21) | copy-start | bytes 3076
  7.2 74.6 %all-gather.2.cloned.1.call-start = ((), (), s32[]{:S(2)}) async-start(), calls=%async_computation | async-start | bytes 2113536 | tf_op jit(solution)/shard_map/all_gather | solution.py:396
  8.5 6.8 %copy-start.11 = (s32[1,2]{1,0:T(1,128)S(1)}, s32[1,2]{1,0:T(1,128)}, u32[]{:S(2)}) copy-start(s32[1,2]{1,0:T(1,128)} %param.20) | copy-start | bytes 28
  15.4 72.1 %copy-start.8 = (s32[104,8]{0,1:T(8,128)S(1)}, s32[104,8]{0,1:T(8,128)}, u32[]{:S(2)}) copy-start(s32[104,8]{0,1:T(8,128)} %param.22) | copy-start | bytes 9988
  15.6 77.3 %copy-start.9 = (s32[104,4]{0,1:T(4,128)S(1)}, s32[104,4]{0,1:T(4,128)}, u32[]{:S(2)}) copy-start(s32[104,4]{0,1:T(4,128)} %param.23) | copy-start | bytes 4996
  84.0 3.7 %collective-permute-start = (f32[1,1,16,9,128]{4,3,2,1,0:T(8,128)S(1)}, f32[1,1,16,9,128]{4,3,2,1,0:T(8,128)S(1)}, u32[]{:S(2)}, u32[]{:S(2)}) collective-permute-start(f32[1,1,16,9,128]{4,3,2,1,0:T(8,128)S(1)} %fusion), channel_id=1, source_target_pairs={{0,16},{16,32},{32,48},{48,64},{64,80},{80,96},{96,112},{1,17},{17... | collective-permute-start | bytes 221192 | tf_op jit(solution)/shard_map/ppermute | solution.py:348
  86.2 3.2 %collective-permute-start.1 = (f32[1,1,16,9,128]{4,3,2,1,0:T(8,128)S(1)}, f32[1,1,16,9,128]{4,3,2,1,0:T(8,128)S(1)}, u32[]{:S(2)}, u32[]{:S(2)}) collective-permute-start(f32[1,1,16,9,128]{4,3,2,1,0:T(8,128)S(1)} %fusion), channel_id=1, source_target_pairs={{16,0},{32,16},{48,32},{64,48},{80,64},{96,80},{112,96},{17,1},{33... | collective-permute-start | bytes 221192 | tf_op jit(solution)/shard_map/ppermute | solution.py:349
  89.5 9.1 %collective-permute-start.2 = (f32[3,1,16,9,128]{4,3,2,1,0:T(8,128)S(1)}, f32[3,1,16,9,128]{4,3,2,1,0:T(8,128)S(1)}, u32[]{:S(2)}, u32[]{:S(2)}) collective-permute-start(f32[3,1,16,9,128]{4,3,2,1,0:T(8,128)S(1)} %pad_maximum_fusion.3), channel_id=1, source_target_pairs={{0,1},{1,2},{2,3},{3,4},{4,5},{5,6},{6,7},{7,8},{8,9},{9,10},{10,1... | collective-permute-start | bytes 663560 | tf_op jit(solution)/shard_map/ppermute | solution.py:348
  91.6 11.6 %collective-permute-start.3 = (f32[3,1,16,9,128]{4,3,2,1,0:T(8,128)S(1)}, f32[3,1,16,9,128]{4,3,2,1,0:T(8,128)S(1)}, u32[]{:S(2)}, u32[]{:S(2)}) collective-permute-start(f32[3,1,16,9,128]{4,3,2,1,0:T(8,128)S(1)} %pad_maximum_fusion.3), channel_id=1, source_target_pairs={{1,0},{2,1},{3,2},{4,3},{5,4},{6,5},{7,6},{8,7},{9,8},{10,9},{11,1... | collective-permute-start | bytes 663560 | tf_op jit(solution)/shard_map/ppermute | solution.py:349
  103.6 1.0 copy-start
  103.6 1.0 copy-start.4
  103.6 1.0 copy-start.5
  104.6 71.7 %copy-start.1 = (f32[32,8,128]{2,1,0:T(8,128)S(1)}, f32[32,8,128]{2,1,0:T(8,128)}, u32[]{:S(2)}) copy-start(f32[32,8,128]{2,1,0:T(8,128)} %constant.71.clone.shift) | copy-start | bytes 393220
  104.6 71.7 %copy-start.2 = (bf16[144,32]{1,0:T(8,128)(2,1)S(1)}, bf16[144,32]{1,0:T(8,128)(2,1)}, u32[]{:S(2)}) copy-start(bf16[144,32]{1,0:T(8,128)(2,1)} %constant.66.clone.place_left) | copy-start | bytes 27652
  104.6 71.7 %copy-start.3 = (bf16[144,32]{1,0:T(8,128)(2,1)S(1)}, bf16[144,32]{1,0:T(8,128)(2,1)}, u32[]{:S(2)}) copy-start(bf16[144,32]{1,0:T(8,128)(2,1)} %constant.67.clone.place_right) | copy-start | bytes 27652
  104.7 71.7 %copy-start.6 = (bf16[32,32]{1,0:T(8,128)(2,1)S(1)}, bf16[32,32]{1,0:T(8,128)(2,1)}, u32[]{:S(2)}) copy-start(bf16[32,32]{1,0:T(8,128)(2,1)} %constant.69.clone.heat_left) | copy-start | bytes 6148
  104.7 71.7 %copy-start.7 = (bf16[32,32]{1,0:T(8,128)(2,1)S(1)}, bf16[32,32]{1,0:T(8,128)(2,1)}, u32[]{:S(2)}) copy-start(bf16[32,32]{1,0:T(8,128)(2,1)} %constant.70.clone.heat_right) | copy-start | bytes 6148
  156.6 5.4 %collective-permute-start.4 = (f32[1,1,16,128]{3,2,1,0:T(8,128)S(1)}, f32[1,1,16,128]{3,2,1,0:T(8,128)S(1)}, u32[]{:S(2)}, u32[]{:S(2)}) collective-permute-start(f32[1,1,16,128]{3,2,1,0:T(8,128)S(1)} %slice_bitcast_fusion), channel_id=1, source_target_pairs={{0,16},{16,32},{32,48},{48,64},{64,80},{80,96},{96,112},{1,17},{17... | collective-permute-start | bytes 24584 | tf_op jit(solution)/shard_map/ppermute | solution.py:348
  160.7 5.6 %collective-permute-start.5 = (f32[1,1,16,128]{3,2,1,0:T(8,128)S(1)}, f32[1,1,16,128]{3,2,1,0:T(8,128)S(1)}, u32[]{:S(2)}, u32[]{:S(2)}) collective-permute-start(f32[1,1,16,128]{3,2,1,0:T(8,128)S(1)} %slice_bitcast_fusion), channel_id=1, source_target_pairs={{16,0},{32,16},{48,32},{64,48},{80,64},{96,80},{112,96},{17,1},{33... | collective-permute-start | bytes 24584 | tf_op jit(solution)/shard_map/ppermute | solution.py:349
  166.3 5.0 %collective-permute-start.6 = (f32[3,1,16,128]{3,2,1,0:T(8,128)S(1)}, f32[3,1,16,128]{3,2,1,0:T(8,128)S(1)}, u32[]{:S(2)}, u32[]{:S(2)}) collective-permute-start(f32[3,1,16,128]{3,2,1,0:T(8,128)S(1)} %pad_maximum_fusion.8), channel_id=1, source_target_pairs={{0,1},{1,2},{2,3},{3,4},{4,5},{5,6},{6,7},{7,8},{8,9},{9,10},{10,1... | collective-permute-start | bytes 73736 | tf_op jit(solution)/shard_map/ppermute | solution.py:348
  169.8 5.7 %collective-permute-start.7 = (f32[3,1,16,128]{3,2,1,0:T(8,128)S(1)}, f32[3,1,16,128]{3,2,1,0:T(8,128)S(1)}, u32[]{:S(2)}, u32[]{:S(2)}) collective-permute-start(f32[3,1,16,128]{3,2,1,0:T(8,128)S(1)} %pad_maximum_fusion.8), channel_id=1, source_target_pairs={{1,0},{2,1},{3,2},{4,3},{5,4},{6,5},{7,6},{8,7},{9,8},{10,9},{11,1... | collective-permute-start | bytes 73736 | tf_op jit(solution)/shard_map/ppermute | solution.py:349
Sparse Core Ops, SparseCore 0:
  14.0 67.6 all-gather.1

commit v2 on v1

--- a/solution.py
+++ b/solution.py
@@ -11,6 +11,9 @@
 
 IN_CAP = 8
 BND = 16
+MIG = 2
+N_GX = 8
+N_GY = 16
 SLOTS = 104
 SOURCES = 232
 LANES = 128
@@ -117,26 +120,32 @@
     return lax.dot_general(a, b, ((contract), ((), ())), preferred_element_type=F32)
 
 
-def spread(place, parts, out, b, base):
+UNROLL = 4
+
+
+def twice(build):
+    own, every = SLOTS // (2 * UNROLL), SOURCES // (2 * UNROLL)
+    lax.fori_loop(0, own, functools.partial(build, both=True), 0)
+    lax.fori_loop(own, every, functools.partial(build, both=False), 0)
+
+
+def spread(place, parts, out, b):
     got = dot(place, parts, ((1,), (0,))).astype(BF16)
     for q in range(2):
-        out[base + b + q] = got[:, LANES * q : LANES * (q + 1)]
+        out[b + q] = got[:, LANES * q : LANES * (q + 1)]
 
 
 def build_pairs(state, place_left, place_right, left, right):
-    def both(b, carry):
-        parts = jnp.concatenate([parts_of(channels(state, 2 * b + q)) for q in range(2)], 1)
-        spread(place_left[...], parts, left, 2 * b, 0)
-        spread(place_right[...], parts, right, 2 * b, 0)
+    def build(b, carry, both):
+        for u in range(UNROLL):
+            at = 2 * (UNROLL * b + u)
+            parts = jnp.concatenate([parts_of(channels(state, at + q)) for q in range(2)], 1)
+            if both:
+                spread(place_left[...], parts, left, at)
+            spread(place_right[...], parts, right, at)
         return carry
 
-    def one(b, carry):
-        parts = jnp.concatenate([parts_of(channels(state, 2 * b + q)) for q in range(2)], 1)
-        spread(place_right[...], parts, right, 2 * b, 0)
-        return carry
-
-    lax.fori_loop(0, SLOTS // 2, both, 0)
-    lax.fori_loop(SLOTS // 2, SOURCES // 2, one, 0)
+    twice(build)
 
 
 GROUPS = ((0, 1), (2, 3), (4,), (5, 6), (7, 8))
@@ -163,19 +172,30 @@
         sources = columns[0] if len(columns) == 1 else jnp.concatenate(columns, 1)
         made = dot(far if group[0] >= 5 else near, sources, ((0,), (0,)))
         into[:, LANES * group[0] : LANES * (group[-1] + 1)] = made
+        yield
+
+
+def run(steps):
+    for _ in steps:
+        pass
 
 
 def paired_loop(stage, work, close):
-    stage(0, 0)
+    run(stage(0, 0))
+
+    def alternate(a, b):
+        live = [a, b]
+        while live:
+            for g in list(live):
+                if next(g, live) is live:
+                    live.remove(g)
 
     def step(u, carry):
         t = 2 * u
-        stage(t + 1, 1)
-        work(t, 0)
         close(jnp.maximum(t - 1, 0), 1)
-        stage(jnp.minimum(t + 2, SLOTS - 1), 0)
-        work(t + 1, 1)
+        alternate(work(t, 0), stage(t + 1, 1))
         close(t, 0)
+        alternate(work(t + 1, 1), stage(jnp.minimum(t + 2, SLOTS - 1), 0))
         return carry
 
     lax.fori_loop(0, SLOTS // 2, step, 0)
@@ -187,7 +207,7 @@
     squares, sums = (s0, s1), (a0, a1)
 
     def stage(t, slot):
-        pair_products(t, rows, codes, left, right, weights, 0, 32, 32, 0, squares[slot])
+        yield from pair_products(t, rows, codes, left, right, weights, 0, 32, 32, 0, squares[slot])
 
     def work(t, slot):
         square = squares[slot]
@@ -201,6 +221,7 @@
                 term = (w2 * w2) * (1.25 - w) * masses[k][7:8, :]
                 total = term if total is None else total + term
             sums[slot][8 * o : 8 * o + 8, :] = total
+            yield
 
     def close(t, slot):
         rho = jnp.sum(sums[slot][...].T, 0, keepdims=True) * (4.0 * KERNEL)
@@ -214,38 +235,39 @@
                  s0, s1, c0, c1, h0, h1, r0, r1, i0, i1, a0, a1):
     build_pairs(state, place_left, place_right, left, right)
 
-    def build(b2, carry, both):
-        mixed = []
-        for q in range(2):
-            b = 2 * b2 + q
-            x, heat, mass, wall = state[b, 0:3, :], state[b, 6:7, :], state[b, 7:8, :], state[b, 8:9, :]
-            rho = jnp.where(mass > 0.0, rho_table[pl.ds(b, 1), :], 1.0)
-            inverse = 1.0 / rho
-            r2 = rho * rho
-            pressure = (r2 * r2 * r2 * rho - 1.0) * (inverse * inverse)
-            zero = jnp.zeros_like(rho)
-            per_source[b] = jnp.concatenate([rho, pressure, mass, mass * x, inverse, zero], 0)
-            ratio = mass * inverse
-            a = ratio * (2.0 + 1.2 * wall)
-            bb = ratio * (1.2 + 3.6 * wall)
-            mixed.append(parts_of(jnp.concatenate([heat, heat * wall, wall, a, bb, a * heat, bb * heat, zero], 0)))
-        parts = jnp.concatenate(mixed, 1)
-        if both:
-            spread(heat_left[...], parts, hleft, 2 * b2, 0)
-        spread(heat_right[...], parts, hright, 2 * b2, 0)
+    def heat_channels(b):
+        x, heat, mass, wall = state[b, 0:3, :], state[b, 6:7, :], state[b, 7:8, :], state[b, 8:9, :]
+        rho = jnp.where(mass > 0.0, rho_table[pl.ds(b, 1), :], 1.0)
+        inverse = 1.0 / rho
+        r2 = rho * rho
+        pressure = (r2 * r2 * r2 * rho - 1.0) * (inverse * inverse)
+        zero = jnp.zeros_like(rho)
+        per_source[b] = jnp.concatenate([rho, pressure, mass, mass * x, inverse, zero], 0)
+        ratio = mass * inverse
+        a = ratio * (2.0 + 1.2 * wall)
+        bb = ratio * (1.2 + 3.6 * wall)
+        return jnp.concatenate([heat, heat * wall, wall, a, bb, a * heat, bb * heat, zero], 0)
+
+    def build(b, carry, both):
+        for u in range(UNROLL):
+            at = 2 * (UNROLL * b + u)
+            parts = jnp.concatenate([parts_of(heat_channels(at + q)) for q in range(2)], 1)
+            if both:
+                spread(heat_left[...], parts, hleft, at)
+            spread(heat_right[...], parts, hright, at)
         return carry
 
-    lax.fori_loop(0, SLOTS // 2, functools.partial(build, both=True), 0)
-    lax.fori_loop(SLOTS // 2, SOURCES // 2, functools.partial(build, both=False), 0)
+    twice(build)
     squares, closings, heats, shifted, own, sums = (s0, s1), (c0, c1), (h0, h1), (r0, r1), (i0, i1), (a0, a1)
 
     def stage(t, slot):
-        pair_products(t, rows, codes, left, right, weights, 0, 32, 32, 0, squares[slot])
-        pair_products(t, rows, codes, left, right, weights, 64, 48, 32, 32, closings[slot])
+        yield from pair_products(t, rows, codes, left, right, weights, 0, 32, 32, 0, squares[slot])
+        yield from pair_products(t, rows, codes, left, right, weights, 64, 48, 32, 32, closings[slot])
         for group in GROUPS:
             columns = [hright[source_row(rows, t, k)] for k in group]
             sources = columns[0] if len(columns) == 1 else jnp.concatenate(columns, 1)
             heats[slot][:, LANES * group[0] : LANES * (group[-1] + 1)] = dot(hleft[t], sources, ((0,), (0,)))
+            yield
         for f in range(4):
             row = source_row(rows, t, 5 + f)
             shifted[slot][f] = per_source[row] + shift[codes[t * 4 + f]] * per_source[row, 2:3, :]
@@ -273,6 +295,7 @@
                 totals = [term if total is None else total + term for total, term in zip(totals, terms)]
             for at in range(5):
                 sums[slot][eight, LANES * at : LANES * (at + 1)] = totals[at]
+            yield
 
     def close(t, slot):
         got = [jnp.sum(sums[slot][:, LANES * at : LANES * (at + 1)].T, 0, keepdims=True) for at in range(5)]
@@ -357,6 +380,39 @@
     return picked.reshape((8 * haloed.shape[2],) + haloed.shape[3:])
 
 
+def owner(x, core, z, y):
+    return (2 * (x % 4) + core) * N_GY + 4 * (z % 4) + y % 4
+
+
+CHIPS = [(x, c, z, y) for x in range(4) for c in range(2) for z in range(4) for y in range(4)]
+STAGES = (
+    [(0, 0, k, 0) for k in (1, 2, 3)],
+    [(0, 0, 0, k) for k in (1, 2, 3)],
+    [(k, 0, 0, 0) for k in (1, 2, 3)],
+    [(0, 1, 0, 0)],
+)
+
+
+def gather_all(shard):
+    for stage in STAGES:
+        pieces = [shard]
+        for dx, dc, dz, dy in stage:
+            pairs = [(owner(x, c, z, y), owner(x + dx, c ^ dc, z + dz, y + dy)) for x, c, z, y in CHIPS]
+            pieces.append(lax.ppermute(shard, ("gx", "gy"), pairs))
+        shard = jnp.concatenate(pieces, 0)
+    return shard
+
+
+def place_of(gx, gy):
+    number = jnp.arange(N_GX * N_GY * MIG)
+    ox, oy = number // (MIG * N_GY), number // MIG % N_GY
+    core = gx % 2 ^ ox % 2
+    x = (gx // 2 - ox // 2) % 4
+    z = (gy // 4 - oy // 4) % 4
+    y = (gy - oy) % 4
+    return (((core * 4 + x) * 4 + y) * 4 + z) * MIG + number % MIG
+
+
 def local(
     cell_local_coords,
     particle_speeds,
@@ -368,8 +424,7 @@
     target_entry_inputs,
     adjacent_cell_label,
 ):
-    along = lax.axis_size("gy")
-    myself = lax.axis_index("gx") * along + lax.axis_index("gy")
+    gx, gy = lax.axis_index("gx"), lax.axis_index("gy")
     state_tables = jnp.concatenate(
         [
             cell_local_coords,
@@ -384,24 +439,27 @@
     lanes = state_tables.shape[2]
     chosen = departing_local_groups[0]
     leaving = jnp.take(state_tables, chosen, axis=0)
-    dest_flat = migrant_target_holder.reshape(-1)
-    total = dest_flat.shape[0]
-    listing = jnp.arange(total)
-    match = dest_flat == myself
-    ranking = jnp.cumsum(match.astype(jnp.int32)) - 1
-    slot_ids = jnp.arange(IN_CAP)
-    taken = match[None, :] & (ranking[None, :] == slot_ids[:, None])
-    wanted = jnp.sum(jnp.where(taken, listing[None, :], 0), 1)
-    present = jnp.any(taken, 1)
-    incoming = lax.all_gather(leaving, ("gx", "gy"), axis=0, tiled=True)
-    picked = jnp.take(incoming, wanted, axis=0)
-    arrived = jnp.where(present[:, None, None], picked, 0.0)
     numbers = jnp.arange(state_tables.shape[0])
     departed = jnp.any(numbers[:, None] == chosen[None, :], 1)
-    blocks = jnp.concatenate([arrived, jnp.where(departed[:, None, None], 0.0, state_tables)], 0)
-    exported = blocks[:BND].reshape((1, 1, BND, width, lanes))
-    haloed = padded(exported, (("gx", 0), ("gy", 1)), 1)
-    state = jnp.concatenate([blocks, eight_around(haloed)], 0)
+    staying = jnp.where(departed[:, None, None], 0.0, state_tables)
+    edge = BND - IN_CAP
+    haloed = padded(staying[:edge].reshape((1, 1, edge * width, lanes)), (("gx", 0), ("gy", 1)), 1)
+    around = haloed.reshape((9, edge, width, lanes))
+    near_x = gx + jnp.array([-1, -1, -1, 0, 0, 0, 1, 1, 1])
+    near_y = gy + jnp.array([-1, 0, 1, -1, 0, 1, -1, 0, 1])
+    inside = (near_x >= 0) & (near_x < N_GX) & (near_y >= 0) & (near_y < N_GY)
+    match = migrant_target_holder.reshape(-1)[None, :] == (near_x * N_GY + near_y)[:, None]
+    match = match & inside[:, None]
+    ranking = jnp.cumsum(match.astype(jnp.int32), axis=1) - 1
+    taken = match[:, None, :] & (ranking[:, None, :] == jnp.arange(IN_CAP)[None, :, None])
+    places = place_of(gx, gy)
+    wanted = jnp.sum(jnp.where(taken, places[None, None, :], 0), 2)
+    present = jnp.any(taken, 2)
+    incoming = gather_all(leaving.reshape(MIG * width, lanes)).reshape(-1, width, lanes)
+    arrived = jnp.where(present[:, :, None, None], jnp.take(incoming, wanted, axis=0), 0.0)
+    first = jnp.concatenate([arrived, around], 1)
+    ghosts = jnp.concatenate([first[:4], first[5:]], 0).reshape((-1, width, lanes))
+    state = jnp.concatenate([arrived[4], staying, ghosts], 0)
     rows = target_entry_inputs.reshape(-1)
     codes = (adjacent_cell_label + (adjacent_cell_label >= 13).astype(jnp.int32)).reshape(-1)
     left, right, weights, shift = pair_rows()

time: 312 us -> 220 us (0.71)
  the two profiles are of different devices: /device:TPU:0 before, /device:TPU:25 now
where the time goes in v2:
time: 220 us; the launch traced here: 219 us
  Pallas kernels  142 us (65%)
  starting transfers between devices  39.1 us (18%)
  waiting for transfers between devices  19.6 us (9%)
  local copies, waits for them, and re-layouts  12.2 us (6%)
  other arithmetic  5.23 us (2%)
    pallas_call x1, Pallas kernels, force_call(): pl.pallas_call(force_kernel, out_shape=(jax.ShapeDtypeStruct((SLOTS, 3, L...  102 us
    pallas_call x1, Pallas kernels, density_call(): pl.pallas_call(density_kernel, out_shape=jax.ShapeDtypeStruct((SLOTS, LAN...  39.8 us
    ppermute x10, starting transfers between devices, gather_all(): pieces.append(lax.ppermute(shard, ('gx', 'gy'), pairs))  16.4 us
    ppermute x4, starting transfers between devices, padded(): before = lax.ppermute(last, axis, up)  13 us
    ppermute x4, waiting for transfers between devices, padded(): after = lax.ppermute(first, axis, down)  10.9 us
    ppermute x4, starting transfers between devices, padded(): after = lax.ppermute(first, axis, down)  9.73 us
    ppermute x10, waiting for transfers between devices, gather_all(): pieces.append(lax.ppermute(shard, ('gx', 'gy'), pairs))  7.49 us
    unnamed x43, local copies, waits for them, and re-layouts  5.65 us
  transfers between devices with their start and end apart: 18, of which 10 were waited for; matrix products, arithmetic and copies ran while one was open for 2% of the time, Pallas kernels for 0%

profile of v2, /device:TPU:25, one launch (start us, length us, event | category | flops | bytes accessed | tf_op | source)
XLA Modules:
  0.0 219.3 jit_solution(11060584354459896405)
XLA Ops:
  7.0 1.6 collective-permute-start
  8.6 3.3 %collective-permute-start.1 = (f32[18,128]{1,0:T(8,128)S(1)}, f32[18,128]{1,0:T(8,128)S(1)}, u32[]{:S(2)}, u32[]{:S(2)}) collective-permute-start(f32[18,128]{1,0:T(8,128)S(1)} %broadcast_select_fusion.1), channel_id=1, source_target_pairs={{0,8},{1,9},{2,10},{3,11},{4,12},{5,13},{6,14},{7,15},{8,0},{9,1},... | collective-permute-start | bytes 27656 | tf_op jit(solution)/shard_map/ppermute | solution.py:401
  13.8 4.5 %collective-permute-start.10 = (f32[1,1,72,128]{3,2,1,0:T(8,128)S(1)}, f32[1,1,72,128]{3,2,1,0:T(8,128)S(1)}, u32[]{:S(2)}, u32[]{:S(2)}) collective-permute-start(f32[1,1,72,128]{3,2,1,0:T(8,128)S(1)} %reshape.290), channel_id=1, source_target_pairs={{0,16},{16,32},{32,48},{48,64},{64,80},{80,96},{96,112},{1,17},{17... | collective-permute-start | bytes 110600 | tf_op jit(solution)/shard_map/ppermute | solution.py:371
  18.3 1.9 collective-permute-start.11
  22.3 2.2 %collective-permute-start.4 = (f32[72,128]{1,0:T(8,128)S(1)}, f32[72,128]{1,0:T(8,128)S(1)}, u32[]{:S(2)}, u32[]{:S(2)}) collective-permute-start(f32[72,128]{1,0:T(8,128)S(1)} %pad_maximum_fusion.5), channel_id=1, source_target_pairs={{0,2},{1,3},{2,0},{3,1},{4,6},{5,7},{6,4},{7,5},{8,10},{9,11},{10,... | collective-permute-start | bytes 110600 | tf_op jit(solution)/shard_map/ppermute | solution.py:401
  25.3 1.5 collective-permute-done.4
  26.7 1.9 collective-permute-done.5
  28.9 1.3 collective-permute-start.6
  30.2 1.4 collective-permute-start.7
  31.6 2.0 collective-permute-start.8
  34.2 1.6 collective-permute-done.7
  37.4 3.7 %collective-permute-start.9 = (f32[1152,128]{1,0:T(8,128)S(1)}, f32[1152,128]{1,0:T(8,128)S(1)}, u32[]{:S(2)}, u32[]{:S(2)}) collective-permute-start(f32[1152,128]{1,0:T(8,128)S(1)} %concatenate.48), channel_id=1, source_target_pairs={{0,16},{1,17},{2,18},{3,19},{4,20},{5,21},{6,22},{7,23},{8,24},{9,... | collective-permute-start | bytes 1769480 | tf_op jit(solution)/shard_map/ppermute | solution.py:401
  42.0 2.8 %collective-permute-start.12 = (f32[3,1,72,128]{3,2,1,0:T(8,128)S(1)}, f32[3,1,72,128]{3,2,1,0:T(8,128)S(1)}, u32[]{:S(2)}, u32[]{:S(2)}) collective-permute-start(f32[3,1,72,128]{3,2,1,0:T(8,128)S(1)} %constant_dynamic-update-slice_fusion), channel_id=1, source_target_pairs={{0,1},{1,2},{2,3},{3,4},{4,5},{5,6},{6,7},{7,8},{8,9},{9,10},{10,1... | collective-permute-start | bytes 331784 | tf_op jit(solution)/shard_map/ppermute | solution.py:371
  44.8 2.5 %collective-permute-start.13 = (f32[3,1,72,128]{3,2,1,0:T(8,128)S(1)}, f32[3,1,72,128]{3,2,1,0:T(8,128)S(1)}, u32[]{:S(2)}, u32[]{:S(2)}) collective-permute-start(f32[3,1,72,128]{3,2,1,0:T(8,128)S(1)} %constant_dynamic-update-slice_fusion), channel_id=1, source_target_pairs={{1,0},{2,1},{3,2},{4,3},{5,4},{6,5},{7,6},{8,7},{9,8},{10,9},{11,1... | collective-permute-start | bytes 331784 | tf_op jit(solution)/shard_map/ppermute | solution.py:372
  47.3 1.3 collective-permute-done.12
  48.6 4.6 %collective-permute-done.13 = f32[3,1,72,128]{3,2,1,0:T(8,128)S(1)} collective-permute-done((f32[3,1,72,128]{3,2,1,0:T(8,128)S(1)}, f32[3,1,72,128]{3,2,1,0:T(8,128)S(1)}, u32[]{:S(2)}, u32[]{:S(2)}) %collective-permute-start.13) | collective-permute-done | bytes 110624 | tf_op jit(solution)/shard_map/ppermute | solution.py:372
  57.7 39.8 %density_pass.1 = f32[104,128]{1,0:T(8,128)} custom-call(s32[832]{0:T(1024)S(1)} %reshape.286.rows, s32[416]{0:T(512)S(1)} %reshape.287.codes, f32[232,9,128]{2,1,0:T(8,128)S(1)} %pad_maximum_fusion.state, bf16[64,32]{1,0:T(8,128)(2,1)S(1)} %copy-done.4, bf16[64,32]{1,0:T(8,128)(2,1)S(1)} %copy-done.5, bf16[32,64,128]{2,1,0:T(8,128)(2,1)S(1)} %copy-done), custom_call_target="tpu_custom_call" | custom-call | tf_op jit(solution)/shard_map/density_pass/pallas_call | solution.py:322
  98.2 3.9 %collective-permute-start.14 = (f32[1,1,16,128]{3,2,1,0:T(8,128)S(1)}, f32[1,1,16,128]{3,2,1,0:T(8,128)S(1)}, u32[]{:S(2)}, u32[]{:S(2)}) collective-permute-start(f32[1,1,16,128]{3,2,1,0:T(8,128)S(1)} %slice_bitcast_fusion.1), channel_id=1, source_target_pairs={{0,16},{16,32},{32,48},{48,64},{64,80},{80,96},{96,112},{1,17},{17... | collective-permute-start | bytes 24584 | tf_op jit(solution)/shard_map/ppermute | solution.py:371
  102.1 1.9 collective-permute-start.15
  104.0 3.0 %collective-permute-done.15 = f32[1,1,16,128]{3,2,1,0:T(8,128)S(1)} collective-permute-done((f32[1,1,16,128]{3,2,1,0:T(8,128)S(1)}, f32[1,1,16,128]{3,2,1,0:T(8,128)S(1)}, u32[]{:S(2)}, u32[]{:S(2)}) %collective-permute-start.15) | collective-permute-done | bytes 8224 | tf_op jit(solution)/shard_map/ppermute | solution.py:372
  107.0 1.9 collective-permute-start.16
  108.9 3.4 %collective-permute-start.17 = (f32[3,1,16,128]{3,2,1,0:T(8,128)S(1)}, f32[3,1,16,128]{3,2,1,0:T(8,128)S(1)}, u32[]{:S(2)}, u32[]{:S(2)}) collective-permute-start(f32[3,1,16,128]{3,2,1,0:T(8,128)S(1)} %pad_maximum_fusion.6), channel_id=1, source_target_pairs={{1,0},{2,1},{3,2},{4,3},{5,4},{6,5},{7,6},{8,7},{9,8},{10,9},{11,1... | collective-permute-start | bytes 73736 | tf_op jit(solution)/shard_map/ppermute | solution.py:372
  112.3 3.3 %collective-permute-done.17 = f32[3,1,16,128]{3,2,1,0:T(8,128)S(1)} collective-permute-done((f32[3,1,16,128]{3,2,1,0:T(8,128)S(1)}, f32[3,1,16,128]{3,2,1,0:T(8,128)S(1)}, u32[]{:S(2)}, u32[]{:S(2)}) %collective-permute-start.17) | collective-permute-done | bytes 24608 | tf_op jit(solution)/shard_map/ppermute | solution.py:372
  116.5 102.1 %force_pass.1 = (f32[104,3,128]{2,1,0:T(4,128)S(1)}, f32[104,128]{1,0:T(8,128)}) custom-call(s32[832]{0:T(1024)S(1)} %reshape.286.rows, s32[416]{0:T(512)S(1)} %reshape.287.codes, f32[232,9,128]{2,1,0:T(8,128)S(1)} %pad_maximum_fusion.state, f32[232,128]{1,0:T(8,128)S(1)} %pad_maximum_fusion.2.rho_table, bf16[144,32]{1,0:T(8,128)(2,1)S(1)} %copy-done.2, ...), custom_call_target="tpu_custom_call" | custom-call | tf_op jit(solution)/shard_map/force_pass/pallas_call | solution.py:340
  (115 shorter events, 20.8 us)
Async XLA Ops:
  7.0 15.2 %collective-permute-start = (f32[18,128]{1,0:T(8,128)S(1)}, f32[18,128]{1,0:T(8,128)S(1)}, u32[]{:S(2)}, u32[]{:S(2)}) collective-permute-start(f32[18,128]{1,0:T(8,128)S(1)} %broadcast_select_fusion.1), channel_id=1, source_target_pairs={{0,4},{1,5},{2,6},{3,7},{4,8},{5,9},{6,10},{7,11},{8,12},{9,13},{1... | collective-permute-start | bytes 27656 | tf_op jit(solution)/shard_map/ppermute | solution.py:401
  8.6 13.6 %collective-permute-start.1 = (f32[18,128]{1,0:T(8,128)S(1)}, f32[18,128]{1,0:T(8,128)S(1)}, u32[]{:S(2)}, u32[]{:S(2)}) collective-permute-start(f32[18,128]{1,0:T(8,128)S(1)} %broadcast_select_fusion.1), channel_id=1, source_target_pairs={{0,8},{1,9},{2,10},{3,11},{4,12},{5,13},{6,14},{7,15},{8,0},{9,1},... | collective-permute-start | bytes 27656 | tf_op jit(solution)/shard_map/ppermute | solution.py:401
  11.9 10.3 %collective-permute-start.2 = (f32[18,128]{1,0:T(8,128)S(1)}, f32[18,128]{1,0:T(8,128)S(1)}, u32[]{:S(2)}, u32[]{:S(2)}) collective-permute-start(f32[18,128]{1,0:T(8,128)S(1)} %broadcast_select_fusion.1), channel_id=1, source_target_pairs={{0,12},{1,13},{2,14},{3,15},{4,0},{5,1},{6,2},{7,3},{8,4},{9,5},{1... | collective-permute-start | bytes 27656 | tf_op jit(solution)/shard_map/ppermute | solution.py:401
  12.7 28.8 %copy-start.11 = (s32[104,8]{0,1:T(8,128)S(1)}, s32[104,8]{0,1:T(8,128)}, u32[]{:S(2)}) copy-start(s32[104,8]{0,1:T(8,128)} %param.24) | copy-start | bytes 9988
  13.8 28.2 %collective-permute-start.10 = (f32[1,1,72,128]{3,2,1,0:T(8,128)S(1)}, f32[1,1,72,128]{3,2,1,0:T(8,128)S(1)}, u32[]{:S(2)}, u32[]{:S(2)}) collective-permute-start(f32[1,1,72,128]{3,2,1,0:T(8,128)S(1)} %reshape.290), channel_id=1, source_target_pairs={{0,16},{16,32},{32,48},{48,64},{64,80},{80,96},{96,112},{1,17},{17... | collective-permute-start | bytes 110600 | tf_op jit(solution)/shard_map/ppermute | solution.py:371
  18.3 23.7 %collective-permute-start.11 = (f32[1,1,72,128]{3,2,1,0:T(8,128)S(1)}, f32[1,1,72,128]{3,2,1,0:T(8,128)S(1)}, u32[]{:S(2)}, u32[]{:S(2)}) collective-permute-start(f32[1,1,72,128]{3,2,1,0:T(8,128)S(1)} %reshape.290), channel_id=1, source_target_pairs={{16,0},{32,16},{48,32},{64,48},{80,64},{96,80},{112,96},{17,1},{33... | collective-permute-start | bytes 110600 | tf_op jit(solution)/shard_map/ppermute | solution.py:372
  22.2 3.0 %collective-permute-start.3 = (f32[72,128]{1,0:T(8,128)S(1)}, f32[72,128]{1,0:T(8,128)S(1)}, u32[]{:S(2)}, u32[]{:S(2)}) collective-permute-start(f32[72,128]{1,0:T(8,128)S(1)} %pad_maximum_fusion.5), channel_id=1, source_target_pairs={{0,1},{1,2},{2,3},{3,0},{4,5},{5,6},{6,7},{7,4},{8,9},{9,10},{10,1... | collective-permute-start | bytes 110600 | tf_op jit(solution)/shard_map/ppermute | solution.py:401
  22.3 4.4 %collective-permute-start.4 = (f32[72,128]{1,0:T(8,128)S(1)}, f32[72,128]{1,0:T(8,128)S(1)}, u32[]{:S(2)}, u32[]{:S(2)}) collective-permute-start(f32[72,128]{1,0:T(8,128)S(1)} %pad_maximum_fusion.5), channel_id=1, source_target_pairs={{0,2},{1,3},{2,0},{3,1},{4,6},{5,7},{6,4},{7,5},{8,10},{9,11},{10,... | collective-permute-start | bytes 110600 | tf_op jit(solution)/shard_map/ppermute | solution.py:401
  24.6 4.0 %collective-permute-start.5 = (f32[72,128]{1,0:T(8,128)S(1)}, f32[72,128]{1,0:T(8,128)S(1)}, u32[]{:S(2)}, u32[]{:S(2)}) collective-permute-start(f32[72,128]{1,0:T(8,128)S(1)} %pad_maximum_fusion.5), channel_id=1, source_target_pairs={{0,3},{1,0},{2,1},{3,2},{4,7},{5,4},{6,5},{7,6},{8,11},{9,8},{10,9... | collective-permute-start | bytes 110600 | tf_op jit(solution)/shard_map/ppermute | solution.py:401
  28.9 5.3 %collective-permute-start.6 = (f32[288,128]{1,0:T(8,128)S(1)}, f32[288,128]{1,0:T(8,128)S(1)}, u32[]{:S(2)}, u32[]{:S(2)}) collective-permute-start(f32[288,128]{1,0:T(8,128)S(1)} %concatenate.47), channel_id=1, source_target_pairs={{0,32},{1,33},{2,34},{3,35},{4,36},{5,37},{6,38},{7,39},{8,40},{9,... | collective-permute-start | bytes 442376 | tf_op jit(solution)/shard_map/ppermute | solution.py:401
  30.2 5.6 %collective-permute-start.7 = (f32[288,128]{1,0:T(8,128)S(1)}, f32[288,128]{1,0:T(8,128)S(1)}, u32[]{:S(2)}, u32[]{:S(2)}) collective-permute-start(f32[288,128]{1,0:T(8,128)S(1)} %concatenate.47), channel_id=1, source_target_pairs={{0,64},{1,65},{2,66},{3,67},{4,68},{5,69},{6,70},{7,71},{8,72},{9,... | collective-permute-start | bytes 442376 | tf_op jit(solution)/shard_map/ppermute | solution.py:401
  31.6 5.5 %collective-permute-start.8 = (f32[288,128]{1,0:T(8,128)S(1)}, f32[288,128]{1,0:T(8,128)S(1)}, u32[]{:S(2)}, u32[]{:S(2)}) collective-permute-start(f32[288,128]{1,0:T(8,128)S(1)} %concatenate.47), channel_id=1, source_target_pairs={{0,96},{1,97},{2,98},{3,99},{4,100},{5,101},{6,102},{7,103},{8,104... | collective-permute-start | bytes 442376 | tf_op jit(solution)/shard_map/ppermute | solution.py:401
  37.4 16.7 %collective-permute-start.9 = (f32[1152,128]{1,0:T(8,128)S(1)}, f32[1152,128]{1,0:T(8,128)S(1)}, u32[]{:S(2)}, u32[]{:S(2)}) collective-permute-start(f32[1152,128]{1,0:T(8,128)S(1)} %concatenate.48), channel_id=1, source_target_pairs={{0,16},{1,17},{2,18},{3,19},{4,20},{5,21},{6,22},{7,23},{8,24},{9,... | collective-permute-start | bytes 1769480 | tf_op jit(solution)/shard_map/ppermute | solution.py:401
  42.0 6.6 %collective-permute-start.12 = (f32[3,1,72,128]{3,2,1,0:T(8,128)S(1)}, f32[3,1,72,128]{3,2,1,0:T(8,128)S(1)}, u32[]{:S(2)}, u32[]{:S(2)}) collective-permute-start(f32[3,1,72,128]{3,2,1,0:T(8,128)S(1)} %constant_dynamic-update-slice_fusion), channel_id=1, source_target_pairs={{0,1},{1,2},{2,3},{3,4},{4,5},{5,6},{6,7},{7,8},{8,9},{9,10},{10,1... | collective-permute-start | bytes 331784 | tf_op jit(solution)/shard_map/ppermute | solution.py:371
  44.8 8.4 %collective-permute-start.13 = (f32[3,1,72,128]{3,2,1,0:T(8,128)S(1)}, f32[3,1,72,128]{3,2,1,0:T(8,128)S(1)}, u32[]{:S(2)}, u32[]{:S(2)}) collective-permute-start(f32[3,1,72,128]{3,2,1,0:T(8,128)S(1)} %constant_dynamic-update-slice_fusion), channel_id=1, source_target_pairs={{1,0},{2,1},{3,2},{4,3},{5,4},{6,5},{7,6},{8,7},{9,8},{10,9},{11,1... | collective-permute-start | bytes 331784 | tf_op jit(solution)/shard_map/ppermute | solution.py:372
  57.7 58.8 %copy-start.1 = (f32[32,8,128]{2,1,0:T(8,128)S(1)}, f32[32,8,128]{2,1,0:T(8,128)}, u32[]{:S(2)}) copy-start(f32[32,8,128]{2,1,0:T(8,128)} %constant.195.clone.shift) | copy-start | bytes 393220
  57.7 58.8 %copy-start.2 = (bf16[144,32]{1,0:T(8,128)(2,1)S(1)}, bf16[144,32]{1,0:T(8,128)(2,1)}, u32[]{:S(2)}) copy-start(bf16[144,32]{1,0:T(8,128)(2,1)} %constant.190.clone.place_left) | copy-start | bytes 27652
  57.7 58.8 %copy-start.3 = (bf16[144,32]{1,0:T(8,128)(2,1)S(1)}, bf16[144,32]{1,0:T(8,128)(2,1)}, u32[]{:S(2)}) copy-start(bf16[144,32]{1,0:T(8,128)(2,1)} %constant.191.clone.place_right) | copy-start | bytes 27652
  57.7 58.8 %copy-start.6 = (bf16[32,32]{1,0:T(8,128)(2,1)S(1)}, bf16[32,32]{1,0:T(8,128)(2,1)}, u32[]{:S(2)}) copy-start(bf16[32,32]{1,0:T(8,128)(2,1)} %constant.193.clone.heat_left) | copy-start | bytes 6148
  57.7 58.8 %copy-start.7 = (bf16[32,32]{1,0:T(8,128)(2,1)S(1)}, bf16[32,32]{1,0:T(8,128)(2,1)}, u32[]{:S(2)}) copy-start(bf16[32,32]{1,0:T(8,128)(2,1)} %constant.194.clone.heat_right) | copy-start | bytes 6148
  98.2 5.8 %collective-permute-start.14 = (f32[1,1,16,128]{3,2,1,0:T(8,128)S(1)}, f32[1,1,16,128]{3,2,1,0:T(8,128)S(1)}, u32[]{:S(2)}, u32[]{:S(2)}) collective-permute-start(f32[1,1,16,128]{3,2,1,0:T(8,128)S(1)} %slice_bitcast_fusion.1), channel_id=1, source_target_pairs={{0,16},{16,32},{32,48},{48,64},{64,80},{80,96},{96,112},{1,17},{17... | collective-permute-start | bytes 24584 | tf_op jit(solution)/shard_map/ppermute | solution.py:371
  102.1 5.0 %collective-permute-start.15 = (f32[1,1,16,128]{3,2,1,0:T(8,128)S(1)}, f32[1,1,16,128]{3,2,1,0:T(8,128)S(1)}, u32[]{:S(2)}, u32[]{:S(2)}) collective-permute-start(f32[1,1,16,128]{3,2,1,0:T(8,128)S(1)} %slice_bitcast_fusion.1), channel_id=1, source_target_pairs={{16,0},{32,16},{48,32},{64,48},{80,64},{96,80},{112,96},{17,1},{33... | collective-permute-start | bytes 24584 | tf_op jit(solution)/shard_map/ppermute | solution.py:372
  107.0 5.3 %collective-permute-start.16 = (f32[3,1,16,128]{3,2,1,0:T(8,128)S(1)}, f32[3,1,16,128]{3,2,1,0:T(8,128)S(1)}, u32[]{:S(2)}, u32[]{:S(2)}) collective-permute-start(f32[3,1,16,128]{3,2,1,0:T(8,128)S(1)} %pad_maximum_fusion.6), channel_id=1, source_target_pairs={{0,1},{1,2},{2,3},{3,4},{4,5},{5,6},{6,7},{7,8},{8,9},{9,10},{10,1... | collective-permute-start | bytes 73736 | tf_op jit(solution)/shard_map/ppermute | solution.py:371
  108.9 6.7 %collective-permute-start.17 = (f32[3,1,16,128]{3,2,1,0:T(8,128)S(1)}, f32[3,1,16,128]{3,2,1,0:T(8,128)S(1)}, u32[]{:S(2)}, u32[]{:S(2)}) collective-permute-start(f32[3,1,16,128]{3,2,1,0:T(8,128)S(1)} %pad_maximum_fusion.6), channel_id=1, source_target_pairs={{1,0},{2,1},{3,2},{4,3},{5,4},{6,5},{7,6},{8,7},{9,8},{10,9},{11,1... | collective-permute-start | bytes 73736 | tf_op jit(solution)/shard_map/ppermute | solution.py:372
  (11 other events, 98.6 us)

commit v3 on v2

v3 whole, which is shorter than its diff:
```python
import functools
import math

import jax
import jax.numpy as jnp
import numpy as np
from jax import lax
from jax.experimental import pallas as pl
from jax.experimental.pallas import tpu as pltpu
from jax.sharding import PartitionSpec as P

IN_CAP = 8
BND = 16
MIG = 2
N_GX = 8
N_GY = 16
SLOTS = 104
SOURCES = 232
LANES = 128
LINKS = 9

SMOOTH = 0.5
KERNEL = 21.0 / (16.0 * math.pi * SMOOTH**3)
SOUND = math.sqrt(7.0)
VISC = 0.1
SOFT = 0.01 * SMOOTH**2
GRAVITY = 1.0
KAPPA = -2.0 * VISC * SOUND * SMOOTH
SLOPE = 5.0 * KERNEL / SMOOTH**2
TINY = 1e-30

F32 = jnp.float32
BF16 = jnp.bfloat16

PARTS = ((0, 0), (0, 1), (0, 2), (1, 0), (1, 1), (2, 0))
ONE = 24
STILL = 64
SHIFTED = 112


def part(p, channel):
    return 8 * p + channel


def source_at(p_target, p_source, channel):
    return 48 + channel if p_source == 2 else 16 * p_target + 8 * p_source + channel


def pair_rows():
    square = np.zeros((SHIFTED, 32), np.float32)
    closing = np.zeros((SHIFTED, 32), np.float32)
    steps = np.array([(c // 9 - 1, c // 3 % 3 - 1, c % 3 - 1) for c in range(27)], np.float32)
    weights = np.zeros((32, SHIFTED - STILL), np.float32)
    for k in range(3):
        for a, b in PARTS:
            square[source_at(a, b, k), part(a, k)] = -2
            closing[source_at(a, b, k), part(a, 3 + k)] = -1
            closing[source_at(a, b, 3 + k), part(a, k)] = -1
        for p in range(3):
            row = 64 + 8 * p
            square[row + k, ONE] = 2
            closing[row + 3 + k, ONE] = 1
            weights[:27, 8 * p + k] = weights[:27, 8 * p + 3 + k] = steps[:, k]
            row = (88, 96, 99)[p] + k
            square[row, part(p, k)] = -2
            closing[row, part(p, 3 + k)] = -1
            weights[:27, row - 64] = steps[:, k]
    for p in range(3):
        square[source_at(0, p, 6), ONE] = 1
        square[56 + p, part(p, 6)] = 1
        closing[source_at(0, p, 7), ONE] = 1
        closing[56 + p, part(p, 7)] = 1
    square[91, ONE] = 1
    weights[:27, 91 - 64] = (steps * steps).sum(1)
    shift = np.zeros((32, 8, LANES), np.float32)
    shift[:27, :3] = steps[:, :, None]
    weights = np.broadcast_to(weights[:, :, None], weights.shape + (LANES,))
    return square, closing, weights, shift


def heat_rows():
    heat, rho = (np.zeros((STILL, 32), np.float32) for _ in range(2))
    for a, b in PARTS:
        heat[source_at(a, b, 0), part(a, 0)] = 1
        heat[source_at(a, b, 1), part(a, 1)] = 1
    for p in range(3):
        heat[source_at(0, p, 2), ONE] = -1
        heat[source_at(0, p, 3), part(0, 2)] = -1
        rho[source_at(0, p, 4), ONE] = 1
        rho[56 + p, part(p, 3)] = 1
    return np.concatenate([heat, rho])


def split(block):
    high = block.astype(BF16).astype(F32)
    rest = block - high
    middle = rest.astype(BF16).astype(F32)
    return high, middle, rest - middle


def parts_of(block):
    return jnp.concatenate([*split(block), jnp.ones_like(block)], 0).astype(BF16)


def stacked(parts, row, lanes_weights=None, ones=False):
    first, second = parts[row, 0:16, :], parts[row, 16:32, :]
    rows = [first, first, first, second]
    if ones:
        more = [first, second, jnp.ones_like(first)]
        if lanes_weights is not None:
            more = [lanes_weights[16 * q : 16 * q + 16, :] * tile for q, tile in enumerate(more)]
        rows += more
    return jnp.concatenate(rows, 0)


def channels(state, b):
    x = state[b, 0:3, :]
    v = state[b, 3:6, :] * KAPPA
    n = jnp.sum(x * x, 0, keepdims=True)
    vx = jnp.sum(x * v, 0, keepdims=True)
    return jnp.concatenate([x, v, n, vx], 0)


def dot(a, b, contract):
    return lax.dot_general(a, b, (contract, ((), ())), preferred_element_type=F32)


def build_targets(place, parts, out, rows, first, count):
    for u in range(count // 2):
        at = first + 2 * u
        both = jnp.concatenate([parts[at], parts[at + 1]], 1)
        got = dot(place[...], both, ((1,), (0,))).astype(BF16)
        for q in range(2):
            for g in range(got.shape[0] // rows):
                out[at + q, :, LANES * g : LANES * (g + 1)] = got[rows * g : rows * (g + 1), LANES * q : LANES * (q + 1)]


def build_tables(own, other, targets):
    def first(u, carry):
        targets(8 * jnp.maximum(u - 1, 0), 8)
        for q in range(8):
            own(8 * jnp.minimum(u, SLOTS // 8 - 1) + q)
        return carry

    def second(u, carry):
        for q in range(8):
            other(8 * u + q)
        return carry

    lax.fori_loop(0, SLOTS // 8 + 1, first, 0)
    lax.fori_loop(SLOTS // 8, SOURCES // 8, second, 0)


def source_row(rows, t, k):
    return t if k == 0 else rows[t * 8 + k - 1]


def run(steps):
    for _ in steps:
        pass


def alternate(*steps):
    live = list(steps)
    while live:
        for g in list(live):
            if next(g, live) is live:
                live.remove(g)


def paired_loop(stage, work, close, batch):
    last = SLOTS // batch - 1
    span = lambda n: [n * batch + q for q in range(batch)]

    def chain(piece, n, slot):
        for q, t in enumerate(span(n)):
            yield from piece(t, slot * batch + q)

    run(chain(stage, 0, 0))

    def step(n, carry):
        for slot in range(2):

            @pl.when(lax.rem(n, 2) == slot)
            def _():
                alternate(
                    chain(close, jnp.maximum(n - 1, 0), 1 - slot),
                    chain(work, n, slot),
                    chain(stage, jnp.minimum(n + 1, last), 1 - slot),
                )

        return carry

    lax.fori_loop(0, last + 1, step, 0)
    run(chain(close, last, last % 2))


GROUPS = ((0, 1), (2, 3), (4,), (5, 6), (7, 8))


def density_kernel(rows, codes, state, place, weights, out, parts, left, *buffers):
    squares, sums = buffers[: 2 * DENSITY_BATCH], buffers[2 * DENSITY_BATCH :]

    def each(b):
        parts[b] = parts_of(channels(state, b))

    build_tables(each, each, lambda t, count: build_targets(place, parts, left, SHIFTED, t, count))

    def stage(t, slot):
        near, far = left[t, 0:STILL, :], left[t]
        for group in GROUPS:
            face = group[0] >= 5
            columns = [
                stacked(parts, source_row(rows, t, k), weights[codes[t * 4 + k - 5]] if face else None, face)
                for k in group
            ]
            sources = columns[0] if len(columns) == 1 else jnp.concatenate(columns, 1)
            made = dot(far if face else near, sources, ((0,), (0,)))
            squares[slot][:, LANES * group[0] : LANES * (group[-1] + 1)] = made
            yield

    def work(t, slot):
        square = squares[slot]
        masses = [state.at[source_row(rows, t, k)] for k in range(LINKS)]
        for o in range(16):
            total = None
            for k in range(LINKS):
                s = jnp.maximum(square[8 * o : 8 * o + 8, LANES * k : LANES * (k + 1)], TINY)
                w = jnp.maximum(1.0 - s * lax.rsqrt(s), 0.0)
                w2 = w * w
                term = (w2 * w2) * (1.25 - w) * masses[k][7:8, :]
                total = term if total is None else total + term
            sums[slot][8 * o : 8 * o + 8, :] = total
            if o % 3 == 0:
                yield

    def close(t, slot):
        rho = jnp.sum(sums[slot][...].T, 0, keepdims=True) * (4.0 * KERNEL)
        out[pl.ds(t, 1), :] = jnp.where(state[t, 7:8, :] > 0.0, rho, 0.0)
        yield

    paired_loop(stage, work, close, DENSITY_BATCH)


def force_kernel(rows, codes, state, rho_table, place, heat_place, weights, shift, out_a, out_h,
                 parts, heat_parts, own_parts, mass_parts, pressures, own_pressure, left, heat_left, *buffers):
    pairs, heats, split_terms, heat_sums = (buffers[2 * FORCE_BATCH * q : 2 * FORCE_BATCH * (q + 1)] for q in range(4))

    def each(b):
        parts[b] = parts_of(channels(state, b))
        x, heat, mass, wall = state[b, 0:3, :], state[b, 6:7, :], state[b, 7:8, :], state[b, 8:9, :]
        rho = jnp.where(mass > 0.0, rho_table[pl.ds(b, 1), :], 1.0)
        inverse = 1.0 / rho
        r2 = rho * rho
        pressure = (r2 * r2 * r2 * rho - 1.0) * (inverse * inverse)
        ratio = mass * inverse
        a = ratio * (2.0 + 1.2 * wall)
        b2 = ratio * (1.2 + 3.6 * wall)
        zero = jnp.zeros_like(rho)
        heat_parts[b] = parts_of(jnp.concatenate([a, b2, a * heat, b2 * heat, rho, zero, zero, zero], 0))
        pressures[b] = jnp.broadcast_to(pressure, (LANES, LANES)).T
        high, middle, low = split(jnp.concatenate([mass, mass * x, zero, zero, zero, zero], 0))
        mass_parts[b] = jnp.concatenate([high[0:4], middle[0:4], low], 0).astype(BF16)
        return [heat, heat * wall, wall, rho, zero, zero, zero, zero], pressure

    def own(b):
        lines, pressure = each(b)
        own_parts[b] = parts_of(jnp.concatenate(lines, 0))
        own_pressure[pl.ds(b, 1), :] = pressure

    def targets(t, count):
        build_targets(place, parts, left, SHIFTED, t, count)
        build_targets(heat_place, own_parts, heat_left, STILL, t, count)

    build_tables(own, each, targets)

    def stage(t, slot):
        near, heat_near = left[t, 0:STILL, :], heat_left[t]
        for k in range(LINKS):
            row = source_row(rows, t, k)
            if k < 5:
                targets = near
            else:
                scale = weights[codes[t * 4 + k - 5]]
                targets = jnp.concatenate(
                    [near, left[t, STILL:SHIFTED, :] * jnp.concatenate([scale, scale], 1)], 0
                )
            block = slice(LANES * k, LANES * (k + 1))
            pairs[slot][block, :] = dot(stacked(parts, row, None, k >= 5), targets, ((0,), (0,)))
            heats[slot][block, :] = dot(stacked(heat_parts, row), heat_near, ((0,), (0,)))
            yield

    def work(t, slot):
        pair, heat, terms = pairs[slot], heats[slot], split_terms[slot]
        totals = [None] * 2
        pressure = own_pressure[pl.ds(t, 1), :]
        for k in range(LINKS):
            near = pressures.at[source_row(rows, t, k)]
            for o in range(8):
                found = []
                for q in range(2):
                    eight = slice(LANES * k + 16 * o + 8 * q, LANES * k + 16 * o + 8 * q + 8)
                    s = jnp.maximum(pair[eight, 0:LANES], TINY)
                    w = jnp.maximum(1.0 - s * lax.rsqrt(s), 0.0)
                    w3 = w * w * w
                    z = w3 * pl.reciprocal(s + SOFT, approx=True)
                    closing = jnp.maximum(pair[eight, LANES : 2 * LANES], 0.0)
                    viscous = closing * pl.reciprocal(heat[eight, LANES : 2 * LANES], approx=True)
                    sum_p = pressure + near[16 * o + 8 * q : 16 * o + 8 * q + 8, :]
                    found.append(sum_p * w3 + viscous * z)
                    warm = (s * z) * heat[eight, 0:LANES]
                    totals[q] = warm if totals[q] is None else totals[q] + warm
                term = jnp.concatenate(found, 0)
                high = term.astype(BF16)
                at = 2 * LANES * k + 16 * o
                terms[at : at + 16, :] = high
                terms[at + LANES : at + LANES + 16, :] = (term - high.astype(F32)).astype(BF16)
            yield
        heat_sums[slot][...] = totals[0] + totals[1]

    def close(t, slot):
        total, moved = None, [None] * 3
        for k in range(LINKS):
            mass = mass_parts[source_row(rows, t, k)]
            got = dot(
                jnp.concatenate([mass, mass], 1),
                split_terms[slot][2 * LANES * k : 2 * LANES * (k + 1), :],
                ((1,), (0,)),
            )
            total = got if total is None else total + got
            if k >= 5:
                pull = got[0:1] + got[4:5] + got[8:9]
                code = codes[t * 4 + k - 5]
                for axis in range(3):
                    more = shift[code, axis : axis + 1, :] * pull
                    moved[axis] = more if moved[axis] is None else moved[axis] + more
            yield
        total = total[0:4] + total[4:8] + total[8:12]
        mass, fluid = state[t, 7:8, :], 1.0 - state[t, 8:9, :]
        living = mass > 0.0
        lines = []
        for k in range(3):
            push = SLOPE * (state[t, k : k + 1, :] * total[0:1] - (total[1 + k : 2 + k] + moved[k]))
            if k == 2:
                push = push - GRAVITY
            lines.append(jnp.where(living, push * fluid, 0.0))
        out_a[t] = jnp.concatenate(lines, 0)
        warm = jnp.sum(heat_sums[slot][...], 0, keepdims=True)
        rho = jnp.where(living, rho_table[pl.ds(t, 1), :], 1.0)
        out_h[pl.ds(t, 1), :] = jnp.where(living, -SLOPE * warm / rho, 0.0)

    paired_loop(stage, work, close, FORCE_BATCH)


SMEM = pl.BlockSpec(memory_space=pltpu.SMEM)
VMEM = pl.BlockSpec(memory_space=pltpu.VMEM)


DENSITY_BATCH = 4
FORCE_BATCH = 2


def density_call(rows, codes, state, place, weights):
    wide = (LANES, LINKS * LANES)
    return pl.pallas_call(
        density_kernel,
        out_shape=jax.ShapeDtypeStruct((SLOTS, LANES), F32),
        in_specs=[SMEM] * 2 + [VMEM] * 3,
        out_specs=VMEM,
        scratch_shapes=[
            pltpu.VMEM((SOURCES, 32, LANES), BF16),
            pltpu.VMEM((SLOTS, SHIFTED, LANES), BF16),
        ]
        + [pltpu.VMEM(wide, F32)] * (2 * DENSITY_BATCH)
        + [pltpu.VMEM((LANES, LANES), F32)] * (2 * DENSITY_BATCH),
        compiler_params=pltpu.CompilerParams(vmem_limit_bytes=32 << 20),
        name="density_pass",
    )(rows, codes, state, place, weights)


def force_call(rows, codes, state, rho_table, place, heat_place, weights, shift):
    tall = LINKS * LANES
    return pl.pallas_call(
        force_kernel,
        out_shape=(
            jax.ShapeDtypeStruct((SLOTS, 3, LANES), F32),
            jax.ShapeDtypeStruct((SLOTS, LANES), F32),
        ),
        in_specs=[SMEM] * 2 + [VMEM] * 6,
        out_specs=(VMEM, VMEM),
        scratch_shapes=[
            pltpu.VMEM((SOURCES, 32, LANES), BF16),
            pltpu.VMEM((SOURCES, 32, LANES), BF16),
            pltpu.VMEM((SLOTS, 32, LANES), BF16),
            pltpu.VMEM((SOURCES, 16, LANES), BF16),
            pltpu.VMEM((SOURCES, LANES, LANES), F32),
            pltpu.VMEM((SLOTS, LANES), F32),
            pltpu.VMEM((SLOTS, SHIFTED, 2 * LANES), BF16),
            pltpu.VMEM((SLOTS, STILL, 2 * LANES), BF16),
        ]
        + [pltpu.VMEM((tall, 2 * LANES), F32)] * (2 * FORCE_BATCH)
        + [pltpu.VMEM((tall, 2 * LANES), F32)] * (2 * FORCE_BATCH)
        + [pltpu.VMEM((2 * tall, LANES), BF16)] * (2 * FORCE_BATCH)
        + [pltpu.VMEM((8, LANES), F32)] * (2 * FORCE_BATCH),
        compiler_params=pltpu.CompilerParams(vmem_limit_bytes=48 << 20),
        name="force_pass",
    )(rows, codes, state, rho_table, place, heat_place, weights, shift)


def padded(shard, sides, width):
    for axis, dim in sides:
        size, length = (lax.axis_size(axis), shard.shape[dim])
        up = [(i, (i + 1) % size) for i in range(size - 1)]
        down = [(j, i) for i, j in up]
        last = lax.slice_in_dim(shard, length - width, length, axis=dim)
        first = lax.slice_in_dim(shard, 0, width, axis=dim)
        before = lax.ppermute(last, axis, up)
        after = lax.ppermute(first, axis, down)
        shard = jnp.concatenate([before, shard, after], axis=dim)
    return shard


def eight_around(haloed):
    flat = haloed.reshape((9,) + haloed.shape[2:])
    picked = jnp.concatenate([flat[:4], flat[5:]], 0)
    return picked.reshape((8 * haloed.shape[2],) + haloed.shape[3:])


def owner(x, core, z, y):
    return (2 * (x % 4) + core) * N_GY + 4 * (z % 4) + y % 4


CHIPS = [(x, c, z, y) for x in range(4) for c in range(2) for z in range(4) for y in range(4)]
STAGES = (
    [(0, 0, k, 0) for k in (1, 2, 3)],
    [(0, 0, 0, k) for k in (1, 2, 3)],
    [(k, 0, 0, 0) for k in (1, 2, 3)],
    [(0, 1, 0, 0)],
)


def gather_all(shard):
    for stage in STAGES:
        pieces = [shard]
        for dx, dc, dz, dy in stage:
            pairs = [(owner(x, c, z, y), owner(x + dx, c ^ dc, z + dz, y + dy)) for x, c, z, y in CHIPS]
            pieces.append(lax.ppermute(shard, ("gx", "gy"), pairs))
        shard = jnp.concatenate(pieces, 0)
    return shard


def place_of(gx, gy):
    number = jnp.arange(N_GX * N_GY * MIG)
    ox, oy = number // (MIG * N_GY), number // MIG % N_GY
    core = gx % 2 ^ ox % 2
    x = (gx // 2 - ox // 2) % 4
    z = (gy // 4 - oy // 4) % 4
    y = (gy - oy) % 4
    return (((core * 4 + x) * 4 + y) * 4 + z) * MIG + number % MIG


def local(
    cell_local_coords,
    particle_speeds,
    thermal_state,
    particle_weights,
    boundary_flag,
    departing_local_groups,
    migrant_target_holder,
    target_entry_inputs,
    adjacent_cell_label,
):
    gx, gy = lax.axis_index("gx"), lax.axis_index("gy")
    state_tables = jnp.concatenate(
        [
            cell_local_coords,
            particle_speeds,
            thermal_state[:, None, :],
            particle_weights[:, None, :],
            boundary_flag.astype(jnp.float32)[:, None, :],
        ],
        1,
    )
    width = state_tables.shape[1]
    lanes = state_tables.shape[2]
    chosen = departing_local_groups[0]
    leaving = jnp.take(state_tables, chosen, axis=0)
    numbers = jnp.arange(state_tables.shape[0])
    departed = jnp.any(numbers[:, None] == chosen[None, :], 1)
    staying = jnp.where(departed[:, None, None], 0.0, state_tables)
    edge = BND - IN_CAP
    haloed = padded(staying[:edge].reshape((1, 1, edge * width, lanes)), (("gx", 0), ("gy", 1)), 1)
    around = haloed.reshape((9, edge, width, lanes))
    near_x = gx + jnp.array([-1, -1, -1, 0, 0, 0, 1, 1, 1])
    near_y = gy + jnp.array([-1, 0, 1, -1, 0, 1, -1, 0, 1])
    inside = (near_x >= 0) & (near_x < N_GX) & (near_y >= 0) & (near_y < N_GY)
    match = migrant_target_holder.reshape(-1)[None, :] == (near_x * N_GY + near_y)[:, None]
    match = match & inside[:, None]
    ranking = jnp.cumsum(match.astype(jnp.int32), axis=1) - 1
    taken = match[:, None, :] & (ranking[:, None, :] == jnp.arange(IN_CAP)[None, :, None])
    places = place_of(gx, gy)
    wanted = jnp.sum(jnp.where(taken, places[None, None, :], 0), 2)
    present = jnp.any(taken, 2)
    incoming = gather_all(leaving.reshape(MIG * width, lanes)).reshape(-1, width, lanes)
    arrived = jnp.where(present[:, :, None, None], jnp.take(incoming, wanted, axis=0), 0.0)
    first = jnp.concatenate([arrived, around], 1)
    ghosts = jnp.concatenate([first[:4], first[5:]], 0).reshape((-1, width, lanes))
    state = jnp.concatenate([arrived[4], staying, ghosts], 0)
    rows = target_entry_inputs.reshape(-1)
    codes = (adjacent_cell_label + (adjacent_cell_label >= 13).astype(jnp.int32)).reshape(-1)
    square, closing, weights, shift = pair_rows()
    square, closing, weights, heat_place = (jnp.asarray(a, BF16) for a in (square, closing, weights, heat_rows()))
    place = jnp.concatenate([square, closing], 0)
    density = density_call(rows, codes, state, square, weights)
    again = eight_around(
        padded(density[:BND].reshape((1, 1, BND, lanes)), (("gx", 0), ("gy", 1)), 1)
    )
    rho_table = jnp.concatenate([density, again], 0)
    acceleration, heating = force_call(
        rows, codes, state, rho_table, place, heat_place, weights, jnp.asarray(shift)
    )
    return density, acceleration, heating


def solution(mesh):
    return jax.shard_map(
        local,
        mesh=mesh,
        in_specs=(
            P(("gx", "gy"), None, None),
            P(("gx", "gy"), None, None),
            P(("gx", "gy"), None),
            P(("gx", "gy"), None),
            P(("gx", "gy"), None),
            P(("gx", "gy"), None),
            P(),
            P(("gx", "gy"), None),
            P(("gx", "gy"), None),
        ),
        out_specs=(P(("gx", "gy"), None), P(("gx", "gy"), None, None), P(("gx", "gy"), None)),
        check_vma=False,
    )
```

time: 220 us -> 184 us (0.84)
  Pallas kernels: 142 us -> 106 us
    pallas_call x1, Pallas kernels: 102 us -> 74.5 us  [force_call(): pl.pallas_call(force_kernel, out_shape=(jax.ShapeDtypeStruct((SLOTS, 3, L...]
    pallas_call x1, Pallas kernels: 39.8 us -> 31.8 us  [density_call(): pl.pallas_call(density_kernel, out_shape=jax.ShapeDtypeStruct((SLOTS, LAN...]
    unnamed x43 -> x37, local copies, waits for them, and re-layouts: 5.65 us -> 5.62 us
where the time goes in v3:
time: 184 us
  Pallas kernels  106 us (58%)
  starting transfers between devices  39.3 us (21%)
  waiting for transfers between devices  19.5 us (11%)
  local copies, waits for them, and re-layouts  12.2 us (7%)
  other arithmetic  5.22 us (3%)
    pallas_call x1, Pallas kernels, force_call(): pl.pallas_call(force_kernel, out_shape=(jax.ShapeDtypeStruct((SLOTS, 3, L...  74.5 us
    pallas_call x1, Pallas kernels, density_call(): pl.pallas_call(density_kernel, out_shape=jax.ShapeDtypeStruct((SLOTS, LAN...  31.8 us
    ppermute x10, starting transfers between devices, gather_all(): pieces.append(lax.ppermute(shard, ('gx', 'gy'), pairs))  16.4 us
    ppermute x4, starting transfers between devices, padded(): before = lax.ppermute(last, axis, up)  13.1 us
    ppermute x4, waiting for transfers between devices, padded(): after = lax.ppermute(first, axis, down)  10.7 us
    ppermute x4, starting transfers between devices, padded(): after = lax.ppermute(first, axis, down)  9.91 us
    ppermute x10, waiting for transfers between devices, gather_all(): pieces.append(lax.ppermute(shard, ('gx', 'gy'), pairs))  7.49 us
    unnamed x37, local copies, waits for them, and re-layouts  5.62 us
  transfers between devices with their start and end apart: 18, of which 10 were waited for; matrix products, arithmetic and copies ran while one was open for 2% of the time, Pallas kernels for 0%

profile of v3, /device:TPU:25, one launch (start us, length us, event | category | flops | bytes accessed | tf_op | source)
XLA Modules:
  0.0 183.7 jit_solution(12707535513643820530)
XLA Ops:
  7.0 1.6 collective-permute-start
  8.6 3.3 %collective-permute-start.1 = (f32[18,128]{1,0:T(8,128)S(1)}, f32[18,128]{1,0:T(8,128)S(1)}, u32[]{:S(2)}, u32[]{:S(2)}) collective-permute-start(f32[18,128]{1,0:T(8,128)S(1)} %broadcast_select_fusion.1), channel_id=1, source_target_pairs={{0,8},{1,9},{2,10},{3,11},{4,12},{5,13},{6,14},{7,15},{8,0},{9,1},... | collective-permute-start | bytes 27656 | tf_op jit(solution)/shard_map/ppermute | solution.py:447
  13.8 4.5 %collective-permute-start.10 = (f32[1,1,72,128]{3,2,1,0:T(8,128)S(1)}, f32[1,1,72,128]{3,2,1,0:T(8,128)S(1)}, u32[]{:S(2)}, u32[]{:S(2)}) collective-permute-start(f32[1,1,72,128]{3,2,1,0:T(8,128)S(1)} %reshape.290), channel_id=1, source_target_pairs={{0,16},{16,32},{32,48},{48,64},{64,80},{80,96},{96,112},{1,17},{17... | collective-permute-start | bytes 110600 | tf_op jit(solution)/shard_map/ppermute | solution.py:417
  18.3 1.9 %collective-permute-start.11 = (f32[1,1,72,128]{3,2,1,0:T(8,128)S(1)}, f32[1,1,72,128]{3,2,1,0:T(8,128)S(1)}, u32[]{:S(2)}, u32[]{:S(2)}) collective-permute-start(f32[1,1,72,128]{3,2,1,0:T(8,128)S(1)} %reshape.290), channel_id=1, source_target_pairs={{16,0},{32,16},{48,32},{64,48},{80,64},{96,80},{112,96},{17,1},{33... | collective-permute-start | bytes 110600 | tf_op jit(solution)/shard_map/ppermute | solution.py:418
  22.3 2.2 %collective-permute-start.4 = (f32[72,128]{1,0:T(8,128)S(1)}, f32[72,128]{1,0:T(8,128)S(1)}, u32[]{:S(2)}, u32[]{:S(2)}) collective-permute-start(f32[72,128]{1,0:T(8,128)S(1)} %pad_maximum_fusion.5), channel_id=1, source_target_pairs={{0,2},{1,3},{2,0},{3,1},{4,6},{5,7},{6,4},{7,5},{8,10},{9,11},{10,... | collective-permute-start | bytes 110600 | tf_op jit(solution)/shard_map/ppermute | solution.py:447
  25.3 1.5 collective-permute-done.4
  26.7 1.9 %collective-permute-done.5 = f32[72,128]{1,0:T(8,128)S(1)} collective-permute-done((f32[72,128]{1,0:T(8,128)S(1)}, f32[72,128]{1,0:T(8,128)S(1)}, u32[]{:S(2)}, u32[]{:S(2)}) %collective-permute-start.5) | collective-permute-done | bytes 36896 | tf_op jit(solution)/shard_map/ppermute | solution.py:447
  28.9 1.3 collective-permute-start.6
  30.2 1.4 collective-permute-start.7
  31.6 2.0 %collective-permute-start.8 = (f32[288,128]{1,0:T(8,128)S(1)}, f32[288,128]{1,0:T(8,128)S(1)}, u32[]{:S(2)}, u32[]{:S(2)}) collective-permute-start(f32[288,128]{1,0:T(8,128)S(1)} %concatenate.50), channel_id=1, source_target_pairs={{0,96},{1,97},{2,98},{3,99},{4,100},{5,101},{6,102},{7,103},{8,104... | collective-permute-start | bytes 442376 | tf_op jit(solution)/shard_map/ppermute | solution.py:447
  34.2 1.6 collective-permute-done.7
  37.4 3.7 %collective-permute-start.9 = (f32[1152,128]{1,0:T(8,128)S(1)}, f32[1152,128]{1,0:T(8,128)S(1)}, u32[]{:S(2)}, u32[]{:S(2)}) collective-permute-start(f32[1152,128]{1,0:T(8,128)S(1)} %concatenate.51), channel_id=1, source_target_pairs={{0,16},{1,17},{2,18},{3,19},{4,20},{5,21},{6,22},{7,23},{8,24},{9,... | collective-permute-start | bytes 1769480 | tf_op jit(solution)/shard_map/ppermute | solution.py:447
  42.1 2.8 %collective-permute-start.12 = (f32[3,1,72,128]{3,2,1,0:T(8,128)S(1)}, f32[3,1,72,128]{3,2,1,0:T(8,128)S(1)}, u32[]{:S(2)}, u32[]{:S(2)}) collective-permute-start(f32[3,1,72,128]{3,2,1,0:T(8,128)S(1)} %constant_dynamic-update-slice_fusion), channel_id=1, source_target_pairs={{0,1},{1,2},{2,3},{3,4},{4,5},{5,6},{6,7},{7,8},{8,9},{9,10},{10,1... | collective-permute-start | bytes 331784 | tf_op jit(solution)/shard_map/ppermute | solution.py:417
  44.8 2.5 %collective-permute-start.13 = (f32[3,1,72,128]{3,2,1,0:T(8,128)S(1)}, f32[3,1,72,128]{3,2,1,0:T(8,128)S(1)}, u32[]{:S(2)}, u32[]{:S(2)}) collective-permute-start(f32[3,1,72,128]{3,2,1,0:T(8,128)S(1)} %constant_dynamic-update-slice_fusion), channel_id=1, source_target_pairs={{1,0},{2,1},{3,2},{4,3},{5,4},{6,5},{7,6},{8,7},{9,8},{10,9},{11,1... | collective-permute-start | bytes 331784 | tf_op jit(solution)/shard_map/ppermute | solution.py:418
  47.4 1.3 collective-permute-done.12
  48.6 4.6 %collective-permute-done.13 = f32[3,1,72,128]{3,2,1,0:T(8,128)S(1)} collective-permute-done((f32[3,1,72,128]{3,2,1,0:T(8,128)S(1)}, f32[3,1,72,128]{3,2,1,0:T(8,128)S(1)}, u32[]{:S(2)}, u32[]{:S(2)}) %collective-permute-start.13) | collective-permute-done | bytes 110624 | tf_op jit(solution)/shard_map/ppermute | solution.py:418
  57.6 31.8 %density_pass.1 = f32[104,128]{1,0:T(8,128)} custom-call(s32[832]{0:T(1024)S(1)} %reshape.286.rows, s32[416]{0:T(512)S(1)} %reshape.287.codes, f32[232,9,128]{2,1,0:T(8,128)S(1)} %pad_maximum_fusion.state, bf16[112,32]{1,0:T(8,128)(2,1)S(1)} %copy-done.4, bf16[32,48,128]{2,1,0:T(8,128)(2,1)S(1)} %copy-done), custom_call_target="tpu_custom_call" | custom-call | tf_op jit(solution)/shard_map/density_pass/pallas_call | solution.py:365
  90.1 3.9 %collective-permute-start.14 = (f32[1,1,16,128]{3,2,1,0:T(8,128)S(1)}, f32[1,1,16,128]{3,2,1,0:T(8,128)S(1)}, u32[]{:S(2)}, u32[]{:S(2)}) collective-permute-start(f32[1,1,16,128]{3,2,1,0:T(8,128)S(1)} %slice_bitcast_fusion.1), channel_id=1, source_target_pairs={{0,16},{16,32},{32,48},{48,64},{64,80},{80,96},{96,112},{1,17},{17... | collective-permute-start | bytes 24584 | tf_op jit(solution)/shard_map/ppermute | solution.py:417
  94.0 1.9 %collective-permute-start.15 = (f32[1,1,16,128]{3,2,1,0:T(8,128)S(1)}, f32[1,1,16,128]{3,2,1,0:T(8,128)S(1)}, u32[]{:S(2)}, u32[]{:S(2)}) collective-permute-start(f32[1,1,16,128]{3,2,1,0:T(8,128)S(1)} %slice_bitcast_fusion.1), channel_id=1, source_target_pairs={{16,0},{32,16},{48,32},{64,48},{80,64},{96,80},{112,96},{17,1},{33... | collective-permute-start | bytes 24584 | tf_op jit(solution)/shard_map/ppermute | solution.py:418
  96.0 3.0 %collective-permute-done.15 = f32[1,1,16,128]{3,2,1,0:T(8,128)S(1)} collective-permute-done((f32[1,1,16,128]{3,2,1,0:T(8,128)S(1)}, f32[1,1,16,128]{3,2,1,0:T(8,128)S(1)}, u32[]{:S(2)}, u32[]{:S(2)}) %collective-permute-start.15) | collective-permute-done | bytes 8224 | tf_op jit(solution)/shard_map/ppermute | solution.py:418
  99.0 1.9 %collective-permute-start.16 = (f32[3,1,16,128]{3,2,1,0:T(8,128)S(1)}, f32[3,1,16,128]{3,2,1,0:T(8,128)S(1)}, u32[]{:S(2)}, u32[]{:S(2)}) collective-permute-start(f32[3,1,16,128]{3,2,1,0:T(8,128)S(1)} %pad_maximum_fusion.6), channel_id=1, source_target_pairs={{0,1},{1,2},{2,3},{3,4},{4,5},{5,6},{6,7},{7,8},{8,9},{9,10},{10,1... | collective-permute-start | bytes 73736 | tf_op jit(solution)/shard_map/ppermute | solution.py:417
  100.9 3.5 %collective-permute-start.17 = (f32[3,1,16,128]{3,2,1,0:T(8,128)S(1)}, f32[3,1,16,128]{3,2,1,0:T(8,128)S(1)}, u32[]{:S(2)}, u32[]{:S(2)}) collective-permute-start(f32[3,1,16,128]{3,2,1,0:T(8,128)S(1)} %pad_maximum_fusion.6), channel_id=1, source_target_pairs={{1,0},{2,1},{3,2},{4,3},{5,4},{6,5},{7,6},{8,7},{9,8},{10,9},{11,1... | collective-permute-start | bytes 73736 | tf_op jit(solution)/shard_map/ppermute | solution.py:418
  104.5 3.1 %collective-permute-done.17 = f32[3,1,16,128]{3,2,1,0:T(8,128)S(1)} collective-permute-done((f32[3,1,16,128]{3,2,1,0:T(8,128)S(1)}, f32[3,1,16,128]{3,2,1,0:T(8,128)S(1)}, u32[]{:S(2)}, u32[]{:S(2)}) %collective-permute-start.17) | collective-permute-done | bytes 24608 | tf_op jit(solution)/shard_map/ppermute | solution.py:418
  108.5 74.5 %force_pass.1 = (f32[104,3,128]{2,1,0:T(4,128)S(1)}, f32[104,128]{1,0:T(8,128)}) custom-call(s32[832]{0:T(1024)S(1)} %reshape.286.rows, s32[416]{0:T(512)S(1)} %reshape.287.codes, f32[232,9,128]{2,1,0:T(8,128)S(1)} %pad_maximum_fusion.state, f32[232,128]{1,0:T(8,128)S(1)} %pad_maximum_fusion.2.rho_table, bf16[224,32]{1,0:T(8,128)(2,1)S(1)} %copy-done.2, ...), custom_call_target="tpu_custom_call" | custom-call | tf_op jit(solution)/shard_map/force_pass/pallas_call | solution.py:383
  (109 shorter events, 20.8 us)
Async XLA Ops:
  3.1 17.3 %copy-start.12 = (s32[128,2]{0,1:T(2,128)S(1)}, s32[128,2]{0,1:T(2,128)}, u32[]{:S(2)}) copy-start(s32[128,2]{0,1:T(2,128)} %param.22) | copy-start | bytes 3076
  4.9 28.6 %copy-start.11 = (s32[104,4]{0,1:T(4,128)S(1)}, s32[104,4]{0,1:T(4,128)}, u32[]{:S(2)}) copy-start(s32[104,4]{0,1:T(4,128)} %param.24) | copy-start | bytes 4996
  7.0 15.3 %collective-permute-start = (f32[18,128]{1,0:T(8,128)S(1)}, f32[18,128]{1,0:T(8,128)S(1)}, u32[]{:S(2)}, u32[]{:S(2)}) collective-permute-start(f32[18,128]{1,0:T(8,128)S(1)} %broadcast_select_fusion.1), channel_id=1, source_target_pairs={{0,4},{1,5},{2,6},{3,7},{4,8},{5,9},{6,10},{7,11},{8,12},{9,13},{1... | collective-permute-start | bytes 27656 | tf_op jit(solution)/shard_map/ppermute | solution.py:447
  8.6 13.6 %collective-permute-start.1 = (f32[18,128]{1,0:T(8,128)S(1)}, f32[18,128]{1,0:T(8,128)S(1)}, u32[]{:S(2)}, u32[]{:S(2)}) collective-permute-start(f32[18,128]{1,0:T(8,128)S(1)} %broadcast_select_fusion.1), channel_id=1, source_target_pairs={{0,8},{1,9},{2,10},{3,11},{4,12},{5,13},{6,14},{7,15},{8,0},{9,1},... | collective-permute-start | bytes 27656 | tf_op jit(solution)/shard_map/ppermute | solution.py:447
  11.9 10.3 %collective-permute-start.2 = (f32[18,128]{1,0:T(8,128)S(1)}, f32[18,128]{1,0:T(8,128)S(1)}, u32[]{:S(2)}, u32[]{:S(2)}) collective-permute-start(f32[18,128]{1,0:T(8,128)S(1)} %broadcast_select_fusion.1), channel_id=1, source_target_pairs={{0,12},{1,13},{2,14},{3,15},{4,0},{5,1},{6,2},{7,3},{8,4},{9,5},{1... | collective-permute-start | bytes 27656 | tf_op jit(solution)/shard_map/ppermute | solution.py:447
  12.7 28.9 %copy-start.8 = (s32[104,8]{0,1:T(8,128)S(1)}, s32[104,8]{0,1:T(8,128)}, u32[]{:S(2)}) copy-start(s32[104,8]{0,1:T(8,128)} %param.23) | copy-start | bytes 9988
  13.8 28.2 %collective-permute-start.10 = (f32[1,1,72,128]{3,2,1,0:T(8,128)S(1)}, f32[1,1,72,128]{3,2,1,0:T(8,128)S(1)}, u32[]{:S(2)}, u32[]{:S(2)}) collective-permute-start(f32[1,1,72,128]{3,2,1,0:T(8,128)S(1)} %reshape.290), channel_id=1, source_target_pairs={{0,16},{16,32},{32,48},{48,64},{64,80},{80,96},{96,112},{1,17},{17... | collective-permute-start | bytes 110600 | tf_op jit(solution)/shard_map/ppermute | solution.py:417
  18.3 23.7 %collective-permute-start.11 = (f32[1,1,72,128]{3,2,1,0:T(8,128)S(1)}, f32[1,1,72,128]{3,2,1,0:T(8,128)S(1)}, u32[]{:S(2)}, u32[]{:S(2)}) collective-permute-start(f32[1,1,72,128]{3,2,1,0:T(8,128)S(1)} %reshape.290), channel_id=1, source_target_pairs={{16,0},{32,16},{48,32},{64,48},{80,64},{96,80},{112,96},{17,1},{33... | collective-permute-start | bytes 110600 | tf_op jit(solution)/shard_map/ppermute | solution.py:418
  22.2 3.0 %collective-permute-start.3 = (f32[72,128]{1,0:T(8,128)S(1)}, f32[72,128]{1,0:T(8,128)S(1)}, u32[]{:S(2)}, u32[]{:S(2)}) collective-permute-start(f32[72,128]{1,0:T(8,128)S(1)} %pad_maximum_fusion.5), channel_id=1, source_target_pairs={{0,1},{1,2},{2,3},{3,0},{4,5},{5,6},{6,7},{7,4},{8,9},{9,10},{10,1... | collective-permute-start | bytes 110600 | tf_op jit(solution)/shard_map/ppermute | solution.py:447
  22.3 4.4 %collective-permute-start.4 = (f32[72,128]{1,0:T(8,128)S(1)}, f32[72,128]{1,0:T(8,128)S(1)}, u32[]{:S(2)}, u32[]{:S(2)}) collective-permute-start(f32[72,128]{1,0:T(8,128)S(1)} %pad_maximum_fusion.5), channel_id=1, source_target_pairs={{0,2},{1,3},{2,0},{3,1},{4,6},{5,7},{6,4},{7,5},{8,10},{9,11},{10,... | collective-permute-start | bytes 110600 | tf_op jit(solution)/shard_map/ppermute | solution.py:447
  24.6 4.0 %collective-permute-start.5 = (f32[72,128]{1,0:T(8,128)S(1)}, f32[72,128]{1,0:T(8,128)S(1)}, u32[]{:S(2)}, u32[]{:S(2)}) collective-permute-start(f32[72,128]{1,0:T(8,128)S(1)} %pad_maximum_fusion.5), channel_id=1, source_target_pairs={{0,3},{1,0},{2,1},{3,2},{4,7},{5,4},{6,5},{7,6},{8,11},{9,8},{10,9... | collective-permute-start | bytes 110600 | tf_op jit(solution)/shard_map/ppermute | solution.py:447
  28.9 5.3 %collective-permute-start.6 = (f32[288,128]{1,0:T(8,128)S(1)}, f32[288,128]{1,0:T(8,128)S(1)}, u32[]{:S(2)}, u32[]{:S(2)}) collective-permute-start(f32[288,128]{1,0:T(8,128)S(1)} %concatenate.50), channel_id=1, source_target_pairs={{0,32},{1,33},{2,34},{3,35},{4,36},{5,37},{6,38},{7,39},{8,40},{9,... | collective-permute-start | bytes 442376 | tf_op jit(solution)/shard_map/ppermute | solution.py:447
  30.2 5.6 %collective-permute-start.7 = (f32[288,128]{1,0:T(8,128)S(1)}, f32[288,128]{1,0:T(8,128)S(1)}, u32[]{:S(2)}, u32[]{:S(2)}) collective-permute-start(f32[288,128]{1,0:T(8,128)S(1)} %concatenate.50), channel_id=1, source_target_pairs={{0,64},{1,65},{2,66},{3,67},{4,68},{5,69},{6,70},{7,71},{8,72},{9,... | collective-permute-start | bytes 442376 | tf_op jit(solution)/shard_map/ppermute | solution.py:447
  31.6 5.5 %collective-permute-start.8 = (f32[288,128]{1,0:T(8,128)S(1)}, f32[288,128]{1,0:T(8,128)S(1)}, u32[]{:S(2)}, u32[]{:S(2)}) collective-permute-start(f32[288,128]{1,0:T(8,128)S(1)} %concatenate.50), channel_id=1, source_target_pairs={{0,96},{1,97},{2,98},{3,99},{4,100},{5,101},{6,102},{7,103},{8,104... | collective-permute-start | bytes 442376 | tf_op jit(solution)/shard_map/ppermute | solution.py:447
  37.4 16.7 %collective-permute-start.9 = (f32[1152,128]{1,0:T(8,128)S(1)}, f32[1152,128]{1,0:T(8,128)S(1)}, u32[]{:S(2)}, u32[]{:S(2)}) collective-permute-start(f32[1152,128]{1,0:T(8,128)S(1)} %concatenate.51), channel_id=1, source_target_pairs={{0,16},{1,17},{2,18},{3,19},{4,20},{5,21},{6,22},{7,23},{8,24},{9,... | collective-permute-start | bytes 1769480 | tf_op jit(solution)/shard_map/ppermute | solution.py:447
  42.1 6.6 %collective-permute-start.12 = (f32[3,1,72,128]{3,2,1,0:T(8,128)S(1)}, f32[3,1,72,128]{3,2,1,0:T(8,128)S(1)}, u32[]{:S(2)}, u32[]{:S(2)}) collective-permute-start(f32[3,1,72,128]{3,2,1,0:T(8,128)S(1)} %constant_dynamic-update-slice_fusion), channel_id=1, source_target_pairs={{0,1},{1,2},{2,3},{3,4},{4,5},{5,6},{6,7},{7,8},{8,9},{9,10},{10,1... | collective-permute-start | bytes 331784 | tf_op jit(solution)/shard_map/ppermute | solution.py:417
  44.8 8.4 %collective-permute-start.13 = (f32[3,1,72,128]{3,2,1,0:T(8,128)S(1)}, f32[3,1,72,128]{3,2,1,0:T(8,128)S(1)}, u32[]{:S(2)}, u32[]{:S(2)}) collective-permute-start(f32[3,1,72,128]{3,2,1,0:T(8,128)S(1)} %constant_dynamic-update-slice_fusion), channel_id=1, source_target_pairs={{1,0},{2,1},{3,2},{4,3},{5,4},{6,5},{7,6},{8,7},{9,8},{10,9},{11,1... | collective-permute-start | bytes 331784 | tf_op jit(solution)/shard_map/ppermute | solution.py:418
  57.6 50.8 %copy-start.1 = (f32[32,8,128]{2,1,0:T(8,128)S(1)}, f32[32,8,128]{2,1,0:T(8,128)}, u32[]{:S(2)}) copy-start(f32[32,8,128]{2,1,0:T(8,128)} %constant.192.clone.shift) | copy-start | bytes 393220
  57.6 50.8 %copy-start.2 = (bf16[224,32]{1,0:T(8,128)(2,1)S(1)}, bf16[224,32]{1,0:T(8,128)(2,1)}, u32[]{:S(2)}) copy-start(bf16[224,32]{1,0:T(8,128)(2,1)} %constant.201.place) | copy-start | bytes 43012
  57.6 50.8 %copy-start.3 = (bf16[128,32]{1,0:T(8,128)(2,1)S(1)}, bf16[128,32]{1,0:T(8,128)(2,1)}, u32[]{:S(2)}) copy-start(bf16[128,32]{1,0:T(8,128)(2,1)} %constant.191.clone.heat_place) | copy-start | bytes 24580
  90.1 5.8 %collective-permute-start.14 = (f32[1,1,16,128]{3,2,1,0:T(8,128)S(1)}, f32[1,1,16,128]{3,2,1,0:T(8,128)S(1)}, u32[]{:S(2)}, u32[]{:S(2)}) collective-permute-start(f32[1,1,16,128]{3,2,1,0:T(8,128)S(1)} %slice_bitcast_fusion.1), channel_id=1, source_target_pairs={{0,16},{16,32},{32,48},{48,64},{64,80},{80,96},{96,112},{1,17},{17... | collective-permute-start | bytes 24584 | tf_op jit(solution)/shard_map/ppermute | solution.py:417
  94.0 5.0 %collective-permute-start.15 = (f32[1,1,16,128]{3,2,1,0:T(8,128)S(1)}, f32[1,1,16,128]{3,2,1,0:T(8,128)S(1)}, u32[]{:S(2)}, u32[]{:S(2)}) collective-permute-start(f32[1,1,16,128]{3,2,1,0:T(8,128)S(1)} %slice_bitcast_fusion.1), channel_id=1, source_target_pairs={{16,0},{32,16},{48,32},{64,48},{80,64},{96,80},{112,96},{17,1},{33... | collective-permute-start | bytes 24584 | tf_op jit(solution)/shard_map/ppermute | solution.py:418
  99.0 5.5 %collective-permute-start.16 = (f32[3,1,16,128]{3,2,1,0:T(8,128)S(1)}, f32[3,1,16,128]{3,2,1,0:T(8,128)S(1)}, u32[]{:S(2)}, u32[]{:S(2)}) collective-permute-start(f32[3,1,16,128]{3,2,1,0:T(8,128)S(1)} %pad_maximum_fusion.6), channel_id=1, source_target_pairs={{0,1},{1,2},{2,3},{3,4},{4,5},{5,6},{6,7},{7,8},{8,9},{9,10},{10,1... | collective-permute-start | bytes 73736 | tf_op jit(solution)/shard_map/ppermute | solution.py:417
  100.9 6.7 %collective-permute-start.17 = (f32[3,1,16,128]{3,2,1,0:T(8,128)S(1)}, f32[3,1,16,128]{3,2,1,0:T(8,128)S(1)}, u32[]{:S(2)}, u32[]{:S(2)}) collective-permute-start(f32[3,1,16,128]{3,2,1,0:T(8,128)S(1)} %pad_maximum_fusion.6), channel_id=1, source_target_pairs={{1,0},{2,1},{3,2},{4,3},{5,4},{6,5},{7,6},{8,7},{9,8},{10,9},{11,1... | collective-permute-start | bytes 73736 | tf_op jit(solution)/shard_map/ppermute | solution.py:418
  (8 other events, 51.6 us)

commit v4 on v3

--- a/solution.py
+++ b/solution.py
@@ -137,18 +137,18 @@
 
 def build_tables(own, other, targets):
     def first(u, carry):
-        targets(8 * jnp.maximum(u - 1, 0), 8)
-        for q in range(8):
-            own(8 * jnp.minimum(u, SLOTS // 8 - 1) + q)
+        for q in range(26):
+            own(26 * u + q)
+        targets(26 * u, 26)
         return carry
 
     def second(u, carry):
-        for q in range(8):
-            other(8 * u + q)
+        for q in range(32):
+            other(SLOTS + 32 * u + q)
         return carry
 
-    lax.fori_loop(0, SLOTS // 8 + 1, first, 0)
-    lax.fori_loop(SLOTS // 8, SOURCES // 8, second, 0)
+    lax.fori_loop(0, SLOTS // 26, first, 0)
+    lax.fori_loop(0, (SOURCES - SLOTS) // 32, second, 0)
 
 
 def source_row(rows, t, k):
@@ -246,7 +246,10 @@
                  parts, heat_parts, own_parts, mass_parts, pressures, own_pressure, left, heat_left, *buffers):
     pairs, heats, split_terms, heat_sums = (buffers[2 * FORCE_BATCH * q : 2 * FORCE_BATCH * (q + 1)] for q in range(4))
 
-    def each(b):
+    row = lax.broadcasted_iota(jnp.int32, (32, LANES), 0)
+    pick = jnp.where((row % 8 == 5) & (row < 24), 1.0, 0.0).astype(BF16)
+
+    def each(b, b_own=False):
         parts[b] = parts_of(channels(state, b))
         x, heat, mass, wall = state[b, 0:3, :], state[b, 6:7, :], state[b, 7:8, :], state[b, 8:9, :]
         rho = jnp.where(mass > 0.0, rho_table[pl.ds(b, 1), :], 1.0)
@@ -257,14 +260,17 @@
         a = ratio * (2.0 + 1.2 * wall)
         b2 = ratio * (1.2 + 3.6 * wall)
         zero = jnp.zeros_like(rho)
-        heat_parts[b] = parts_of(jnp.concatenate([a, b2, a * heat, b2 * heat, rho, zero, zero, zero], 0))
-        pressures[b] = jnp.broadcast_to(pressure, (LANES, LANES)).T
+        heat_parts[b] = parts_of(jnp.concatenate([a, b2, a * heat, b2 * heat, rho, pressure, zero, zero], 0))
+        if b_own:
+            pressures[b] = jnp.broadcast_to(pressure, (LANES, LANES)).T
+        else:
+            pressures[b] = dot(heat_parts[b], pick, ((0,), (0,)))
         high, middle, low = split(jnp.concatenate([mass, mass * x, zero, zero, zero, zero], 0))
         mass_parts[b] = jnp.concatenate([high[0:4], middle[0:4], low], 0).astype(BF16)
         return [heat, heat * wall, wall, rho, zero, zero, zero, zero], pressure
 
     def own(b):
-        lines, pressure = each(b)
+        lines, pressure = each(b, True)
         own_parts[b] = parts_of(jnp.concatenate(lines, 0))
         own_pressure[pl.ds(b, 1), :] = pressure
 
@@ -407,17 +413,18 @@
     )(rows, codes, state, rho_table, place, heat_place, weights, shift)
 
 
-def padded(shard, sides, width):
-    for axis, dim in sides:
-        size, length = (lax.axis_size(axis), shard.shape[dim])
-        up = [(i, (i + 1) % size) for i in range(size - 1)]
-        down = [(j, i) for i, j in up]
-        last = lax.slice_in_dim(shard, length - width, length, axis=dim)
-        first = lax.slice_in_dim(shard, 0, width, axis=dim)
-        before = lax.ppermute(last, axis, up)
-        after = lax.ppermute(first, axis, down)
-        shard = jnp.concatenate([before, shard, after], axis=dim)
-    return shard
+def padded(shard, axis, dim):
+    size, here = lax.axis_size(axis), lax.axis_index(axis)
+    even = lax.ppermute(shard, axis, [(i, i ^ 1) for i in range(size)])
+    odd = lax.ppermute(shard, axis, [(i, (((i - 1) ^ 1) + 1) % size if i else size - 1) for i in range(size)])
+    odd = jnp.where((here == 0) | (here == size - 1), 0.0, odd)
+    lower = here % 2 == 0
+    before, after = jnp.where(lower, odd, even), jnp.where(lower, even, odd)
+    return jnp.concatenate([before, shard, after], axis=dim)
+
+
+def halo(shard):
+    return padded(padded(shard[None, None], "gx", 0), "gy", 1)
 
 
 def eight_around(haloed):
@@ -427,7 +434,7 @@
 
 
 def owner(x, core, z, y):
-    return (2 * (x % 4) + core) * N_GY + 4 * (z % 4) + y % 4
+    return (2 * x + core) * N_GY + 4 * z + y
 
 
 CHIPS = [(x, c, z, y) for x in range(4) for c in range(2) for z in range(4) for y in range(4)]
@@ -443,7 +450,7 @@
     for stage in STAGES:
         pieces = [shard]
         for dx, dc, dz, dy in stage:
-            pairs = [(owner(x, c, z, y), owner(x + dx, c ^ dc, z + dz, y + dy)) for x, c, z, y in CHIPS]
+            pairs = [(owner(x, c, z, y), owner(x ^ dx, c ^ dc, z ^ dz, y ^ dy)) for x, c, z, y in CHIPS]
             pieces.append(lax.ppermute(shard, ("gx", "gy"), pairs))
         shard = jnp.concatenate(pieces, 0)
     return shard
@@ -453,9 +460,9 @@
     number = jnp.arange(N_GX * N_GY * MIG)
     ox, oy = number // (MIG * N_GY), number // MIG % N_GY
     core = gx % 2 ^ ox % 2
-    x = (gx // 2 - ox // 2) % 4
-    z = (gy // 4 - oy // 4) % 4
-    y = (gy - oy) % 4
+    x = gx // 2 ^ ox // 2
+    z = gy // 4 ^ oy // 4
+    y = gy % 4 ^ oy % 4
     return (((core * 4 + x) * 4 + y) * 4 + z) * MIG + number % MIG
 
 
@@ -484,12 +491,17 @@
     width = state_tables.shape[1]
     lanes = state_tables.shape[2]
     chosen = departing_local_groups[0]
-    leaving = jnp.take(state_tables, chosen, axis=0)
+    leaving = []
+    for k in range(MIG):
+        for array in (cell_local_coords, particle_speeds, thermal_state, particle_weights, boundary_flag):
+            one = lax.dynamic_index_in_dim(array, chosen[k], 0, False)
+            leaving.append(one.reshape(-1, lanes).astype(jnp.float32))
+    leaving = jnp.concatenate(leaving, 0)
     numbers = jnp.arange(state_tables.shape[0])
     departed = jnp.any(numbers[:, None] == chosen[None, :], 1)
     staying = jnp.where(departed[:, None, None], 0.0, state_tables)
     edge = BND - IN_CAP
-    haloed = padded(staying[:edge].reshape((1, 1, edge * width, lanes)), (("gx", 0), ("gy", 1)), 1)
+    haloed = halo(staying[:edge].reshape((edge * width, lanes)))
     around = haloed.reshape((9, edge, width, lanes))
     near_x = gx + jnp.array([-1, -1, -1, 0, 0, 0, 1, 1, 1])
     near_y = gy + jnp.array([-1, 0, 1, -1, 0, 1, -1, 0, 1])
@@ -501,7 +513,7 @@
     places = place_of(gx, gy)
     wanted = jnp.sum(jnp.where(taken, places[None, None, :], 0), 2)
     present = jnp.any(taken, 2)
-    incoming = gather_all(leaving.reshape(MIG * width, lanes)).reshape(-1, width, lanes)
+    incoming = gather_all(leaving).reshape(-1, width, lanes)
     arrived = jnp.where(present[:, :, None, None], jnp.take(incoming, wanted, axis=0), 0.0)
     first = jnp.concatenate([arrived, around], 1)
     ghosts = jnp.concatenate([first[:4], first[5:]], 0).reshape((-1, width, lanes))
@@ -512,9 +524,7 @@
     square, closing, weights, heat_place = (jnp.asarray(a, BF16) for a in (square, closing, weights, heat_rows()))
     place = jnp.concatenate([square, closing], 0)
     density = density_call(rows, codes, state, square, weights)
-    again = eight_around(
-        padded(density[:BND].reshape((1, 1, BND, lanes)), (("gx", 0), ("gy", 1)), 1)
-    )
+    again = eight_around(halo(density[:BND]))
     rho_table = jnp.concatenate([density, again], 0)
     acceleration, heating = force_call(
         rows, codes, state, rho_table, place, heat_place, weights, jnp.asarray(shift)

time: 184 us -> 175 us (0.951)
  the two profiles are of different devices: /device:TPU:25 before, /device:TPU:0 now
where the time goes in v4:
time: 175 us; the launch traced here: 174 us
  Pallas kernels  102 us (58%)
  starting transfers between devices  24.6 us (14%)
  waiting for transfers between devices  22.1 us (13%)
  local copies, waits for them, and re-layouts  15.1 us (9%)
  other arithmetic  5.17 us (3%)
  between operations  4.96 us (3%)
    pallas_call x1, Pallas kernels, force_call(): pl.pallas_call(force_kernel, out_shape=(jax.ShapeDtypeStruct((SLOTS, 3, L...  71.7 us
    pallas_call x1, Pallas kernels, density_call(): pl.pallas_call(density_kernel, out_shape=jax.ShapeDtypeStruct((SLOTS, LAN...  30.3 us
    ppermute x10, starting transfers between devices, gather_all(): pieces.append(lax.ppermute(shard, ('gx', 'gy'), pairs))  15.3 us
    ppermute x4, waiting for transfers between devices, padded(): lax.ppermute(shard, axis, [(i, ((i - 1 ^ 1) + 1) % size if i else size -...  12.7 us
    ppermute x10, waiting for transfers between devices, gather_all(): pieces.append(lax.ppermute(shard, ('gx', 'gy'), pairs))  9.35 us
    ppermute x4, starting transfers between devices, padded(): lax.ppermute(shard, axis, [(i, ((i - 1 ^ 1) + 1) % size if i else size -...  9.31 us
    unnamed x37, local copies, waits for them, and re-layouts  5.59 us
  transfers between devices with their start and end apart: 18, of which 8 were waited for; matrix products, arithmetic and copies ran while one was open for 6% of the time, Pallas kernels for 0%

profile of v4, /device:TPU:0, one launch (start us, length us, event | category | flops | bytes accessed | tf_op | source)
XLA Modules:
  0.0 174.0 jit_solution(9387778594772577273)
XLA Ops:
  0.6 1.3 fusion.13
  8.2 2.1 %collective-permute-start = (f32[18,128]{1,0:T(8,128)S(1)}, f32[18,128]{1,0:T(8,128)S(1)}, u32[]{:S(2)}, u32[]{:S(2)}) collective-permute-start(f32[18,128]{1,0:T(8,128)S(1)} %concatenate.52), channel_id=1, source_target_pairs={{0,4},{1,5},{2,6},{3,7},{4,0},{5,1},{6,2},{7,3},{8,12},{9,13},{10,... | collective-permute-start | bytes 27656 | tf_op jit(solution)/shard_map/ppermute | solution.py:454
  10.2 3.6 %collective-permute-start.1 = (f32[18,128]{1,0:T(8,128)S(1)}, f32[18,128]{1,0:T(8,128)S(1)}, u32[]{:S(2)}, u32[]{:S(2)}) collective-permute-start(f32[18,128]{1,0:T(8,128)S(1)} %concatenate.52), channel_id=1, source_target_pairs={{0,8},{1,9},{2,10},{3,11},{4,12},{5,13},{6,14},{7,15},{8,0},{9,1},... | collective-permute-start | bytes 27656 | tf_op jit(solution)/shard_map/ppermute | solution.py:454
  13.8 1.0 copy.41
  14.9 1.0 copy.42
  17.5 1.2 concatenate.57
  19.8 1.7 collective-permute-start.10
  23.9 1.7 collective-permute-start.3
  25.5 2.9 %collective-permute-start.4 = (f32[72,128]{1,0:T(8,128)S(1)}, f32[72,128]{1,0:T(8,128)S(1)}, u32[]{:S(2)}, u32[]{:S(2)}) collective-permute-start(f32[72,128]{1,0:T(8,128)S(1)} %concatenate.53), channel_id=1, source_target_pairs={{0,2},{1,3},{2,0},{3,1},{4,6},{5,7},{6,4},{7,5},{8,10},{9,11},{10,... | collective-permute-start | bytes 110600 | tf_op jit(solution)/shard_map/ppermute | solution.py:454
  28.7 2.4 %collective-permute-done.4 = f32[72,128]{1,0:T(8,128)S(1)} collective-permute-done((f32[72,128]{1,0:T(8,128)S(1)}, f32[72,128]{1,0:T(8,128)S(1)}, u32[]{:S(2)}, u32[]{:S(2)}) %collective-permute-start.4) | collective-permute-done | bytes 36896 | tf_op jit(solution)/shard_map/ppermute | solution.py:454
  31.1 2.5 %collective-permute-done.5 = f32[72,128]{1,0:T(8,128)S(1)} collective-permute-done((f32[72,128]{1,0:T(8,128)S(1)}, f32[72,128]{1,0:T(8,128)S(1)}, u32[]{:S(2)}, u32[]{:S(2)}) %collective-permute-start.5) | collective-permute-done | bytes 36896 | tf_op jit(solution)/shard_map/ppermute | solution.py:454
  34.1 1.5 collective-permute-start.6
  35.6 1.7 collective-permute-start.7
  37.3 1.5 collective-permute-start.8
  40.3 2.3 %collective-permute-done.7 = f32[288,128]{1,0:T(8,128)S(1)} collective-permute-done((f32[288,128]{1,0:T(8,128)S(1)}, f32[288,128]{1,0:T(8,128)S(1)}, u32[]{:S(2)}, u32[]{:S(2)}) %collective-permute-start.7) | collective-permute-done | bytes 147488 | tf_op jit(solution)/shard_map/ppermute | solution.py:454
  42.6 1.5 collective-permute-done.8
  44.7 3.0 %collective-permute-start.12 = (f32[3,1,72,128]{3,2,1,0:T(8,128)S(1)}, f32[3,1,72,128]{3,2,1,0:T(8,128)S(1)}, u32[]{:S(2)}, u32[]{:S(2)}) collective-permute-start(f32[3,1,72,128]{3,2,1,0:T(8,128)S(1)} %pad_maximum_fusion.3), channel_id=1, source_target_pairs={{0,15},{1,2},{2,1},{3,4},{4,3},{5,6},{6,5},{7,8},{8,7},{9,10},{10,... | collective-permute-start | bytes 331784 | tf_op jit(solution)/shard_map/ppermute | solution.py:419
  47.8 5.8 %collective-permute-done.12 = f32[3,1,72,128]{3,2,1,0:T(8,128)S(1)} collective-permute-done((f32[3,1,72,128]{3,2,1,0:T(8,128)S(1)}, f32[3,1,72,128]{3,2,1,0:T(8,128)S(1)}, u32[]{:S(2)}, u32[]{:S(2)}) %collective-permute-start.12) | collective-permute-done | bytes 110624 | tf_op jit(solution)/shard_map/ppermute | solution.py:419
  58.1 30.3 %density_pass.1 = f32[104,128]{1,0:T(8,128)} custom-call(s32[832]{0:T(1024)S(1)} %reshape.231.rows, s32[416]{0:T(512)S(1)} %reshape.232.codes, f32[232,9,128]{2,1,0:T(8,128)S(1)} %pad_maximum_fusion.state, bf16[112,32]{1,0:T(8,128)(2,1)S(1)} %copy-done.4, bf16[32,48,128]{2,1,0:T(8,128)(2,1)S(1)} %copy-done), custom_call_target="tpu_custom_call" | custom-call | tf_op jit(solution)/shard_map/density_pass/pallas_call | solution.py:371
  89.2 1.5 collective-permute-start.14
  90.7 2.8 %collective-permute-done.14 = f32[1,1,16,128]{3,2,1,0:T(8,128)S(1)} collective-permute-done((f32[1,1,16,128]{3,2,1,0:T(8,128)S(1)}, f32[1,1,16,128]{3,2,1,0:T(8,128)S(1)}, u32[]{:S(2)}, u32[]{:S(2)}) %collective-permute-start.14) | collective-permute-done | bytes 8224 | tf_op jit(solution)/shard_map/ppermute | solution.py:419
  93.5 3.0 %collective-permute-start.16 = (f32[3,1,16,128]{3,2,1,0:T(8,128)S(1)}, f32[3,1,16,128]{3,2,1,0:T(8,128)S(1)}, u32[]{:S(2)}, u32[]{:S(2)}) collective-permute-start(f32[3,1,16,128]{3,2,1,0:T(8,128)S(1)} %pad_maximum_fusion.6), channel_id=1, source_target_pairs={{0,15},{1,2},{2,1},{3,4},{4,3},{5,6},{6,5},{7,8},{8,7},{9,10},{10,... | collective-permute-start | bytes 73736 | tf_op jit(solution)/shard_map/ppermute | solution.py:419
  96.5 4.2 %collective-permute-done.16 = f32[3,1,16,128]{3,2,1,0:T(8,128)S(1)} collective-permute-done((f32[3,1,16,128]{3,2,1,0:T(8,128)S(1)}, f32[3,1,16,128]{3,2,1,0:T(8,128)S(1)}, u32[]{:S(2)}, u32[]{:S(2)}) %collective-permute-start.16) | collective-permute-done | bytes 24608 | tf_op jit(solution)/shard_map/ppermute | solution.py:419
  101.6 71.7 %force_pass.1 = (f32[104,3,128]{2,1,0:T(4,128)S(1)}, f32[104,128]{1,0:T(8,128)}) custom-call(s32[832]{0:T(1024)S(1)} %reshape.231.rows, s32[416]{0:T(512)S(1)} %reshape.232.codes, f32[232,9,128]{2,1,0:T(8,128)S(1)} %pad_maximum_fusion.state, f32[232,128]{1,0:T(8,128)S(1)} %pad_maximum_fusion.2.rho_table, bf16[224,32]{1,0:T(8,128)(2,1)S(1)} %copy-done.2, ...), custom_call_target="tpu_custom_call" | custom-call | tf_op jit(solution)/shard_map/force_pass/pallas_call | solution.py:389
  (110 shorter events, 16.6 us)
Async XLA Ops:
  8.2 15.2 %collective-permute-start = (f32[18,128]{1,0:T(8,128)S(1)}, f32[18,128]{1,0:T(8,128)S(1)}, u32[]{:S(2)}, u32[]{:S(2)}) collective-permute-start(f32[18,128]{1,0:T(8,128)S(1)} %concatenate.52), channel_id=1, source_target_pairs={{0,4},{1,5},{2,6},{3,7},{4,0},{5,1},{6,2},{7,3},{8,12},{9,13},{10,... | collective-permute-start | bytes 27656 | tf_op jit(solution)/shard_map/ppermute | solution.py:454
  10.2 13.2 %collective-permute-start.1 = (f32[18,128]{1,0:T(8,128)S(1)}, f32[18,128]{1,0:T(8,128)S(1)}, u32[]{:S(2)}, u32[]{:S(2)}) collective-permute-start(f32[18,128]{1,0:T(8,128)S(1)} %concatenate.52), channel_id=1, source_target_pairs={{0,8},{1,9},{2,10},{3,11},{4,12},{5,13},{6,14},{7,15},{8,0},{9,1},... | collective-permute-start | bytes 27656 | tf_op jit(solution)/shard_map/ppermute | solution.py:454
  13.8 9.6 %collective-permute-start.2 = (f32[18,128]{1,0:T(8,128)S(1)}, f32[18,128]{1,0:T(8,128)S(1)}, u32[]{:S(2)}, u32[]{:S(2)}) collective-permute-start(f32[18,128]{1,0:T(8,128)S(1)} %concatenate.52), channel_id=1, source_target_pairs={{0,12},{1,13},{2,14},{3,15},{4,8},{5,9},{6,10},{7,11},{8,4},{9,5},... | collective-permute-start | bytes 27656 | tf_op jit(solution)/shard_map/ppermute | solution.py:454
  14.9 6.7 %copy-start.12 = (s32[128,2]{0,1:T(2,128)S(1)}, s32[128,2]{0,1:T(2,128)}, u32[]{:S(2)}) copy-start(s32[128,2]{0,1:T(2,128)} %param.22) | copy-start | bytes 3076
  17.4 21.4 %copy-start.11 = (s32[104,4]{0,1:T(4,128)S(1)}, s32[104,4]{0,1:T(4,128)}, u32[]{:S(2)}) copy-start(s32[104,4]{0,1:T(4,128)} %param.24) | copy-start | bytes 4996
  17.4 21.8 %copy-start.8 = (s32[104,8]{0,1:T(8,128)S(1)}, s32[104,8]{0,1:T(8,128)}, u32[]{:S(2)}) copy-start(s32[104,8]{0,1:T(8,128)} %param.23) | copy-start | bytes 9988
  19.8 24.9 %collective-permute-start.10 = (f32[1,1,72,128]{3,2,1,0:T(8,128)S(1)}, f32[1,1,72,128]{3,2,1,0:T(8,128)S(1)}, u32[]{:S(2)}, u32[]{:S(2)}) collective-permute-start(f32[1,1,72,128]{3,2,1,0:T(8,128)S(1)} %broadcast_in_dim_reshape.4), channel_id=1, source_target_pairs={{0,112},{16,32},{32,16},{48,64},{64,48},{80,96},{96,80},{112,0},{1... | collective-permute-start | bytes 110600 | tf_op jit(solution)/shard_map/ppermute | solution.py:419
  21.5 23.2 %collective-permute-start.11 = (f32[1,1,72,128]{3,2,1,0:T(8,128)S(1)}, f32[1,1,72,128]{3,2,1,0:T(8,128)S(1)}, u32[]{:S(2)}, u32[]{:S(2)}) collective-permute-start(f32[1,1,72,128]{3,2,1,0:T(8,128)S(1)} %broadcast_in_dim_reshape.4), channel_id=1, source_target_pairs={{0,16},{16,0},{32,48},{48,32},{64,80},{80,64},{96,112},{112,96},{1... | collective-permute-start | bytes 110600 | tf_op jit(solution)/shard_map/ppermute | solution.py:418
  23.9 4.8 %collective-permute-start.3 = (f32[72,128]{1,0:T(8,128)S(1)}, f32[72,128]{1,0:T(8,128)S(1)}, u32[]{:S(2)}, u32[]{:S(2)}) collective-permute-start(f32[72,128]{1,0:T(8,128)S(1)} %concatenate.53), channel_id=1, source_target_pairs={{0,1},{1,0},{2,3},{3,2},{4,5},{5,4},{6,7},{7,6},{8,9},{9,8},{10,11... | collective-permute-start | bytes 110600 | tf_op jit(solution)/shard_map/ppermute | solution.py:454
  25.5 5.5 %collective-permute-start.4 = (f32[72,128]{1,0:T(8,128)S(1)}, f32[72,128]{1,0:T(8,128)S(1)}, u32[]{:S(2)}, u32[]{:S(2)}) collective-permute-start(f32[72,128]{1,0:T(8,128)S(1)} %concatenate.53), channel_id=1, source_target_pairs={{0,2},{1,3},{2,0},{3,1},{4,6},{5,7},{6,4},{7,5},{8,10},{9,11},{10,... | collective-permute-start | bytes 110600 | tf_op jit(solution)/shard_map/ppermute | solution.py:454
  28.4 5.2 %collective-permute-start.5 = (f32[72,128]{1,0:T(8,128)S(1)}, f32[72,128]{1,0:T(8,128)S(1)}, u32[]{:S(2)}, u32[]{:S(2)}) collective-permute-start(f32[72,128]{1,0:T(8,128)S(1)} %concatenate.53), channel_id=1, source_target_pairs={{0,3},{1,2},{2,1},{3,0},{4,7},{5,6},{6,5},{7,4},{8,11},{9,10},{10,... | collective-permute-start | bytes 110600 | tf_op jit(solution)/shard_map/ppermute | solution.py:454
  34.1 6.2 %collective-permute-start.6 = (f32[288,128]{1,0:T(8,128)S(1)}, f32[288,128]{1,0:T(8,128)S(1)}, u32[]{:S(2)}, u32[]{:S(2)}) collective-permute-start(f32[288,128]{1,0:T(8,128)S(1)} %concatenate.54), channel_id=1, source_target_pairs={{0,32},{1,33},{2,34},{3,35},{4,36},{5,37},{6,38},{7,39},{8,40},{9,... | collective-permute-start | bytes 442376 | tf_op jit(solution)/shard_map/ppermute | solution.py:454
  35.6 7.0 %collective-permute-start.7 = (f32[288,128]{1,0:T(8,128)S(1)}, f32[288,128]{1,0:T(8,128)S(1)}, u32[]{:S(2)}, u32[]{:S(2)}) collective-permute-start(f32[288,128]{1,0:T(8,128)S(1)} %concatenate.54), channel_id=1, source_target_pairs={{0,64},{1,65},{2,66},{3,67},{4,68},{5,69},{6,70},{7,71},{8,72},{9,... | collective-permute-start | bytes 442376 | tf_op jit(solution)/shard_map/ppermute | solution.py:454
  37.3 6.8 %collective-permute-start.8 = (f32[288,128]{1,0:T(8,128)S(1)}, f32[288,128]{1,0:T(8,128)S(1)}, u32[]{:S(2)}, u32[]{:S(2)}) collective-permute-start(f32[288,128]{1,0:T(8,128)S(1)} %concatenate.54), channel_id=1, source_target_pairs={{0,96},{1,97},{2,98},{3,99},{4,100},{5,101},{6,102},{7,103},{8,104... | collective-permute-start | bytes 442376 | tf_op jit(solution)/shard_map/ppermute | solution.py:454
  44.6 9.9 %collective-permute-start.9 = (f32[1152,128]{1,0:T(8,128)S(1)}, f32[1152,128]{1,0:T(8,128)S(1)}, u32[]{:S(2)}, u32[]{:S(2)}) collective-permute-start(f32[1152,128]{1,0:T(8,128)S(1)} %concatenate.55), channel_id=1, source_target_pairs={{0,16},{1,17},{2,18},{3,19},{4,20},{5,21},{6,22},{7,23},{8,24},{9,... | collective-permute-start | bytes 1769480 | tf_op jit(solution)/shard_map/ppermute | solution.py:454
  44.7 8.8 %collective-permute-start.12 = (f32[3,1,72,128]{3,2,1,0:T(8,128)S(1)}, f32[3,1,72,128]{3,2,1,0:T(8,128)S(1)}, u32[]{:S(2)}, u32[]{:S(2)}) collective-permute-start(f32[3,1,72,128]{3,2,1,0:T(8,128)S(1)} %pad_maximum_fusion.3), channel_id=1, source_target_pairs={{0,15},{1,2},{2,1},{3,4},{4,3},{5,6},{6,5},{7,8},{8,7},{9,10},{10,... | collective-permute-start | bytes 331784 | tf_op jit(solution)/shard_map/ppermute | solution.py:419
  47.8 5.8 %collective-permute-start.13 = (f32[3,1,72,128]{3,2,1,0:T(8,128)S(1)}, f32[3,1,72,128]{3,2,1,0:T(8,128)S(1)}, u32[]{:S(2)}, u32[]{:S(2)}) collective-permute-start(f32[3,1,72,128]{3,2,1,0:T(8,128)S(1)} %pad_maximum_fusion.3), channel_id=1, source_target_pairs={{0,1},{1,0},{2,3},{3,2},{4,5},{5,4},{6,7},{7,6},{8,9},{9,8},{10,11... | collective-permute-start | bytes 331784 | tf_op jit(solution)/shard_map/ppermute | solution.py:418
  58.1 43.4 %copy-start.1 = (f32[32,8,128]{2,1,0:T(8,128)S(1)}, f32[32,8,128]{2,1,0:T(8,128)}, u32[]{:S(2)}) copy-start(f32[32,8,128]{2,1,0:T(8,128)} %constant.212.clone.shift) | copy-start | bytes 393220
  58.1 43.4 %copy-start.2 = (bf16[224,32]{1,0:T(8,128)(2,1)S(1)}, bf16[224,32]{1,0:T(8,128)(2,1)}, u32[]{:S(2)}) copy-start(bf16[224,32]{1,0:T(8,128)(2,1)} %constant.221.place) | copy-start | bytes 43012
  58.1 43.5 %copy-start.3 = (bf16[128,32]{1,0:T(8,128)(2,1)S(1)}, bf16[128,32]{1,0:T(8,128)(2,1)}, u32[]{:S(2)}) copy-start(bf16[128,32]{1,0:T(8,128)(2,1)} %constant.211.clone.heat_place) | copy-start | bytes 24580
  89.2 4.3 %collective-permute-start.14 = (f32[1,1,16,128]{3,2,1,0:T(8,128)S(1)}, f32[1,1,16,128]{3,2,1,0:T(8,128)S(1)}, u32[]{:S(2)}, u32[]{:S(2)}) collective-permute-start(f32[1,1,16,128]{3,2,1,0:T(8,128)S(1)} %slice_bitcast_fusion.1), channel_id=1, source_target_pairs={{0,112},{16,32},{32,16},{48,64},{64,48},{80,96},{96,80},{112,0},{1... | collective-permute-start | bytes 24584 | tf_op jit(solution)/shard_map/ppermute | solution.py:419
  90.7 2.8 %collective-permute-start.15 = (f32[1,1,16,128]{3,2,1,0:T(8,128)S(1)}, f32[1,1,16,128]{3,2,1,0:T(8,128)S(1)}, u32[]{:S(2)}, u32[]{:S(2)}) collective-permute-start(f32[1,1,16,128]{3,2,1,0:T(8,128)S(1)} %slice_bitcast_fusion.1), channel_id=1, source_target_pairs={{0,16},{16,0},{32,48},{48,32},{64,80},{80,64},{96,112},{112,96},{1... | collective-permute-start | bytes 24584 | tf_op jit(solution)/shard_map/ppermute | solution.py:418
  93.5 7.2 %collective-permute-start.16 = (f32[3,1,16,128]{3,2,1,0:T(8,128)S(1)}, f32[3,1,16,128]{3,2,1,0:T(8,128)S(1)}, u32[]{:S(2)}, u32[]{:S(2)}) collective-permute-start(f32[3,1,16,128]{3,2,1,0:T(8,128)S(1)} %pad_maximum_fusion.6), channel_id=1, source_target_pairs={{0,15},{1,2},{2,1},{3,4},{4,3},{5,6},{6,5},{7,8},{8,7},{9,10},{10,... | collective-permute-start | bytes 73736 | tf_op jit(solution)/shard_map/ppermute | solution.py:419
  96.5 4.2 %collective-permute-start.17 = (f32[3,1,16,128]{3,2,1,0:T(8,128)S(1)}, f32[3,1,16,128]{3,2,1,0:T(8,128)S(1)}, u32[]{:S(2)}, u32[]{:S(2)}) collective-permute-start(f32[3,1,16,128]{3,2,1,0:T(8,128)S(1)} %pad_maximum_fusion.6), channel_id=1, source_target_pairs={{0,1},{1,0},{2,3},{3,2},{4,5},{5,4},{6,7},{7,6},{8,9},{9,8},{10,11... | collective-permute-start | bytes 73736 | tf_op jit(solution)/shard_map/ppermute | solution.py:418
  (7 other events, 18.4 us)

commit v5 on v4

--- a/solution.py
+++ b/solution.py
@@ -113,12 +113,16 @@
     return jnp.concatenate(rows, 0)
 
 
+def line(state, channel, b):
+    return state[channel, pl.ds(b, 1), :]
+
+
 def channels(state, b):
-    x = state[b, 0:3, :]
-    v = state[b, 3:6, :] * KAPPA
-    n = jnp.sum(x * x, 0, keepdims=True)
-    vx = jnp.sum(x * v, 0, keepdims=True)
-    return jnp.concatenate([x, v, n, vx], 0)
+    x = [line(state, k, b) for k in range(3)]
+    v = [line(state, 3 + k, b) * KAPPA for k in range(3)]
+    n = x[0] * x[0] + x[1] * x[1] + x[2] * x[2]
+    vx = x[0] * v[0] + x[1] * v[1] + x[2] * v[2]
+    return jnp.concatenate([*x, *v, n, vx], 0)
 
 
 def dot(a, b, contract):
@@ -221,14 +225,14 @@
 
     def work(t, slot):
         square = squares[slot]
-        masses = [state.at[source_row(rows, t, k)] for k in range(LINKS)]
+        row = [source_row(rows, t, k) for k in range(LINKS)]
         for o in range(16):
             total = None
             for k in range(LINKS):
                 s = jnp.maximum(square[8 * o : 8 * o + 8, LANES * k : LANES * (k + 1)], TINY)
                 w = jnp.maximum(1.0 - s * lax.rsqrt(s), 0.0)
                 w2 = w * w
-                term = (w2 * w2) * (1.25 - w) * masses[k][7:8, :]
+                term = (w2 * w2) * (1.25 - w) * line(state, 7, row[k])
                 total = term if total is None else total + term
             sums[slot][8 * o : 8 * o + 8, :] = total
             if o % 3 == 0:
@@ -236,7 +240,7 @@
 
     def close(t, slot):
         rho = jnp.sum(sums[slot][...].T, 0, keepdims=True) * (4.0 * KERNEL)
-        out[pl.ds(t, 1), :] = jnp.where(state[t, 7:8, :] > 0.0, rho, 0.0)
+        out[pl.ds(t, 1), :] = jnp.where(line(state, 7, t) > 0.0, rho, 0.0)
         yield
 
     paired_loop(stage, work, close, DENSITY_BATCH)
@@ -251,7 +255,7 @@
 
     def each(b, b_own=False):
         parts[b] = parts_of(channels(state, b))
-        x, heat, mass, wall = state[b, 0:3, :], state[b, 6:7, :], state[b, 7:8, :], state[b, 8:9, :]
+        heat, mass, wall = (line(state, channel, b) for channel in (6, 7, 8))
         rho = jnp.where(mass > 0.0, rho_table[pl.ds(b, 1), :], 1.0)
         inverse = 1.0 / rho
         r2 = rho * rho
@@ -265,7 +269,9 @@
             pressures[b] = jnp.broadcast_to(pressure, (LANES, LANES)).T
         else:
             pressures[b] = dot(heat_parts[b], pick, ((0,), (0,)))
-        high, middle, low = split(jnp.concatenate([mass, mass * x, zero, zero, zero, zero], 0))
+        high, middle, low = split(
+            jnp.concatenate([mass, *(mass * line(state, k, b) for k in range(3)), zero, zero, zero, zero], 0)
+        )
         mass_parts[b] = jnp.concatenate([high[0:4], middle[0:4], low], 0).astype(BF16)
         return [heat, heat * wall, wall, rho, zero, zero, zero, zero], pressure
 
@@ -342,15 +348,13 @@
                     moved[axis] = more if moved[axis] is None else moved[axis] + more
             yield
         total = total[0:4] + total[4:8] + total[8:12]
-        mass, fluid = state[t, 7:8, :], 1.0 - state[t, 8:9, :]
+        mass, fluid = line(state, 7, t), 1.0 - line(state, 8, t)
         living = mass > 0.0
-        lines = []
         for k in range(3):
-            push = SLOPE * (state[t, k : k + 1, :] * total[0:1] - (total[1 + k : 2 + k] + moved[k]))
+            push = SLOPE * (line(state, k, t) * total[0:1] - (total[1 + k : 2 + k] + moved[k]))
             if k == 2:
                 push = push - GRAVITY
-            lines.append(jnp.where(living, push * fluid, 0.0))
-        out_a[t] = jnp.concatenate(lines, 0)
+            out_a[k, pl.ds(t, 1), :] = jnp.where(living, push * fluid, 0.0)
         warm = jnp.sum(heat_sums[slot][...], 0, keepdims=True)
         rho = jnp.where(living, rho_table[pl.ds(t, 1), :], 1.0)
         out_h[pl.ds(t, 1), :] = jnp.where(living, -SLOPE * warm / rho, 0.0)
@@ -389,7 +393,7 @@
     return pl.pallas_call(
         force_kernel,
         out_shape=(
-            jax.ShapeDtypeStruct((SLOTS, 3, LANES), F32),
+            jax.ShapeDtypeStruct((3, SLOTS, LANES), F32),
             jax.ShapeDtypeStruct((SLOTS, LANES), F32),
         ),
         in_specs=[SMEM] * 2 + [VMEM] * 6,
@@ -446,14 +450,20 @@
 )
 
 
-def gather_all(shard):
-    for stage in STAGES:
-        pieces = [shard]
-        for dx, dc, dz, dy in stage:
-            pairs = [(owner(x, c, z, y), owner(x ^ dx, c ^ dc, z ^ dz, y ^ dy)) for x, c, z, y in CHIPS]
-            pieces.append(lax.ppermute(shard, ("gx", "gy"), pairs))
-        shard = jnp.concatenate(pieces, 0)
-    return shard
+def gather_stage(shard, stage):
+    pieces = [shard]
+    for dx, dc, dz, dy in STAGES[stage]:
+        pairs = [(owner(x, c, z, y), owner(x ^ dx, c ^ dc, z ^ dz, y ^ dy)) for x, c, z, y in CHIPS]
+        pieces.append(lax.ppermute(shard, ("gx", "gy"), pairs))
+    return jnp.concatenate(pieces, 0)
+
+
+def exchange(leaving, edge):
+    leaving = gather_stage(leaving, 0)
+    leaving, edge = lax.optimization_barrier((leaving, edge[None, None]))
+    leaving, edge = lax.optimization_barrier((gather_stage(leaving, 1), padded(edge, "gx", 0)))
+    leaving, edge = lax.optimization_barrier((gather_stage(leaving, 2), padded(edge, "gy", 1)))
+    return gather_stage(leaving, 3), edge
 
 
 def place_of(gx, gy):
@@ -480,29 +490,22 @@
     gx, gy = lax.axis_index("gx"), lax.axis_index("gy")
     state_tables = jnp.concatenate(
         [
-            cell_local_coords,
-            particle_speeds,
-            thermal_state[:, None, :],
-            particle_weights[:, None, :],
-            boundary_flag.astype(jnp.float32)[:, None, :],
+            cell_local_coords.transpose(1, 0, 2),
+            particle_speeds.transpose(1, 0, 2),
+            thermal_state[None],
+            particle_weights[None],
+            boundary_flag.astype(jnp.float32)[None],
         ],
-        1,
+        0,
     )
-    width = state_tables.shape[1]
-    lanes = state_tables.shape[2]
+    width, blocks, lanes = state_tables.shape
     chosen = departing_local_groups[0]
-    leaving = []
-    for k in range(MIG):
-        for array in (cell_local_coords, particle_speeds, thermal_state, particle_weights, boundary_flag):
-            one = lax.dynamic_index_in_dim(array, chosen[k], 0, False)
-            leaving.append(one.reshape(-1, lanes).astype(jnp.float32))
-    leaving = jnp.concatenate(leaving, 0)
-    numbers = jnp.arange(state_tables.shape[0])
-    departed = jnp.any(numbers[:, None] == chosen[None, :], 1)
-    staying = jnp.where(departed[:, None, None], 0.0, state_tables)
+    leaving = jnp.take(state_tables, chosen, axis=1).transpose(1, 0, 2)
+    departed = jnp.any(jnp.arange(blocks)[:, None] == chosen[None, :], 1)
+    staying = jnp.where(departed[None, :, None], 0.0, state_tables)
     edge = BND - IN_CAP
-    haloed = halo(staying[:edge].reshape((edge * width, lanes)))
-    around = haloed.reshape((9, edge, width, lanes))
+    incoming, haloed = exchange(leaving.reshape(MIG * width, lanes), staying[:, :edge].reshape(width * edge, lanes))
+    around = haloed.reshape((9, width, edge, lanes))
     near_x = gx + jnp.array([-1, -1, -1, 0, 0, 0, 1, 1, 1])
     near_y = gy + jnp.array([-1, 0, 1, -1, 0, 1, -1, 0, 1])
     inside = (near_x >= 0) & (near_x < N_GX) & (near_y >= 0) & (near_y < N_GY)
@@ -513,11 +516,11 @@
     places = place_of(gx, gy)
     wanted = jnp.sum(jnp.where(taken, places[None, None, :], 0), 2)
     present = jnp.any(taken, 2)
-    incoming = gather_all(leaving).reshape(-1, width, lanes)
-    arrived = jnp.where(present[:, :, None, None], jnp.take(incoming, wanted, axis=0), 0.0)
-    first = jnp.concatenate([arrived, around], 1)
-    ghosts = jnp.concatenate([first[:4], first[5:]], 0).reshape((-1, width, lanes))
-    state = jnp.concatenate([arrived[4], staying, ghosts], 0)
+    incoming = incoming.reshape(-1, width, lanes)
+    arrived = jnp.where(present[:, :, None, None], jnp.take(incoming, wanted, axis=0), 0.0).transpose(0, 2, 1, 3)
+    first = jnp.concatenate([arrived, around], 2)
+    ghosts = [first[q] for q in range(9) if q != 4]
+    state = jnp.concatenate([arrived[4], staying, *ghosts], 1)
     rows = target_entry_inputs.reshape(-1)
     codes = (adjacent_cell_label + (adjacent_cell_label >= 13).astype(jnp.int32)).reshape(-1)
     square, closing, weights, shift = pair_rows()
@@ -529,7 +532,7 @@
     acceleration, heating = force_call(
         rows, codes, state, rho_table, place, heat_place, weights, jnp.asarray(shift)
     )
-    return density, acceleration, heating
+    return density, acceleration.transpose(1, 0, 2), heating
 
 
 def solution(mesh):

time: 175 us -> 165 us (0.943)
  local copies, waits for them, and re-layouts: 15.1 us -> 10.9 us
  between operations: 4.96 us -> 1.12 us
    ppermute x4, waiting for transfers between devices: 12.7 us -> 7.62 us  [padded(): lax.ppermute(shard, axis, [(i, ((i - 1 ^ 1) + 1) % size if i else size -...]
    concatenate x6 -> x1, local copies, waits for them, and re-layouts: 3.29 us -> 0.28 us  [local(): jnp.concatenate([cell_local_coords.transpose(1, 0, 2), particle_speeds.tr...]
    ppermute x10, waiting for transfers between devices: 9.35 us -> 11.5 us  [gather_stage(): pieces.append(lax.ppermute(shard, ('gx', 'gy'), pairs))]
    ppermute x4, starting transfers between devices: 9.31 us -> 7.19 us  [padded(): lax.ppermute(shard, axis, [(i, ((i - 1 ^ 1) + 1) % size if i else size -...]
    unnamed x37 -> x31, local copies, waits for them, and re-layouts: 5.59 us -> 4.69 us
  transfers between devices with their start and end apart: 18 -> 18, of which waited for: 8 -> 10; matrix products, arithmetic and copies ran while one was open for 6% -> 2% of each run, Pallas kernels for 0% -> 0%
where the time goes in v5:
time: 165 us; the launch traced here: 164 us
  Pallas kernels  102 us (62%)
  starting transfers between devices  23.7 us (14%)
  waiting for transfers between devices  20.8 us (13%)
  local copies, waits for them, and re-layouts  10.9 us (7%)
  other arithmetic  5.16 us (3%)
    pallas_call x1, Pallas kernels, force_call(): pl.pallas_call(force_kernel, out_shape=(jax.ShapeDtypeStruct((3, SLOTS, L...  71.8 us
    pallas_call x1, Pallas kernels, density_call(): pl.pallas_call(density_kernel, out_shape=jax.ShapeDtypeStruct((SLOTS, LAN...  30.6 us
    ppermute x10, starting transfers between devices, gather_stage(): pieces.append(lax.ppermute(shard, ('gx', 'gy'), pairs))  15.2 us
    ppermute x10, waiting for transfers between devices, gather_stage(): pieces.append(lax.ppermute(shard, ('gx', 'gy'), pairs))  11.5 us
    ppermute x4, waiting for transfers between devices, padded(): lax.ppermute(shard, axis, [(i, ((i - 1 ^ 1) + 1) % size if i else size -...  7.62 us
    ppermute x4, starting transfers between devices, padded(): lax.ppermute(shard, axis, [(i, ((i - 1 ^ 1) + 1) % size if i else size -...  7.19 us
    unnamed x31, local copies, waits for them, and re-layouts  4.69 us
  transfers between devices with their start and end apart: 18, of which 10 were waited for; matrix products, arithmetic and copies ran while one was open for 2% of the time, Pallas kernels for 0%

profile of v5, /device:TPU:0, one launch (start us, length us, event | category | flops | bytes accessed | tf_op | source)
XLA Modules:
  0.0 164.2 jit_solution(1919606694460590639)
XLA Ops:
  2.0 0.9 bitcast_dynamic-update-slice_fusion.1
  7.2 2.0 %collective-permute-start = (f32[18,128]{1,0:T(8,128)S(1)}, f32[18,128]{1,0:T(8,128)S(1)}, u32[]{:S(2)}, u32[]{:S(2)}) collective-permute-start(f32[18,128]{1,0:T(8,128)S(1)} %reshape.258), channel_id=1, source_target_pairs={{0,4},{1,5},{2,6},{3,7},{4,0},{5,1},{6,2},{7,3},{8,12},{9,13},{10,... | collective-permute-start | bytes 27656 | tf_op jit(solution)/shard_map/ppermute | solution.py:457
  9.2 3.6 %collective-permute-start.1 = (f32[18,128]{1,0:T(8,128)S(1)}, f32[18,128]{1,0:T(8,128)S(1)}, u32[]{:S(2)}, u32[]{:S(2)}) collective-permute-start(f32[18,128]{1,0:T(8,128)S(1)} %reshape.258), channel_id=1, source_target_pairs={{0,8},{1,9},{2,10},{3,11},{4,12},{5,13},{6,14},{7,15},{8,0},{9,1},... | collective-permute-start | bytes 27656 | tf_op jit(solution)/shard_map/ppermute | solution.py:457
  14.6 3.1 %collective-permute-done.2 = f32[18,128]{1,0:T(8,128)S(1)} collective-permute-done((f32[18,128]{1,0:T(8,128)S(1)}, f32[18,128]{1,0:T(8,128)S(1)}, u32[]{:S(2)}, u32[]{:S(2)}) %collective-permute-start.2) | collective-permute-done | bytes 9248 | tf_op jit(solution)/shard_map/ppermute | solution.py:457
  18.3 1.1 collective-permute-start.7
  19.8 1.6 collective-permute-start.3
  21.4 2.9 %collective-permute-start.4 = (f32[72,128]{1,0:T(8,128)S(1)}, f32[72,128]{1,0:T(8,128)S(1)}, u32[]{:S(2)}, u32[]{:S(2)}) collective-permute-start(f32[72,128]{1,0:T(8,128)S(1)} %pad_maximum_fusion.9), channel_id=1, source_target_pairs={{0,2},{1,3},{2,0},{3,1},{4,6},{5,7},{6,4},{7,5},{8,10},{9,11},{10,... | collective-permute-start | bytes 110600 | tf_op jit(solution)/shard_map/ppermute | solution.py:457
  24.5 2.3 %collective-permute-done.4 = f32[72,128]{1,0:T(8,128)S(1)} collective-permute-done((f32[72,128]{1,0:T(8,128)S(1)}, f32[72,128]{1,0:T(8,128)S(1)}, u32[]{:S(2)}, u32[]{:S(2)}) %collective-permute-start.4) | collective-permute-done | bytes 36896 | tf_op jit(solution)/shard_map/ppermute | solution.py:457
  26.8 2.6 %collective-permute-done.5 = f32[72,128]{1,0:T(8,128)S(1)} collective-permute-done((f32[72,128]{1,0:T(8,128)S(1)}, f32[72,128]{1,0:T(8,128)S(1)}, u32[]{:S(2)}, u32[]{:S(2)}) %collective-permute-start.5) | collective-permute-done | bytes 36896 | tf_op jit(solution)/shard_map/ppermute | solution.py:457
  30.2 1.8 %collective-permute-start.10 = (f32[288,128]{1,0:T(8,128)S(1)}, f32[288,128]{1,0:T(8,128)S(1)}, u32[]{:S(2)}, u32[]{:S(2)}) collective-permute-start(f32[288,128]{1,0:T(8,128)S(1)} %pad_maximum_fusion.3), channel_id=1, source_target_pairs={{0,96},{1,97},{2,98},{3,99},{4,100},{5,101},{6,102},{7,103},{8,104... | collective-permute-start | bytes 442376 | tf_op jit(solution)/shard_map/ppermute | solution.py:457
  32.0 0.9 collective-permute-start.8
  32.9 2.0 %collective-permute-start.9 = (f32[288,128]{1,0:T(8,128)S(1)}, f32[288,128]{1,0:T(8,128)S(1)}, u32[]{:S(2)}, u32[]{:S(2)}) collective-permute-start(f32[288,128]{1,0:T(8,128)S(1)} %pad_maximum_fusion.3), channel_id=1, source_target_pairs={{0,64},{1,65},{2,66},{3,67},{4,68},{5,69},{6,70},{7,71},{8,72},{9,... | collective-permute-start | bytes 442376 | tf_op jit(solution)/shard_map/ppermute | solution.py:457
  34.9 2.6 %collective-permute-done.11 = f32[3,1,72,128]{3,2,1,0:T(8,128)S(1)} collective-permute-done((f32[3,1,72,128]{3,2,1,0:T(8,128)S(1)}, f32[3,1,72,128]{3,2,1,0:T(8,128)S(1)}, u32[]{:S(2)}, u32[]{:S(2)}) %collective-permute-start.11) | collective-permute-done | bytes 110624 | tf_op jit(solution)/shard_map/ppermute | solution.py:423
  38.1 1.6 collective-permute-done.9
  40.4 1.5 collective-permute-done.13
  41.9 1.5 reshape.259
  43.4 2.2 %gather_fusion.1 = f32[72,9,128]{2,1,0:T(8,128)S(1)} fusion(f32[256,9,128]{2,1,0:T(8,128)} %reshape.259, s32[1024]{0:T(1024)S(1)} %pad_clamp_fusion), kind=kCustom, calls=%fused_computation.1 | custom fusion | bytes 663840 | tf_op jit(solution)/shard_map/jit(_take)/gather | solution.py:520
  47.0 30.6 %density_pass.1 = f32[104,128]{1,0:T(8,128)} custom-call(s32[832]{0:T(1024)S(1)} %reshape.255.rows, s32[416]{0:T(512)S(1)} %reshape.256.codes, f32[9,232,128]{2,1,0:T(8,128)S(1)} %fusion.3.state, bf16[112,32]{1,0:T(8,128)(2,1)S(1)} %copy-done.4, bf16[32,48,128]{2,1,0:T(8,128)(2,1)S(1)} %copy-done), custom_call_target="tpu_custom_call" | custom-call | tf_op jit(solution)/shard_map/density_pass/pallas_call | solution.py:375
  78.3 1.5 collective-permute-start.14
  79.8 2.8 %collective-permute-done.14 = f32[1,1,16,128]{3,2,1,0:T(8,128)S(1)} collective-permute-done((f32[1,1,16,128]{3,2,1,0:T(8,128)S(1)}, f32[1,1,16,128]{3,2,1,0:T(8,128)S(1)}, u32[]{:S(2)}, u32[]{:S(2)}) %collective-permute-start.14) | collective-permute-done | bytes 8224 | tf_op jit(solution)/shard_map/ppermute | solution.py:423
  82.6 5.1 %collective-permute-start.16 = (f32[3,1,16,128]{3,2,1,0:T(8,128)S(1)}, f32[3,1,16,128]{3,2,1,0:T(8,128)S(1)}, u32[]{:S(2)}, u32[]{:S(2)}) collective-permute-start(f32[3,1,16,128]{3,2,1,0:T(8,128)S(1)} %pad_maximum_fusion.10), channel_id=1, source_target_pairs={{0,15},{1,2},{2,1},{3,4},{4,3},{5,6},{6,5},{7,8},{8,7},{9,10},{10,... | collective-permute-start | bytes 73736 | tf_op jit(solution)/shard_map/ppermute | solution.py:423
  87.6 2.2 %collective-permute-done.16 = f32[3,1,16,128]{3,2,1,0:T(8,128)S(1)} collective-permute-done((f32[3,1,16,128]{3,2,1,0:T(8,128)S(1)}, f32[3,1,16,128]{3,2,1,0:T(8,128)S(1)}, u32[]{:S(2)}, u32[]{:S(2)}) %collective-permute-start.16) | collective-permute-done | bytes 24608 | tf_op jit(solution)/shard_map/ppermute | solution.py:423
  89.8 1.7 %collective-permute-done.17 = f32[3,1,16,128]{3,2,1,0:T(8,128)S(1)} collective-permute-done((f32[3,1,16,128]{3,2,1,0:T(8,128)S(1)}, f32[3,1,16,128]{3,2,1,0:T(8,128)S(1)}, u32[]{:S(2)}, u32[]{:S(2)}) %collective-permute-start.17) | collective-permute-done | bytes 24608 | tf_op jit(solution)/shard_map/ppermute | solution.py:422
  92.4 71.8 %force_pass.1 = (f32[3,104,128]{2,1,0:T(8,128)}, f32[104,128]{1,0:T(8,128)}) custom-call(s32[832]{0:T(1024)S(1)} %reshape.255.rows, s32[416]{0:T(512)S(1)} %reshape.256.codes, f32[9,232,128]{2,1,0:T(8,128)S(1)} %fusion.3.state, f32[232,128]{1,0:T(8,128)S(1)} %pad_maximum_fusion.4.rho_table, bf16[224,32]{1,0:T(8,128)(2,1)S(1)} %copy-done.2, ...), custom_call_target="tpu_custom_call" | custom-call | tf_op jit(solution)/shard_map/force_pass/pallas_call | solution.py:393
  (109 shorter events, 13.2 us)
Async XLA Ops:
  2.0 10.9 %copy-start.7 = (s32[9]{0:T(128)S(1)}, s32[9]{0:T(128)}, u32[]{:S(2)}) copy-start(s32[9]{0:T(128)} %constant.194.clone) | copy-start | bytes 112
  2.0 10.9 %copy-start.9 = (s32[128,2]{0,1:T(2,128)S(1)}, s32[128,2]{0,1:T(2,128)}, u32[]{:S(2)}) copy-start(s32[128,2]{0,1:T(2,128)} %param.22) | copy-start | bytes 3076
  7.2 7.4 %collective-permute-start = (f32[18,128]{1,0:T(8,128)S(1)}, f32[18,128]{1,0:T(8,128)S(1)}, u32[]{:S(2)}, u32[]{:S(2)}) collective-permute-start(f32[18,128]{1,0:T(8,128)S(1)} %reshape.258), channel_id=1, source_target_pairs={{0,4},{1,5},{2,6},{3,7},{4,0},{5,1},{6,2},{7,3},{8,12},{9,13},{10,... | collective-permute-start | bytes 27656 | tf_op jit(solution)/shard_map/ppermute | solution.py:457
  9.2 5.4 %collective-permute-start.1 = (f32[18,128]{1,0:T(8,128)S(1)}, f32[18,128]{1,0:T(8,128)S(1)}, u32[]{:S(2)}, u32[]{:S(2)}) collective-permute-start(f32[18,128]{1,0:T(8,128)S(1)} %reshape.258), channel_id=1, source_target_pairs={{0,8},{1,9},{2,10},{3,11},{4,12},{5,13},{6,14},{7,15},{8,0},{9,1},... | collective-permute-start | bytes 27656 | tf_op jit(solution)/shard_map/ppermute | solution.py:457
  12.8 4.9 %collective-permute-start.2 = (f32[18,128]{1,0:T(8,128)S(1)}, f32[18,128]{1,0:T(8,128)S(1)}, u32[]{:S(2)}, u32[]{:S(2)}) collective-permute-start(f32[18,128]{1,0:T(8,128)S(1)} %reshape.258), channel_id=1, source_target_pairs={{0,12},{1,13},{2,14},{3,15},{4,8},{5,9},{6,10},{7,11},{8,4},{9,5},... | collective-permute-start | bytes 27656 | tf_op jit(solution)/shard_map/ppermute | solution.py:457
  13.1 16.8 %copy-start.5 = (s32[104,8]{0,1:T(8,128)S(1)}, s32[104,8]{0,1:T(8,128)}, u32[]{:S(2)}) copy-start(s32[104,8]{0,1:T(8,128)} %param.23) | copy-start | bytes 9988
  17.7 6.7 %collective-permute-start.6 = (f32[1,1,72,128]{3,2,1,0:T(8,128)S(1)}, f32[1,1,72,128]{3,2,1,0:T(8,128)S(1)}, u32[]{:S(2)}, u32[]{:S(2)}) collective-permute-start(f32[1,1,72,128]{3,2,1,0:T(8,128)S(1)} %slice_bitcast_fusion.1), channel_id=1, source_target_pairs={{0,112},{16,32},{32,16},{48,64},{64,48},{80,96},{96,80},{112,0},{1... | collective-permute-start | bytes 110600 | tf_op jit(solution)/shard_map/ppermute | solution.py:423
  18.3 6.2 %collective-permute-start.7 = (f32[1,1,72,128]{3,2,1,0:T(8,128)S(1)}, f32[1,1,72,128]{3,2,1,0:T(8,128)S(1)}, u32[]{:S(2)}, u32[]{:S(2)}) collective-permute-start(f32[1,1,72,128]{3,2,1,0:T(8,128)S(1)} %slice_bitcast_fusion.1), channel_id=1, source_target_pairs={{0,16},{16,0},{32,48},{48,32},{64,80},{80,64},{96,112},{112,96},{1... | collective-permute-start | bytes 110600 | tf_op jit(solution)/shard_map/ppermute | solution.py:422
  19.8 4.8 %collective-permute-start.3 = (f32[72,128]{1,0:T(8,128)S(1)}, f32[72,128]{1,0:T(8,128)S(1)}, u32[]{:S(2)}, u32[]{:S(2)}) collective-permute-start(f32[72,128]{1,0:T(8,128)S(1)} %pad_maximum_fusion.9), channel_id=1, source_target_pairs={{0,1},{1,0},{2,3},{3,2},{4,5},{5,4},{6,7},{7,6},{8,9},{9,8},{10,11... | collective-permute-start | bytes 110600 | tf_op jit(solution)/shard_map/ppermute | solution.py:457
  21.4 5.5 %collective-permute-start.4 = (f32[72,128]{1,0:T(8,128)S(1)}, f32[72,128]{1,0:T(8,128)S(1)}, u32[]{:S(2)}, u32[]{:S(2)}) collective-permute-start(f32[72,128]{1,0:T(8,128)S(1)} %pad_maximum_fusion.9), channel_id=1, source_target_pairs={{0,2},{1,3},{2,0},{3,1},{4,6},{5,7},{6,4},{7,5},{8,10},{9,11},{10,... | collective-permute-start | bytes 110600 | tf_op jit(solution)/shard_map/ppermute | solution.py:457
  24.3 5.2 %collective-permute-start.5 = (f32[72,128]{1,0:T(8,128)S(1)}, f32[72,128]{1,0:T(8,128)S(1)}, u32[]{:S(2)}, u32[]{:S(2)}) collective-permute-start(f32[72,128]{1,0:T(8,128)S(1)} %pad_maximum_fusion.9), channel_id=1, source_target_pairs={{0,3},{1,2},{2,1},{3,0},{4,7},{5,6},{6,5},{7,4},{8,11},{9,10},{10,... | collective-permute-start | bytes 110600 | tf_op jit(solution)/shard_map/ppermute | solution.py:457
  29.4 8.1 %collective-permute-start.11 = (f32[3,1,72,128]{3,2,1,0:T(8,128)S(1)}, f32[3,1,72,128]{3,2,1,0:T(8,128)S(1)}, u32[]{:S(2)}, u32[]{:S(2)}) collective-permute-start(f32[3,1,72,128]{3,2,1,0:T(8,128)S(1)} %pad_maximum_fusion.5), channel_id=1, source_target_pairs={{0,15},{1,2},{2,1},{3,4},{4,3},{5,6},{6,5},{7,8},{8,7},{9,10},{10,... | collective-permute-start | bytes 331784 | tf_op jit(solution)/shard_map/ppermute | solution.py:423
  29.5 8.1 %collective-permute-start.12 = (f32[3,1,72,128]{3,2,1,0:T(8,128)S(1)}, f32[3,1,72,128]{3,2,1,0:T(8,128)S(1)}, u32[]{:S(2)}, u32[]{:S(2)}) collective-permute-start(f32[3,1,72,128]{3,2,1,0:T(8,128)S(1)} %pad_maximum_fusion.5), channel_id=1, source_target_pairs={{0,1},{1,0},{2,3},{3,2},{4,5},{5,4},{6,7},{7,6},{8,9},{9,8},{10,11... | collective-permute-start | bytes 331784 | tf_op jit(solution)/shard_map/ppermute | solution.py:422
  30.2 8.0 %collective-permute-start.10 = (f32[288,128]{1,0:T(8,128)S(1)}, f32[288,128]{1,0:T(8,128)S(1)}, u32[]{:S(2)}, u32[]{:S(2)}) collective-permute-start(f32[288,128]{1,0:T(8,128)S(1)} %pad_maximum_fusion.3), channel_id=1, source_target_pairs={{0,96},{1,97},{2,98},{3,99},{4,100},{5,101},{6,102},{7,103},{8,104... | collective-permute-start | bytes 442376 | tf_op jit(solution)/shard_map/ppermute | solution.py:457
  32.0 6.1 %collective-permute-start.8 = (f32[288,128]{1,0:T(8,128)S(1)}, f32[288,128]{1,0:T(8,128)S(1)}, u32[]{:S(2)}, u32[]{:S(2)}) collective-permute-start(f32[288,128]{1,0:T(8,128)S(1)} %pad_maximum_fusion.3), channel_id=1, source_target_pairs={{0,32},{1,33},{2,34},{3,35},{4,36},{5,37},{6,38},{7,39},{8,40},{9,... | collective-permute-start | bytes 442376 | tf_op jit(solution)/shard_map/ppermute | solution.py:457
  32.9 6.8 %collective-permute-start.9 = (f32[288,128]{1,0:T(8,128)S(1)}, f32[288,128]{1,0:T(8,128)S(1)}, u32[]{:S(2)}, u32[]{:S(2)}) collective-permute-start(f32[288,128]{1,0:T(8,128)S(1)} %pad_maximum_fusion.3), channel_id=1, source_target_pairs={{0,64},{1,65},{2,66},{3,67},{4,68},{5,69},{6,70},{7,71},{8,72},{9,... | collective-permute-start | bytes 442376 | tf_op jit(solution)/shard_map/ppermute | solution.py:457
  39.8 2.1 %collective-permute-start.13 = (f32[1152,128]{1,0:T(8,128)S(1)}, f32[1152,128]{1,0:T(8,128)S(1)}, u32[]{:S(2)}, u32[]{:S(2)}) collective-permute-start(f32[1152,128]{1,0:T(8,128)S(1)} %pad_maximum_fusion.1), channel_id=1, source_target_pairs={{0,16},{1,17},{2,18},{3,19},{4,20},{5,21},{6,22},{7,23},{8,24},{9,... | collective-permute-start | bytes 1769480 | tf_op jit(solution)/shard_map/ppermute | solution.py:457
  47.0 45.4 %copy-start.1 = (f32[32,8,128]{2,1,0:T(8,128)S(1)}, f32[32,8,128]{2,1,0:T(8,128)}, u32[]{:S(2)}) copy-start(f32[32,8,128]{2,1,0:T(8,128)} %constant.199.clone.shift) | copy-start | bytes 393220
  47.0 45.4 %copy-start.2 = (bf16[224,32]{1,0:T(8,128)(2,1)S(1)}, bf16[224,32]{1,0:T(8,128)(2,1)}, u32[]{:S(2)}) copy-start(bf16[224,32]{1,0:T(8,128)(2,1)} %constant.208.place) | copy-start | bytes 43012
  47.0 45.4 %copy-start.3 = (bf16[128,32]{1,0:T(8,128)(2,1)S(1)}, bf16[128,32]{1,0:T(8,128)(2,1)}, u32[]{:S(2)}) copy-start(bf16[128,32]{1,0:T(8,128)(2,1)} %constant.198.clone.heat_place) | copy-start | bytes 24580
  78.3 4.3 %collective-permute-start.14 = (f32[1,1,16,128]{3,2,1,0:T(8,128)S(1)}, f32[1,1,16,128]{3,2,1,0:T(8,128)S(1)}, u32[]{:S(2)}, u32[]{:S(2)}) collective-permute-start(f32[1,1,16,128]{3,2,1,0:T(8,128)S(1)} %slice_bitcast_fusion.2), channel_id=1, source_target_pairs={{0,112},{16,32},{32,16},{48,64},{64,48},{80,96},{96,80},{112,0},{1... | collective-permute-start | bytes 24584 | tf_op jit(solution)/shard_map/ppermute | solution.py:423
  79.8 2.8 %collective-permute-start.15 = (f32[1,1,16,128]{3,2,1,0:T(8,128)S(1)}, f32[1,1,16,128]{3,2,1,0:T(8,128)S(1)}, u32[]{:S(2)}, u32[]{:S(2)}) collective-permute-start(f32[1,1,16,128]{3,2,1,0:T(8,128)S(1)} %slice_bitcast_fusion.2), channel_id=1, source_target_pairs={{0,16},{16,0},{32,48},{48,32},{64,80},{80,64},{96,112},{112,96},{1... | collective-permute-start | bytes 24584 | tf_op jit(solution)/shard_map/ppermute | solution.py:422
  82.6 7.2 %collective-permute-start.16 = (f32[3,1,16,128]{3,2,1,0:T(8,128)S(1)}, f32[3,1,16,128]{3,2,1,0:T(8,128)S(1)}, u32[]{:S(2)}, u32[]{:S(2)}) collective-permute-start(f32[3,1,16,128]{3,2,1,0:T(8,128)S(1)} %pad_maximum_fusion.10), channel_id=1, source_target_pairs={{0,15},{1,2},{2,1},{3,4},{4,3},{5,6},{6,5},{7,8},{8,7},{9,10},{10,... | collective-permute-start | bytes 73736 | tf_op jit(solution)/shard_map/ppermute | solution.py:423
  87.6 3.8 %collective-permute-start.17 = (f32[3,1,16,128]{3,2,1,0:T(8,128)S(1)}, f32[3,1,16,128]{3,2,1,0:T(8,128)S(1)}, u32[]{:S(2)}, u32[]{:S(2)}) collective-permute-start(f32[3,1,16,128]{3,2,1,0:T(8,128)S(1)} %pad_maximum_fusion.10), channel_id=1, source_target_pairs={{0,1},{1,0},{2,3},{3,2},{4,5},{5,4},{6,7},{7,6},{8,9},{9,8},{10,11... | collective-permute-start | bytes 73736 | tf_op jit(solution)/shard_map/ppermute | solution.py:422
  (5 other events, 32.9 us)

commit v6 on v5

--- a/solution.py
+++ b/solution.py
@@ -202,7 +202,28 @@
 GROUPS = ((0, 1), (2, 3), (4,), (5, 6), (7, 8))
 
 
-def density_kernel(rows, codes, state, place, weights, out, parts, left, *buffers):
+def fill_state(wanted, staying, around, incoming, state):
+    width = state.shape[0]
+
+    def owner_slots(q, first):
+        for s in range(IN_CAP):
+            place = wanted[IN_CAP * q + s]
+            for c in range(width):
+                found = incoming[pl.ds(jnp.maximum(place, 0) * width + c, 1), :]
+                state[c, first + s : first + s + 1, :] = jnp.where(place >= 0, found, 0.0)
+
+    for c in range(width):
+        state[c, IN_CAP:SLOTS, :] = staying[c]
+    owner_slots(4, 0)
+    for at, q in enumerate((0, 1, 2, 3, 5, 6, 7, 8)):
+        first = SLOTS + BND * at
+        owner_slots(q, first)
+        for c in range(width):
+            state[c, first + IN_CAP : first + BND, :] = around[q, c]
+
+
+def density_kernel(rows, codes, wanted, staying, around, incoming, place, weights, out, state, parts, left, *buffers):
+    fill_state(wanted, staying, around, incoming, state)
     squares, sums = buffers[: 2 * DENSITY_BATCH], buffers[2 * DENSITY_BATCH :]
 
     def each(b):
@@ -370,13 +391,16 @@
 FORCE_BATCH = 2
 
 
-def density_call(rows, codes, state, place, weights):
+def density_call(rows, codes, wanted, staying, around, incoming, place, weights):
     wide = (LANES, LINKS * LANES)
     return pl.pallas_call(
         density_kernel,
-        out_shape=jax.ShapeDtypeStruct((SLOTS, LANES), F32),
-        in_specs=[SMEM] * 2 + [VMEM] * 3,
-        out_specs=VMEM,
+        out_shape=(
+            jax.ShapeDtypeStruct((SLOTS, LANES), F32),
+            jax.ShapeDtypeStruct((staying.shape[0], SOURCES, LANES), F32),
+        ),
+        in_specs=[SMEM] * 3 + [VMEM] * 5,
+        out_specs=(VMEM, VMEM),
         scratch_shapes=[
             pltpu.VMEM((SOURCES, 32, LANES), BF16),
             pltpu.VMEM((SLOTS, SHIFTED, LANES), BF16),
@@ -385,7 +409,7 @@
         + [pltpu.VMEM((LANES, LANES), F32)] * (2 * DENSITY_BATCH),
         compiler_params=pltpu.CompilerParams(vmem_limit_bytes=32 << 20),
         name="density_pass",
-    )(rows, codes, state, place, weights)
+    )(rows, codes, wanted, staying, around, incoming, place, weights)
 
 
 def force_call(rows, codes, state, rho_table, place, heat_place, weights, shift):
@@ -516,17 +540,13 @@
     places = place_of(gx, gy)
     wanted = jnp.sum(jnp.where(taken, places[None, None, :], 0), 2)
     present = jnp.any(taken, 2)
-    incoming = incoming.reshape(-1, width, lanes)
-    arrived = jnp.where(present[:, :, None, None], jnp.take(incoming, wanted, axis=0), 0.0).transpose(0, 2, 1, 3)
-    first = jnp.concatenate([arrived, around], 2)
-    ghosts = [first[q] for q in range(9) if q != 4]
-    state = jnp.concatenate([arrived[4], staying, *ghosts], 1)
+    wanted = jnp.where(present, wanted, -1).reshape(-1)
     rows = target_entry_inputs.reshape(-1)
     codes = (adjacent_cell_label + (adjacent_cell_label >= 13).astype(jnp.int32)).reshape(-1)
     square, closing, weights, shift = pair_rows()
     square, closing, weights, heat_place = (jnp.asarray(a, BF16) for a in (square, closing, weights, heat_rows()))
     place = jnp.concatenate([square, closing], 0)
-    density = density_call(rows, codes, state, square, weights)
+    density, state = density_call(rows, codes, wanted, staying, around, incoming, square, weights)
     again = eight_around(halo(density[:BND]))
     rho_table = jnp.concatenate([density, again], 0)
     acceleration, heating = force_call(

time: 165 us -> 160 us (0.970)
  local copies, waits for them, and re-layouts: 10.9 us -> 6.14 us
    gather x1 -> x0, local copies, waits for them, and re-layouts: 2.19 us -> none  [local(): jnp.take(incoming, wanted, axis=0)]
    unnamed x31 -> x30, local copies, waits for them, and re-layouts: 4.69 us -> 3.74 us
  transfers between devices with their start and end apart: 18 -> 18, of which waited for: 10 -> 11; matrix products, arithmetic and copies ran while one was open for 2% -> 2% of each run, Pallas kernels for 0% -> 0%
where the time goes in v6:
time: 160 us; the launch traced here: 159 us
  Pallas kernels  103 us (64%)
  starting transfers between devices  23.8 us (15%)
  waiting for transfers between devices  20.7 us (13%)
  local copies, waits for them, and re-layouts  6.14 us (4%)
  other arithmetic  4.92 us (3%)
    pallas_call x1, Pallas kernels, force_call(): pl.pallas_call(force_kernel, out_shape=(jax.ShapeDtypeStruct((3, SLOTS, L...  71.8 us
    pallas_call x1, Pallas kernels, density_call(): pl.pallas_call(density_kernel, out_shape=(jax.ShapeDtypeStruct((SLOTS, LA...  31 us
    ppermute x10, starting transfers between devices, gather_stage(): pieces.append(lax.ppermute(shard, ('gx', 'gy'), pairs))  15.3 us
    ppermute x10, waiting for transfers between devices, gather_stage(): pieces.append(lax.ppermute(shard, ('gx', 'gy'), pairs))  11.3 us
    ppermute x4, waiting for transfers between devices, padded(): lax.ppermute(shard, axis, [(i, ((i - 1 ^ 1) + 1) % size if i else size -...  7.74 us
    ppermute x4, starting transfers between devices, padded(): lax.ppermute(shard, axis, [(i, ((i - 1 ^ 1) + 1) % size if i else size -...  7.18 us
    unnamed x30, local copies, waits for them, and re-layouts  3.74 us
  transfers between devices with their start and end apart: 18, of which 11 were waited for; matrix products, arithmetic and copies ran while one was open for 2% of the time, Pallas kernels for 0%

profile of v6, /device:TPU:0, one launch (start us, length us, event | category | flops | bytes accessed | tf_op | source)
XLA Modules:
  0.0 159.4 jit_solution(11416203299749522474)
XLA Ops:
  2.1 0.9 bitcast_dynamic-update-slice_fusion.1
  3.0 0.9 bitcast_dynamic-update-slice_fusion
  7.3 2.0 %collective-permute-start = (f32[18,128]{1,0:T(8,128)S(1)}, f32[18,128]{1,0:T(8,128)S(1)}, u32[]{:S(2)}, u32[]{:S(2)}) collective-permute-start(f32[18,128]{1,0:T(8,128)S(1)} %reshape.241), channel_id=1, source_target_pairs={{0,4},{1,5},{2,6},{3,7},{4,0},{5,1},{6,2},{7,3},{8,12},{9,13},{10,... | collective-permute-start | bytes 27656 | tf_op jit(solution)/shard_map/ppermute | solution.py:481
  9.3 3.6 %collective-permute-start.1 = (f32[18,128]{1,0:T(8,128)S(1)}, f32[18,128]{1,0:T(8,128)S(1)}, u32[]{:S(2)}, u32[]{:S(2)}) collective-permute-start(f32[18,128]{1,0:T(8,128)S(1)} %reshape.241), channel_id=1, source_target_pairs={{0,8},{1,9},{2,10},{3,11},{4,12},{5,13},{6,14},{7,15},{8,0},{9,1},... | collective-permute-start | bytes 27656 | tf_op jit(solution)/shard_map/ppermute | solution.py:481
  14.7 3.1 %collective-permute-done.2 = f32[18,128]{1,0:T(8,128)S(1)} collective-permute-done((f32[18,128]{1,0:T(8,128)S(1)}, f32[18,128]{1,0:T(8,128)S(1)}, u32[]{:S(2)}, u32[]{:S(2)}) %collective-permute-start.2) | collective-permute-done | bytes 9248 | tf_op jit(solution)/shard_map/ppermute | solution.py:481
  18.4 1.1 collective-permute-start.7
  19.6 1.7 %collective-permute-start.3 = (f32[72,128]{1,0:T(8,128)S(1)}, f32[72,128]{1,0:T(8,128)S(1)}, u32[]{:S(2)}, u32[]{:S(2)}) collective-permute-start(f32[72,128]{1,0:T(8,128)S(1)} %pad_maximum_fusion.8), channel_id=1, source_target_pairs={{0,1},{1,0},{2,3},{3,2},{4,5},{5,4},{6,7},{7,6},{8,9},{9,8},{10,11... | collective-permute-start | bytes 110600 | tf_op jit(solution)/shard_map/ppermute | solution.py:481
  21.3 2.9 %collective-permute-start.4 = (f32[72,128]{1,0:T(8,128)S(1)}, f32[72,128]{1,0:T(8,128)S(1)}, u32[]{:S(2)}, u32[]{:S(2)}) collective-permute-start(f32[72,128]{1,0:T(8,128)S(1)} %pad_maximum_fusion.8), channel_id=1, source_target_pairs={{0,2},{1,3},{2,0},{3,1},{4,6},{5,7},{6,4},{7,5},{8,10},{9,11},{10,... | collective-permute-start | bytes 110600 | tf_op jit(solution)/shard_map/ppermute | solution.py:481
  24.4 2.3 %collective-permute-done.4 = f32[72,128]{1,0:T(8,128)S(1)} collective-permute-done((f32[72,128]{1,0:T(8,128)S(1)}, f32[72,128]{1,0:T(8,128)S(1)}, u32[]{:S(2)}, u32[]{:S(2)}) %collective-permute-start.4) | collective-permute-done | bytes 36896 | tf_op jit(solution)/shard_map/ppermute | solution.py:481
  26.7 2.6 %collective-permute-done.5 = f32[72,128]{1,0:T(8,128)S(1)} collective-permute-done((f32[72,128]{1,0:T(8,128)S(1)}, f32[72,128]{1,0:T(8,128)S(1)}, u32[]{:S(2)}, u32[]{:S(2)}) %collective-permute-start.5) | collective-permute-done | bytes 36896 | tf_op jit(solution)/shard_map/ppermute | solution.py:481
  30.0 1.8 %collective-permute-start.10 = (f32[288,128]{1,0:T(8,128)S(1)}, f32[288,128]{1,0:T(8,128)S(1)}, u32[]{:S(2)}, u32[]{:S(2)}) collective-permute-start(f32[288,128]{1,0:T(8,128)S(1)} %pad_maximum_fusion.3), channel_id=1, source_target_pairs={{0,96},{1,97},{2,98},{3,99},{4,100},{5,101},{6,102},{7,103},{8,104... | collective-permute-start | bytes 442376 | tf_op jit(solution)/shard_map/ppermute | solution.py:481
  31.8 0.9 collective-permute-start.8
  32.7 2.0 %collective-permute-start.9 = (f32[288,128]{1,0:T(8,128)S(1)}, f32[288,128]{1,0:T(8,128)S(1)}, u32[]{:S(2)}, u32[]{:S(2)}) collective-permute-start(f32[288,128]{1,0:T(8,128)S(1)} %pad_maximum_fusion.3), channel_id=1, source_target_pairs={{0,64},{1,65},{2,66},{3,67},{4,68},{5,69},{6,70},{7,71},{8,72},{9,... | collective-permute-start | bytes 442376 | tf_op jit(solution)/shard_map/ppermute | solution.py:481
  34.8 2.8 %collective-permute-done.11 = f32[3,1,72,128]{3,2,1,0:T(8,128)S(1)} collective-permute-done((f32[3,1,72,128]{3,2,1,0:T(8,128)S(1)}, f32[3,1,72,128]{3,2,1,0:T(8,128)S(1)}, u32[]{:S(2)}, u32[]{:S(2)}) %collective-permute-start.11) | collective-permute-done | bytes 110624 | tf_op jit(solution)/shard_map/ppermute | solution.py:447
  37.9 1.6 collective-permute-done.9
  40.5 1.2 collective-permute-done.13
  41.8 31.0 %density_pass.1 = (f32[104,128]{1,0:T(8,128)}, f32[9,232,128]{2,1,0:T(8,128)S(1)}) custom-call(s32[832]{0:T(1024)S(1)} %reshape.238.rows, s32[416]{0:T(512)S(1)} %reshape.239.codes, s32[72]{0:T(128)S(1)} %select_n.232.wanted, f32[9,96,128]{2,1,0:T(8,128)S(1)} %broadcast_select_fusion.staying, f32[9,9,8,128]{3,2,1,0:T(8,128)S(1)} %bitcast.27, ...), custom_call_target="tpu_custom_call" | custom-call | tf_op jit(solution)/shard_map/density_pass/pallas_call | solution.py:396
  73.5 1.5 collective-permute-start.14
  75.0 2.8 %collective-permute-done.14 = f32[1,1,16,128]{3,2,1,0:T(8,128)S(1)} collective-permute-done((f32[1,1,16,128]{3,2,1,0:T(8,128)S(1)}, f32[1,1,16,128]{3,2,1,0:T(8,128)S(1)}, u32[]{:S(2)}, u32[]{:S(2)}) %collective-permute-start.14) | collective-permute-done | bytes 8224 | tf_op jit(solution)/shard_map/ppermute | solution.py:447
  77.8 5.0 %collective-permute-start.16 = (f32[3,1,16,128]{3,2,1,0:T(8,128)S(1)}, f32[3,1,16,128]{3,2,1,0:T(8,128)S(1)}, u32[]{:S(2)}, u32[]{:S(2)}) collective-permute-start(f32[3,1,16,128]{3,2,1,0:T(8,128)S(1)} %pad_maximum_fusion.9), channel_id=1, source_target_pairs={{0,15},{1,2},{2,1},{3,4},{4,3},{5,6},{6,5},{7,8},{8,7},{9,10},{10,... | collective-permute-start | bytes 73736 | tf_op jit(solution)/shard_map/ppermute | solution.py:447
  82.9 2.2 %collective-permute-done.16 = f32[3,1,16,128]{3,2,1,0:T(8,128)S(1)} collective-permute-done((f32[3,1,16,128]{3,2,1,0:T(8,128)S(1)}, f32[3,1,16,128]{3,2,1,0:T(8,128)S(1)}, u32[]{:S(2)}, u32[]{:S(2)}) %collective-permute-start.16) | collective-permute-done | bytes 24608 | tf_op jit(solution)/shard_map/ppermute | solution.py:447
  85.1 1.6 %collective-permute-done.17 = f32[3,1,16,128]{3,2,1,0:T(8,128)S(1)} collective-permute-done((f32[3,1,16,128]{3,2,1,0:T(8,128)S(1)}, f32[3,1,16,128]{3,2,1,0:T(8,128)S(1)}, u32[]{:S(2)}, u32[]{:S(2)}) %collective-permute-start.17) | collective-permute-done | bytes 24608 | tf_op jit(solution)/shard_map/ppermute | solution.py:446
  86.7 0.8 pad_maximum_fusion.4.rho_table
  87.6 71.8 %force_pass.1 = (f32[3,104,128]{2,1,0:T(8,128)}, f32[104,128]{1,0:T(8,128)}) custom-call(s32[832]{0:T(1024)S(1)} %reshape.238.rows, s32[416]{0:T(512)S(1)} %reshape.239.codes, f32[9,232,128]{2,1,0:T(8,128)S(1)} %get-tuple-element.20.state, f32[232,128]{1,0:T(8,128)S(1)} %pad_maximum_fusion.4.rho_table, bf16[224,32]{1,0:T(8,128)(2,1)S(1)} %copy-done.2, ...), custom_call_target="tpu_custom_call" | custom-call | tf_op jit(solution)/shard_map/force_pass/pallas_call | solution.py:417
  (92 shorter events, 10.1 us)
Async XLA Ops:
  0.6 12.2 %copy-start.6 = (s32[9]{0:T(128)S(1)}, s32[9]{0:T(128)}, u32[]{:S(2)}) copy-start(s32[9]{0:T(128)} %constant.180.clone) | copy-start | bytes 112
  0.6 12.2 %copy-start.7 = (s32[9]{0:T(128)S(1)}, s32[9]{0:T(128)}, u32[]{:S(2)}) copy-start(s32[9]{0:T(128)} %constant.181.clone) | copy-start | bytes 112
  0.7 12.3 %copy-start.10 = (s32[1,2]{1,0:T(1,128)S(1)}, s32[1,2]{1,0:T(1,128)}, u32[]{:S(2)}) copy-start(s32[1,2]{1,0:T(1,128)} %param.21) | copy-start | bytes 28
  7.3 7.2 %collective-permute-start = (f32[18,128]{1,0:T(8,128)S(1)}, f32[18,128]{1,0:T(8,128)S(1)}, u32[]{:S(2)}, u32[]{:S(2)}) collective-permute-start(f32[18,128]{1,0:T(8,128)S(1)} %reshape.241), channel_id=1, source_target_pairs={{0,4},{1,5},{2,6},{3,7},{4,0},{5,1},{6,2},{7,3},{8,12},{9,13},{10,... | collective-permute-start | bytes 27656 | tf_op jit(solution)/shard_map/ppermute | solution.py:481
  9.3 5.4 %collective-permute-start.1 = (f32[18,128]{1,0:T(8,128)S(1)}, f32[18,128]{1,0:T(8,128)S(1)}, u32[]{:S(2)}, u32[]{:S(2)}) collective-permute-start(f32[18,128]{1,0:T(8,128)S(1)} %reshape.241), channel_id=1, source_target_pairs={{0,8},{1,9},{2,10},{3,11},{4,12},{5,13},{6,14},{7,15},{8,0},{9,1},... | collective-permute-start | bytes 27656 | tf_op jit(solution)/shard_map/ppermute | solution.py:481
  12.9 4.9 %collective-permute-start.2 = (f32[18,128]{1,0:T(8,128)S(1)}, f32[18,128]{1,0:T(8,128)S(1)}, u32[]{:S(2)}, u32[]{:S(2)}) collective-permute-start(f32[18,128]{1,0:T(8,128)S(1)} %reshape.241), channel_id=1, source_target_pairs={{0,12},{1,13},{2,14},{3,15},{4,8},{5,9},{6,10},{7,11},{8,4},{9,5},... | collective-permute-start | bytes 27656 | tf_op jit(solution)/shard_map/ppermute | solution.py:481
  17.8 6.6 %collective-permute-start.6 = (f32[1,1,72,128]{3,2,1,0:T(8,128)S(1)}, f32[1,1,72,128]{3,2,1,0:T(8,128)S(1)}, u32[]{:S(2)}, u32[]{:S(2)}) collective-permute-start(f32[1,1,72,128]{3,2,1,0:T(8,128)S(1)} %slice_bitcast_fusion), channel_id=1, source_target_pairs={{0,112},{16,32},{32,16},{48,64},{64,48},{80,96},{96,80},{112,0},{1... | collective-permute-start | bytes 110600 | tf_op jit(solution)/shard_map/ppermute | solution.py:447
  18.4 6.0 %collective-permute-start.7 = (f32[1,1,72,128]{3,2,1,0:T(8,128)S(1)}, f32[1,1,72,128]{3,2,1,0:T(8,128)S(1)}, u32[]{:S(2)}, u32[]{:S(2)}) collective-permute-start(f32[1,1,72,128]{3,2,1,0:T(8,128)S(1)} %slice_bitcast_fusion), channel_id=1, source_target_pairs={{0,16},{16,0},{32,48},{48,32},{64,80},{80,64},{96,112},{112,96},{1... | collective-permute-start | bytes 110600 | tf_op jit(solution)/shard_map/ppermute | solution.py:446
  19.6 4.8 %collective-permute-start.3 = (f32[72,128]{1,0:T(8,128)S(1)}, f32[72,128]{1,0:T(8,128)S(1)}, u32[]{:S(2)}, u32[]{:S(2)}) collective-permute-start(f32[72,128]{1,0:T(8,128)S(1)} %pad_maximum_fusion.8), channel_id=1, source_target_pairs={{0,1},{1,0},{2,3},{3,2},{4,5},{5,4},{6,7},{7,6},{8,9},{9,8},{10,11... | collective-permute-start | bytes 110600 | tf_op jit(solution)/shard_map/ppermute | solution.py:481
  21.3 5.5 %collective-permute-start.4 = (f32[72,128]{1,0:T(8,128)S(1)}, f32[72,128]{1,0:T(8,128)S(1)}, u32[]{:S(2)}, u32[]{:S(2)}) collective-permute-start(f32[72,128]{1,0:T(8,128)S(1)} %pad_maximum_fusion.8), channel_id=1, source_target_pairs={{0,2},{1,3},{2,0},{3,1},{4,6},{5,7},{6,4},{7,5},{8,10},{9,11},{10,... | collective-permute-start | bytes 110600 | tf_op jit(solution)/shard_map/ppermute | solution.py:481
  24.2 5.2 %collective-permute-start.5 = (f32[72,128]{1,0:T(8,128)S(1)}, f32[72,128]{1,0:T(8,128)S(1)}, u32[]{:S(2)}, u32[]{:S(2)}) collective-permute-start(f32[72,128]{1,0:T(8,128)S(1)} %pad_maximum_fusion.8), channel_id=1, source_target_pairs={{0,3},{1,2},{2,1},{3,0},{4,7},{5,6},{6,5},{7,4},{8,11},{9,10},{10,... | collective-permute-start | bytes 110600 | tf_op jit(solution)/shard_map/ppermute | solution.py:481
  29.4 8.1 %collective-permute-start.11 = (f32[3,1,72,128]{3,2,1,0:T(8,128)S(1)}, f32[3,1,72,128]{3,2,1,0:T(8,128)S(1)}, u32[]{:S(2)}, u32[]{:S(2)}) collective-permute-start(f32[3,1,72,128]{3,2,1,0:T(8,128)S(1)} %pad_maximum_fusion.5), channel_id=1, source_target_pairs={{0,15},{1,2},{2,1},{3,4},{4,3},{5,6},{6,5},{7,8},{8,7},{9,10},{10,... | collective-permute-start | bytes 331784 | tf_op jit(solution)/shard_map/ppermute | solution.py:447
  29.5 8.1 %collective-permute-start.12 = (f32[3,1,72,128]{3,2,1,0:T(8,128)S(1)}, f32[3,1,72,128]{3,2,1,0:T(8,128)S(1)}, u32[]{:S(2)}, u32[]{:S(2)}) collective-permute-start(f32[3,1,72,128]{3,2,1,0:T(8,128)S(1)} %pad_maximum_fusion.5), channel_id=1, source_target_pairs={{0,1},{1,0},{2,3},{3,2},{4,5},{5,4},{6,7},{7,6},{8,9},{9,8},{10,11... | collective-permute-start | bytes 331784 | tf_op jit(solution)/shard_map/ppermute | solution.py:446
  30.0 8.0 %collective-permute-start.10 = (f32[288,128]{1,0:T(8,128)S(1)}, f32[288,128]{1,0:T(8,128)S(1)}, u32[]{:S(2)}, u32[]{:S(2)}) collective-permute-start(f32[288,128]{1,0:T(8,128)S(1)} %pad_maximum_fusion.3), channel_id=1, source_target_pairs={{0,96},{1,97},{2,98},{3,99},{4,100},{5,101},{6,102},{7,103},{8,104... | collective-permute-start | bytes 442376 | tf_op jit(solution)/shard_map/ppermute | solution.py:481
  31.8 6.1 %collective-permute-start.8 = (f32[288,128]{1,0:T(8,128)S(1)}, f32[288,128]{1,0:T(8,128)S(1)}, u32[]{:S(2)}, u32[]{:S(2)}) collective-permute-start(f32[288,128]{1,0:T(8,128)S(1)} %pad_maximum_fusion.3), channel_id=1, source_target_pairs={{0,32},{1,33},{2,34},{3,35},{4,36},{5,37},{6,38},{7,39},{8,40},{9,... | collective-permute-start | bytes 442376 | tf_op jit(solution)/shard_map/ppermute | solution.py:481
  32.7 6.8 %collective-permute-start.9 = (f32[288,128]{1,0:T(8,128)S(1)}, f32[288,128]{1,0:T(8,128)S(1)}, u32[]{:S(2)}, u32[]{:S(2)}) collective-permute-start(f32[288,128]{1,0:T(8,128)S(1)} %pad_maximum_fusion.3), channel_id=1, source_target_pairs={{0,64},{1,65},{2,66},{3,67},{4,68},{5,69},{6,70},{7,71},{8,72},{9,... | collective-permute-start | bytes 442376 | tf_op jit(solution)/shard_map/ppermute | solution.py:481
  39.6 2.1 %collective-permute-start.13 = (f32[1152,128]{1,0:T(8,128)S(1)}, f32[1152,128]{1,0:T(8,128)S(1)}, u32[]{:S(2)}, u32[]{:S(2)}) collective-permute-start(f32[1152,128]{1,0:T(8,128)S(1)} %pad_maximum_fusion.1), channel_id=1, source_target_pairs={{0,16},{1,17},{2,18},{3,19},{4,20},{5,21},{6,22},{7,23},{8,24},{9,... | collective-permute-start | bytes 1769480 | tf_op jit(solution)/shard_map/ppermute | solution.py:481
  41.7 45.8 %copy-start.1 = (f32[32,8,128]{2,1,0:T(8,128)S(1)}, f32[32,8,128]{2,1,0:T(8,128)}, u32[]{:S(2)}) copy-start(f32[32,8,128]{2,1,0:T(8,128)} %constant.186.clone.shift) | copy-start | bytes 393220
  41.7 45.8 %copy-start.2 = (bf16[224,32]{1,0:T(8,128)(2,1)S(1)}, bf16[224,32]{1,0:T(8,128)(2,1)}, u32[]{:S(2)}) copy-start(bf16[224,32]{1,0:T(8,128)(2,1)} %constant.195.place) | copy-start | bytes 43012
  41.8 45.8 %copy-start.3 = (bf16[128,32]{1,0:T(8,128)(2,1)S(1)}, bf16[128,32]{1,0:T(8,128)(2,1)}, u32[]{:S(2)}) copy-start(bf16[128,32]{1,0:T(8,128)(2,1)} %constant.185.clone.heat_place) | copy-start | bytes 24580
  73.5 4.3 %collective-permute-start.14 = (f32[1,1,16,128]{3,2,1,0:T(8,128)S(1)}, f32[1,1,16,128]{3,2,1,0:T(8,128)S(1)}, u32[]{:S(2)}, u32[]{:S(2)}) collective-permute-start(f32[1,1,16,128]{3,2,1,0:T(8,128)S(1)} %slice_bitcast_fusion.1), channel_id=1, source_target_pairs={{0,112},{16,32},{32,16},{48,64},{64,48},{80,96},{96,80},{112,0},{1... | collective-permute-start | bytes 24584 | tf_op jit(solution)/shard_map/ppermute | solution.py:447
  75.0 2.8 %collective-permute-start.15 = (f32[1,1,16,128]{3,2,1,0:T(8,128)S(1)}, f32[1,1,16,128]{3,2,1,0:T(8,128)S(1)}, u32[]{:S(2)}, u32[]{:S(2)}) collective-permute-start(f32[1,1,16,128]{3,2,1,0:T(8,128)S(1)} %slice_bitcast_fusion.1), channel_id=1, source_target_pairs={{0,16},{16,0},{32,48},{48,32},{64,80},{80,64},{96,112},{112,96},{1... | collective-permute-start | bytes 24584 | tf_op jit(solution)/shard_map/ppermute | solution.py:446
  77.8 7.2 %collective-permute-start.16 = (f32[3,1,16,128]{3,2,1,0:T(8,128)S(1)}, f32[3,1,16,128]{3,2,1,0:T(8,128)S(1)}, u32[]{:S(2)}, u32[]{:S(2)}) collective-permute-start(f32[3,1,16,128]{3,2,1,0:T(8,128)S(1)} %pad_maximum_fusion.9), channel_id=1, source_target_pairs={{0,15},{1,2},{2,1},{3,4},{4,3},{5,6},{6,5},{7,8},{8,7},{9,10},{10,... | collective-permute-start | bytes 73736 | tf_op jit(solution)/shard_map/ppermute | solution.py:447
  82.9 3.8 %collective-permute-start.17 = (f32[3,1,16,128]{3,2,1,0:T(8,128)S(1)}, f32[3,1,16,128]{3,2,1,0:T(8,128)S(1)}, u32[]{:S(2)}, u32[]{:S(2)}) collective-permute-start(f32[3,1,16,128]{3,2,1,0:T(8,128)S(1)} %pad_maximum_fusion.9), channel_id=1, source_target_pairs={{0,1},{1,0},{2,3},{3,2},{4,5},{5,4},{6,7},{7,6},{8,9},{9,8},{10,11... | collective-permute-start | bytes 73736 | tf_op jit(solution)/shard_map/ppermute | solution.py:446
  (5 other events, 30.5 us)

commit v7 on v6

--- a/solution.py
+++ b/solution.py
@@ -388,7 +388,7 @@
 
 
 DENSITY_BATCH = 4
-FORCE_BATCH = 2
+FORCE_BATCH = 4
 
 
 def density_call(rows, codes, wanted, staying, around, incoming, place, weights):
@@ -436,7 +436,7 @@
         + [pltpu.VMEM((tall, 2 * LANES), F32)] * (2 * FORCE_BATCH)
         + [pltpu.VMEM((2 * tall, LANES), BF16)] * (2 * FORCE_BATCH)
         + [pltpu.VMEM((8, LANES), F32)] * (2 * FORCE_BATCH),
-        compiler_params=pltpu.CompilerParams(vmem_limit_bytes=48 << 20),
+        compiler_params=pltpu.CompilerParams(vmem_limit_bytes=60 << 20),
         name="force_pass",
     )(rows, codes, state, rho_table, place, heat_place, weights, shift)
 

time: 160 us -> 159 us (level)
  Pallas kernels: 103 us -> 100 us
    pallas_call x1, Pallas kernels: 71.8 us -> 69.2 us  [force_call(): pl.pallas_call(force_kernel, out_shape=(jax.ShapeDtypeStruct((3, SLOTS, L...]
where the time goes in v7:
time: 159 us; the launch traced here: 158 us
  Pallas kernels  100 us (63%)
  starting transfers between devices  23.9 us (15%)
  waiting for transfers between devices  20.6 us (13%)
  local copies, waits for them, and re-layouts  7.11 us (4%)
  other arithmetic  5.57 us (4%)
    pallas_call x1, Pallas kernels, force_call(): pl.pallas_call(force_kernel, out_shape=(jax.ShapeDtypeStruct((3, SLOTS, L...  69.2 us
    pallas_call x1, Pallas kernels, density_call(): pl.pallas_call(density_kernel, out_shape=(jax.ShapeDtypeStruct((SLOTS, LA...  31 us
    ppermute x10, starting transfers between devices, gather_stage(): pieces.append(lax.ppermute(shard, ('gx', 'gy'), pairs))  15.3 us
    ppermute x10, waiting for transfers between devices, gather_stage(): pieces.append(lax.ppermute(shard, ('gx', 'gy'), pairs))  11.3 us
    ppermute x4, waiting for transfers between devices, padded(): lax.ppermute(shard, axis, [(i, ((i - 1 ^ 1) + 1) % size if i else size -...  7.59 us
    ppermute x4, starting transfers between devices, padded(): lax.ppermute(shard, axis, [(i, ((i - 1 ^ 1) + 1) % size if i else size -...  7.33 us
    unnamed x30, local copies, waits for them, and re-layouts  4.71 us
  transfers between devices with their start and end apart: 18, of which 11 were waited for; matrix products, arithmetic and copies ran while one was open for 2% of the time, Pallas kernels for 0%

profile of v7, /device:TPU:0, one launch (start us, length us, event | category | flops | bytes accessed | tf_op | source)
XLA Modules:
  0.0 158.4 jit_solution(2562715186570525043)
XLA Ops:
  3.0 0.9 bitcast_dynamic-update-slice_fusion
  7.3 2.0 %collective-permute-start = (f32[18,128]{1,0:T(8,128)S(1)}, f32[18,128]{1,0:T(8,128)S(1)}, u32[]{:S(2)}, u32[]{:S(2)}) collective-permute-start(f32[18,128]{1,0:T(8,128)S(1)} %reshape.241), channel_id=1, source_target_pairs={{0,4},{1,5},{2,6},{3,7},{4,0},{5,1},{6,2},{7,3},{8,12},{9,13},{10,... | collective-permute-start | bytes 27656 | tf_op jit(solution)/shard_map/ppermute | solution.py:481
  9.3 3.6 %collective-permute-start.1 = (f32[18,128]{1,0:T(8,128)S(1)}, f32[18,128]{1,0:T(8,128)S(1)}, u32[]{:S(2)}, u32[]{:S(2)}) collective-permute-start(f32[18,128]{1,0:T(8,128)S(1)} %reshape.241), channel_id=1, source_target_pairs={{0,8},{1,9},{2,10},{3,11},{4,12},{5,13},{6,14},{7,15},{8,0},{9,1},... | collective-permute-start | bytes 27656 | tf_op jit(solution)/shard_map/ppermute | solution.py:481
  14.7 3.1 %collective-permute-done.2 = f32[18,128]{1,0:T(8,128)S(1)} collective-permute-done((f32[18,128]{1,0:T(8,128)S(1)}, f32[18,128]{1,0:T(8,128)S(1)}, u32[]{:S(2)}, u32[]{:S(2)}) %collective-permute-start.2) | collective-permute-done | bytes 9248 | tf_op jit(solution)/shard_map/ppermute | solution.py:481
  18.4 1.1 collective-permute-start.7
  19.6 1.7 %collective-permute-start.3 = (f32[72,128]{1,0:T(8,128)S(1)}, f32[72,128]{1,0:T(8,128)S(1)}, u32[]{:S(2)}, u32[]{:S(2)}) collective-permute-start(f32[72,128]{1,0:T(8,128)S(1)} %pad_maximum_fusion.8), channel_id=1, source_target_pairs={{0,1},{1,0},{2,3},{3,2},{4,5},{5,4},{6,7},{7,6},{8,9},{9,8},{10,11... | collective-permute-start | bytes 110600 | tf_op jit(solution)/shard_map/ppermute | solution.py:481
  21.3 2.9 %collective-permute-start.4 = (f32[72,128]{1,0:T(8,128)S(1)}, f32[72,128]{1,0:T(8,128)S(1)}, u32[]{:S(2)}, u32[]{:S(2)}) collective-permute-start(f32[72,128]{1,0:T(8,128)S(1)} %pad_maximum_fusion.8), channel_id=1, source_target_pairs={{0,2},{1,3},{2,0},{3,1},{4,6},{5,7},{6,4},{7,5},{8,10},{9,11},{10,... | collective-permute-start | bytes 110600 | tf_op jit(solution)/shard_map/ppermute | solution.py:481
  24.4 2.3 %collective-permute-done.4 = f32[72,128]{1,0:T(8,128)S(1)} collective-permute-done((f32[72,128]{1,0:T(8,128)S(1)}, f32[72,128]{1,0:T(8,128)S(1)}, u32[]{:S(2)}, u32[]{:S(2)}) %collective-permute-start.4) | collective-permute-done | bytes 36896 | tf_op jit(solution)/shard_map/ppermute | solution.py:481
  26.7 2.6 %collective-permute-done.5 = f32[72,128]{1,0:T(8,128)S(1)} collective-permute-done((f32[72,128]{1,0:T(8,128)S(1)}, f32[72,128]{1,0:T(8,128)S(1)}, u32[]{:S(2)}, u32[]{:S(2)}) %collective-permute-start.5) | collective-permute-done | bytes 36896 | tf_op jit(solution)/shard_map/ppermute | solution.py:481
  30.0 1.8 %collective-permute-start.10 = (f32[288,128]{1,0:T(8,128)S(1)}, f32[288,128]{1,0:T(8,128)S(1)}, u32[]{:S(2)}, u32[]{:S(2)}) collective-permute-start(f32[288,128]{1,0:T(8,128)S(1)} %pad_maximum_fusion.3), channel_id=1, source_target_pairs={{0,96},{1,97},{2,98},{3,99},{4,100},{5,101},{6,102},{7,103},{8,104... | collective-permute-start | bytes 442376 | tf_op jit(solution)/shard_map/ppermute | solution.py:481
  31.8 0.9 collective-permute-start.8
  32.7 2.0 %collective-permute-start.9 = (f32[288,128]{1,0:T(8,128)S(1)}, f32[288,128]{1,0:T(8,128)S(1)}, u32[]{:S(2)}, u32[]{:S(2)}) collective-permute-start(f32[288,128]{1,0:T(8,128)S(1)} %pad_maximum_fusion.3), channel_id=1, source_target_pairs={{0,64},{1,65},{2,66},{3,67},{4,68},{5,69},{6,70},{7,71},{8,72},{9,... | collective-permute-start | bytes 442376 | tf_op jit(solution)/shard_map/ppermute | solution.py:481
  34.8 2.8 %collective-permute-done.11 = f32[3,1,72,128]{3,2,1,0:T(8,128)S(1)} collective-permute-done((f32[3,1,72,128]{3,2,1,0:T(8,128)S(1)}, f32[3,1,72,128]{3,2,1,0:T(8,128)S(1)}, u32[]{:S(2)}, u32[]{:S(2)}) %collective-permute-start.11) | collective-permute-done | bytes 110624 | tf_op jit(solution)/shard_map/ppermute | solution.py:447
  37.9 1.6 collective-permute-done.9
  40.5 1.2 collective-permute-done.13
  41.8 31.0 %density_pass.1 = (f32[104,128]{1,0:T(8,128)}, f32[9,232,128]{2,1,0:T(8,128)S(1)}) custom-call(s32[832]{0:T(1024)S(1)} %reshape.238.rows, s32[416]{0:T(512)S(1)} %reshape.239.codes, s32[72]{0:T(128)S(1)} %select_n.232.wanted, f32[9,96,128]{2,1,0:T(8,128)S(1)} %broadcast_select_fusion.staying, f32[9,9,8,128]{3,2,1,0:T(8,128)S(1)} %bitcast.27, ...), custom_call_target="tpu_custom_call" | custom-call | tf_op jit(solution)/shard_map/density_pass/pallas_call | solution.py:396
  72.8 1.0 copy-done.1
  74.4 1.5 collective-permute-start.14
  76.0 2.7 %collective-permute-done.14 = f32[1,1,16,128]{3,2,1,0:T(8,128)S(1)} collective-permute-done((f32[1,1,16,128]{3,2,1,0:T(8,128)S(1)}, f32[1,1,16,128]{3,2,1,0:T(8,128)S(1)}, u32[]{:S(2)}, u32[]{:S(2)}) %collective-permute-start.14) | collective-permute-done | bytes 8224 | tf_op jit(solution)/shard_map/ppermute | solution.py:447
  78.8 5.1 %collective-permute-start.16 = (f32[3,1,16,128]{3,2,1,0:T(8,128)S(1)}, f32[3,1,16,128]{3,2,1,0:T(8,128)S(1)}, u32[]{:S(2)}, u32[]{:S(2)}) collective-permute-start(f32[3,1,16,128]{3,2,1,0:T(8,128)S(1)} %pad_maximum_fusion.9), channel_id=1, source_target_pairs={{0,15},{1,2},{2,1},{3,4},{4,3},{5,6},{6,5},{7,8},{8,7},{9,10},{10,... | collective-permute-start | bytes 73736 | tf_op jit(solution)/shard_map/ppermute | solution.py:447
  83.9 2.1 %collective-permute-done.16 = f32[3,1,16,128]{3,2,1,0:T(8,128)S(1)} collective-permute-done((f32[3,1,16,128]{3,2,1,0:T(8,128)S(1)}, f32[3,1,16,128]{3,2,1,0:T(8,128)S(1)}, u32[]{:S(2)}, u32[]{:S(2)}) %collective-permute-start.16) | collective-permute-done | bytes 24608 | tf_op jit(solution)/shard_map/ppermute | solution.py:447
  86.0 1.7 %collective-permute-done.17 = f32[3,1,16,128]{3,2,1,0:T(8,128)S(1)} collective-permute-done((f32[3,1,16,128]{3,2,1,0:T(8,128)S(1)}, f32[3,1,16,128]{3,2,1,0:T(8,128)S(1)}, u32[]{:S(2)}, u32[]{:S(2)}) %collective-permute-start.17) | collective-permute-done | bytes 24608 | tf_op jit(solution)/shard_map/ppermute | solution.py:446
  87.8 1.5 pad_maximum_fusion.4.rho_table
  89.2 69.2 %force_pass.1 = (f32[3,104,128]{2,1,0:T(8,128)}, f32[104,128]{1,0:T(8,128)}) custom-call(s32[832]{0:T(1024)} %copy-done.2, s32[416]{0:T(512)} %copy-done.4, f32[9,232,128]{2,1,0:T(8,128)} %copy-done.1, f32[232,128]{1,0:T(8,128)} %pad_maximum_fusion.4.rho_table, bf16[224,32]{1,0:T(8,128)(2,1)} %constant.195.place, ...), custom_call_target="tpu_custom_call" | custom-call | tf_op jit(solution)/shard_map/force_pass/pallas_call | solution.py:417
  (92 shorter events, 11.0 us)
Async XLA Ops:
  0.6 12.2 %copy-start.6 = (s32[9]{0:T(128)S(1)}, s32[9]{0:T(128)}, u32[]{:S(2)}) copy-start(s32[9]{0:T(128)} %constant.180.clone) | copy-start | bytes 112
  0.6 12.2 %copy-start.7 = (s32[9]{0:T(128)S(1)}, s32[9]{0:T(128)}, u32[]{:S(2)}) copy-start(s32[9]{0:T(128)} %constant.181.clone) | copy-start | bytes 112
  0.7 12.3 %copy-start.10 = (s32[1,2]{1,0:T(1,128)S(1)}, s32[1,2]{1,0:T(1,128)}, u32[]{:S(2)}) copy-start(s32[1,2]{1,0:T(1,128)} %param.21) | copy-start | bytes 28
  5.5 7.6 %copy-start.9 = (s32[128,2]{0,1:T(2,128)S(1)}, s32[128,2]{0,1:T(2,128)}, u32[]{:S(2)}) copy-start(s32[128,2]{0,1:T(2,128)} %param.22) | copy-start | bytes 3076
  7.3 7.2 %collective-permute-start = (f32[18,128]{1,0:T(8,128)S(1)}, f32[18,128]{1,0:T(8,128)S(1)}, u32[]{:S(2)}, u32[]{:S(2)}) collective-permute-start(f32[18,128]{1,0:T(8,128)S(1)} %reshape.241), channel_id=1, source_target_pairs={{0,4},{1,5},{2,6},{3,7},{4,0},{5,1},{6,2},{7,3},{8,12},{9,13},{10,... | collective-permute-start | bytes 27656 | tf_op jit(solution)/shard_map/ppermute | solution.py:481
  9.3 5.4 %collective-permute-start.1 = (f32[18,128]{1,0:T(8,128)S(1)}, f32[18,128]{1,0:T(8,128)S(1)}, u32[]{:S(2)}, u32[]{:S(2)}) collective-permute-start(f32[18,128]{1,0:T(8,128)S(1)} %reshape.241), channel_id=1, source_target_pairs={{0,8},{1,9},{2,10},{3,11},{4,12},{5,13},{6,14},{7,15},{8,0},{9,1},... | collective-permute-start | bytes 27656 | tf_op jit(solution)/shard_map/ppermute | solution.py:481
  12.9 4.9 %collective-permute-start.2 = (f32[18,128]{1,0:T(8,128)S(1)}, f32[18,128]{1,0:T(8,128)S(1)}, u32[]{:S(2)}, u32[]{:S(2)}) collective-permute-start(f32[18,128]{1,0:T(8,128)S(1)} %reshape.241), channel_id=1, source_target_pairs={{0,12},{1,13},{2,14},{3,15},{4,8},{5,9},{6,10},{7,11},{8,4},{9,5},... | collective-permute-start | bytes 27656 | tf_op jit(solution)/shard_map/ppermute | solution.py:481
  17.8 6.6 %collective-permute-start.6 = (f32[1,1,72,128]{3,2,1,0:T(8,128)S(1)}, f32[1,1,72,128]{3,2,1,0:T(8,128)S(1)}, u32[]{:S(2)}, u32[]{:S(2)}) collective-permute-start(f32[1,1,72,128]{3,2,1,0:T(8,128)S(1)} %slice_bitcast_fusion), channel_id=1, source_target_pairs={{0,112},{16,32},{32,16},{48,64},{64,48},{80,96},{96,80},{112,0},{1... | collective-permute-start | bytes 110600 | tf_op jit(solution)/shard_map/ppermute | solution.py:447
  18.4 6.0 %collective-permute-start.7 = (f32[1,1,72,128]{3,2,1,0:T(8,128)S(1)}, f32[1,1,72,128]{3,2,1,0:T(8,128)S(1)}, u32[]{:S(2)}, u32[]{:S(2)}) collective-permute-start(f32[1,1,72,128]{3,2,1,0:T(8,128)S(1)} %slice_bitcast_fusion), channel_id=1, source_target_pairs={{0,16},{16,0},{32,48},{48,32},{64,80},{80,64},{96,112},{112,96},{1... | collective-permute-start | bytes 110600 | tf_op jit(solution)/shard_map/ppermute | solution.py:446
  19.6 4.8 %collective-permute-start.3 = (f32[72,128]{1,0:T(8,128)S(1)}, f32[72,128]{1,0:T(8,128)S(1)}, u32[]{:S(2)}, u32[]{:S(2)}) collective-permute-start(f32[72,128]{1,0:T(8,128)S(1)} %pad_maximum_fusion.8), channel_id=1, source_target_pairs={{0,1},{1,0},{2,3},{3,2},{4,5},{5,4},{6,7},{7,6},{8,9},{9,8},{10,11... | collective-permute-start | bytes 110600 | tf_op jit(solution)/shard_map/ppermute | solution.py:481
  21.3 5.5 %collective-permute-start.4 = (f32[72,128]{1,0:T(8,128)S(1)}, f32[72,128]{1,0:T(8,128)S(1)}, u32[]{:S(2)}, u32[]{:S(2)}) collective-permute-start(f32[72,128]{1,0:T(8,128)S(1)} %pad_maximum_fusion.8), channel_id=1, source_target_pairs={{0,2},{1,3},{2,0},{3,1},{4,6},{5,7},{6,4},{7,5},{8,10},{9,11},{10,... | collective-permute-start | bytes 110600 | tf_op jit(solution)/shard_map/ppermute | solution.py:481
  24.2 5.2 %collective-permute-start.5 = (f32[72,128]{1,0:T(8,128)S(1)}, f32[72,128]{1,0:T(8,128)S(1)}, u32[]{:S(2)}, u32[]{:S(2)}) collective-permute-start(f32[72,128]{1,0:T(8,128)S(1)} %pad_maximum_fusion.8), channel_id=1, source_target_pairs={{0,3},{1,2},{2,1},{3,0},{4,7},{5,6},{6,5},{7,4},{8,11},{9,10},{10,... | collective-permute-start | bytes 110600 | tf_op jit(solution)/shard_map/ppermute | solution.py:481
  29.4 8.1 %collective-permute-start.11 = (f32[3,1,72,128]{3,2,1,0:T(8,128)S(1)}, f32[3,1,72,128]{3,2,1,0:T(8,128)S(1)}, u32[]{:S(2)}, u32[]{:S(2)}) collective-permute-start(f32[3,1,72,128]{3,2,1,0:T(8,128)S(1)} %pad_maximum_fusion.5), channel_id=1, source_target_pairs={{0,15},{1,2},{2,1},{3,4},{4,3},{5,6},{6,5},{7,8},{8,7},{9,10},{10,... | collective-permute-start | bytes 331784 | tf_op jit(solution)/shard_map/ppermute | solution.py:447
  29.5 8.1 %collective-permute-start.12 = (f32[3,1,72,128]{3,2,1,0:T(8,128)S(1)}, f32[3,1,72,128]{3,2,1,0:T(8,128)S(1)}, u32[]{:S(2)}, u32[]{:S(2)}) collective-permute-start(f32[3,1,72,128]{3,2,1,0:T(8,128)S(1)} %pad_maximum_fusion.5), channel_id=1, source_target_pairs={{0,1},{1,0},{2,3},{3,2},{4,5},{5,4},{6,7},{7,6},{8,9},{9,8},{10,11... | collective-permute-start | bytes 331784 | tf_op jit(solution)/shard_map/ppermute | solution.py:446
  29.9 10.1 %copy-start.5 = (s32[104,8]{0,1:T(8,128)S(1)}, s32[104,8]{0,1:T(8,128)}, u32[]{:S(2)}) copy-start(s32[104,8]{0,1:T(8,128)} %param.23) | copy-start | bytes 9988
  30.0 10.2 %copy-start.8 = (s32[104,4]{0,1:T(4,128)S(1)}, s32[104,4]{0,1:T(4,128)}, u32[]{:S(2)}) copy-start(s32[104,4]{0,1:T(4,128)} %param.24) | copy-start | bytes 4996
  30.0 8.0 %collective-permute-start.10 = (f32[288,128]{1,0:T(8,128)S(1)}, f32[288,128]{1,0:T(8,128)S(1)}, u32[]{:S(2)}, u32[]{:S(2)}) collective-permute-start(f32[288,128]{1,0:T(8,128)S(1)} %pad_maximum_fusion.3), channel_id=1, source_target_pairs={{0,96},{1,97},{2,98},{3,99},{4,100},{5,101},{6,102},{7,103},{8,104... | collective-permute-start | bytes 442376 | tf_op jit(solution)/shard_map/ppermute | solution.py:481
  31.8 6.1 %collective-permute-start.8 = (f32[288,128]{1,0:T(8,128)S(1)}, f32[288,128]{1,0:T(8,128)S(1)}, u32[]{:S(2)}, u32[]{:S(2)}) collective-permute-start(f32[288,128]{1,0:T(8,128)S(1)} %pad_maximum_fusion.3), channel_id=1, source_target_pairs={{0,32},{1,33},{2,34},{3,35},{4,36},{5,37},{6,38},{7,39},{8,40},{9,... | collective-permute-start | bytes 442376 | tf_op jit(solution)/shard_map/ppermute | solution.py:481
  32.7 6.8 %collective-permute-start.9 = (f32[288,128]{1,0:T(8,128)S(1)}, f32[288,128]{1,0:T(8,128)S(1)}, u32[]{:S(2)}, u32[]{:S(2)}) collective-permute-start(f32[288,128]{1,0:T(8,128)S(1)} %pad_maximum_fusion.3), channel_id=1, source_target_pairs={{0,64},{1,65},{2,66},{3,67},{4,68},{5,69},{6,70},{7,71},{8,72},{9,... | collective-permute-start | bytes 442376 | tf_op jit(solution)/shard_map/ppermute | solution.py:481
  39.6 2.1 %collective-permute-start.13 = (f32[1152,128]{1,0:T(8,128)S(1)}, f32[1152,128]{1,0:T(8,128)S(1)}, u32[]{:S(2)}, u32[]{:S(2)}) collective-permute-start(f32[1152,128]{1,0:T(8,128)S(1)} %pad_maximum_fusion.1), channel_id=1, source_target_pairs={{0,16},{1,17},{2,18},{3,19},{4,20},{5,21},{6,22},{7,23},{8,24},{9,... | collective-permute-start | bytes 1769480 | tf_op jit(solution)/shard_map/ppermute | solution.py:481
  74.4 4.3 %collective-permute-start.14 = (f32[1,1,16,128]{3,2,1,0:T(8,128)S(1)}, f32[1,1,16,128]{3,2,1,0:T(8,128)S(1)}, u32[]{:S(2)}, u32[]{:S(2)}) collective-permute-start(f32[1,1,16,128]{3,2,1,0:T(8,128)S(1)} %slice_bitcast_fusion.1), channel_id=1, source_target_pairs={{0,112},{16,32},{32,16},{48,64},{64,48},{80,96},{96,80},{112,0},{1... | collective-permute-start | bytes 24584 | tf_op jit(solution)/shard_map/ppermute | solution.py:447
  76.0 2.7 %collective-permute-start.15 = (f32[1,1,16,128]{3,2,1,0:T(8,128)S(1)}, f32[1,1,16,128]{3,2,1,0:T(8,128)S(1)}, u32[]{:S(2)}, u32[]{:S(2)}) collective-permute-start(f32[1,1,16,128]{3,2,1,0:T(8,128)S(1)} %slice_bitcast_fusion.1), channel_id=1, source_target_pairs={{0,16},{16,0},{32,48},{48,32},{64,80},{80,64},{96,112},{112,96},{1... | collective-permute-start | bytes 24584 | tf_op jit(solution)/shard_map/ppermute | solution.py:446
  78.8 7.2 %collective-permute-start.16 = (f32[3,1,16,128]{3,2,1,0:T(8,128)S(1)}, f32[3,1,16,128]{3,2,1,0:T(8,128)S(1)}, u32[]{:S(2)}, u32[]{:S(2)}) collective-permute-start(f32[3,1,16,128]{3,2,1,0:T(8,128)S(1)} %pad_maximum_fusion.9), channel_id=1, source_target_pairs={{0,15},{1,2},{2,1},{3,4},{4,3},{5,6},{6,5},{7,8},{8,7},{9,10},{10,... | collective-permute-start | bytes 73736 | tf_op jit(solution)/shard_map/ppermute | solution.py:447
  83.9 3.8 %collective-permute-start.17 = (f32[3,1,16,128]{3,2,1,0:T(8,128)S(1)}, f32[3,1,16,128]{3,2,1,0:T(8,128)S(1)}, u32[]{:S(2)}, u32[]{:S(2)}) collective-permute-start(f32[3,1,16,128]{3,2,1,0:T(8,128)S(1)} %pad_maximum_fusion.9), channel_id=1, source_target_pairs={{0,1},{1,0},{2,3},{3,2},{4,5},{5,4},{6,7},{7,6},{8,9},{9,8},{10,11... | collective-permute-start | bytes 73736 | tf_op jit(solution)/shard_map/ppermute | solution.py:446
  (5 other events, 6.3 us)
